TPU v7x, 32 devices: a whole 2x2x4 slice. The times are simulated.
32 devices in a mesh: dp: 8 (over y, x, core), mp: 4 (over z).
Axes of the slice: x: 2, y: 2, z: 4, core: 2. Of those that a mesh axis runs over, the one named last changes fastest.
Arguments:
- tokens: bfloat16 [16384, 8192], P('dp', 'mp'), may hold values from -24 to 24
- grid_codes: int32 [8192, 28672], P('mp', 'dp'), may hold values from 0 to 255, as said below
- residue: bfloat16 [8192, 28672], P('mp', 'dp'), may hold values from 0 to 1
- tile_spans: int32 [64, 224], P('mp', 'dp'), may hold values from 16 to 256, as said below
- tile_scales: float32 [64, 224], P('mp', 'dp'), may hold values from 0.25 to 4
- other_bits: int32 [8], replicated, may hold values from 47308 to 53043
Outputs:
- served: bfloat16 [8192, 28672], P(None, ('dp', 'mp'))
- tile_bits: float32 [64, 224], P('mp', 'dp')
Inputs may be any that keep to these rules, and one draw needn't show every extreme that they name: `grid_codes`: every code lies in its tile's span around 128: 128 - tile_spans / 2 <= code < 128 + tile_spans / 2. `tile_spans`: spans are powers of two, 16 to 256, each of the five values on a fifth of the tiles.
All inputs are finite; a program needn't handle non-finite values.
Results may differ from a plain program's by a relative error of at most 0.0006.
Values may be sent and summed in bfloat16 or wider, within the bound.
No kernel may reach another device: no remote copies, remote signals or barrier semaphores. Data moves between devices by JAX's collectives and lax.ppermute only.
A program may use at most 448 MiB of HBM per device.

v0:
```python
import jax
import jax.numpy as jnp
from jax import lax
from jax.sharding import PartitionSpec as P

GROUP = 128
TRIALS = 24
OTHER = 8
TILES = 14336


BIT_WIDTHS = (2, 3, 4, 8)
ERR_WEIGHT = 16.0
SOFTMAX_WARMTH = 0.03
SLOPE_LIMIT = 16.0
TARGET_BITS = 3.5


def candidates(grid_codes, residue, tile_spans, tile_scales):
    group_count, tile_count = tile_spans.shape
    shape = (group_count, GROUP, tile_count, GROUP)
    code_grid = grid_codes.reshape(shape)
    span_grid = tile_spans.reshape(group_count, 1, tile_count, 1)
    scale_grid = tile_scales.reshape(group_count, 1, tile_count, 1)
    low_edge = 128 - span_grid // 2
    values_f = code_grid.astype(jnp.float32) + residue.reshape(shape).astype(jnp.float32)
    errors_list = []
    levels_list = []
    for bit_width in BIT_WIDTHS:
        step_size = jnp.maximum(jnp.right_shift(span_grid, bit_width), 1)
        level_index = (code_grid - low_edge) // step_size
        centers = low_edge.astype(jnp.float32) + (
            level_index.astype(jnp.float32) + 0.5
        ) * step_size.astype(jnp.float32)
        errors_list.append(scale_grid * (values_f - centers) / 128.0)
        levels_list.append(scale_grid * (centers / 128.0 - 1.0))
    return (jnp.stack(errors_list), jnp.stack(levels_list))


def error_table(hessian, error_values):
    weighted = jnp.einsum(
        "gij,bgjtc->bgitc", hessian, error_values, precision=lax.Precision.HIGHEST
    )
    return jnp.sum(error_values * weighted, axis=(2, 4)) / float(GROUP * GROUP)


def tile_probs(table, slope_now):
    column_of_bits = jnp.array(BIT_WIDTHS, dtype=jnp.float32).reshape(
        (len(BIT_WIDTHS),) + (1,) * (table.ndim - 1)
    )
    tile_score = ERR_WEIGHT * table + slope_now * column_of_bits
    return (jax.nn.softmax(-tile_score / SOFTMAX_WARMTH, axis=0), column_of_bits)


def total_rate(table, slope_now):
    probs, column_of_bits = tile_probs(table, slope_now)
    return jnp.sum(probs * column_of_bits)


def local(tokens, grid_codes, residue, tile_spans, tile_scales, other_bits):
    tok_count, width_local = tokens.shape
    group_count = width_local // GROUP
    blocks = tokens.reshape(tok_count, group_count, GROUP)
    partial_gram = jnp.einsum("tgi,tgj->gij", blocks, blocks, preferred_element_type=jnp.float32)
    hessian = lax.psum(partial_gram, "dp") / float(tok_count * lax.axis_size("dp"))
    error_values, levels = candidates(grid_codes, residue, tile_spans, tile_scales)
    table = error_table(hessian, error_values)
    goal = TARGET_BITS * (OTHER + 1) * TILES - jnp.sum(other_bits).astype(jnp.float32)

    def trial(index, bounds):
        lower, upper = bounds
        middle = 0.5 * (lower + upper)
        summed = lax.psum(total_rate(table, middle), ("dp", "mp"))
        above = summed > goal
        return (jnp.where(above, middle, lower), jnp.where(above, upper, middle))

    lower, upper = lax.fori_loop(0, TRIALS, trial, (jnp.float32(0.0), jnp.float32(SLOPE_LIMIT)))
    slope_final = 0.5 * (lower + upper)
    probs, column_of_bits = tile_probs(table, slope_final)
    tile_bits = jnp.sum(probs * column_of_bits, axis=0)
    mixed = (
        jnp.sum(probs[:, :, None, :, None] * levels, axis=0)
        .reshape(grid_codes.shape)
        .astype(jnp.bfloat16)
    )
    served = lax.all_to_all(mixed, "mp", split_axis=1, concat_axis=0, tiled=True)
    return (served, tile_bits)


def solution(mesh):
    placed = (P("dp", "mp"), P("mp", "dp"), P("mp", "dp"), P("mp", "dp"), P("mp", "dp"), P())
    return jax.shard_map(
        local,
        mesh=mesh,
        in_specs=placed,
        out_specs=(P(None, ("dp", "mp")), P("mp", "dp")),
        check_vma=False,
    )
```

profile of v0, /device:TPU:0, one launch (start us, length us, event | category | flops | bytes accessed | tf_op | source)
XLA Modules:
  0.0 2945.2 jit_solution(4846515422781286110)
XLA Ops:
  7.2 11.1 fusion.26
  18.3 0.7 shift-right-arithmetic_maximum_fusion.3
  19.0 0.7 fusion.43
  19.7 33.4 %reshape.87 = s32[16,128,28,128]{3,2,1,0:T(8,128)} reshape(s32[2048,3584]{1,0:T(8,128)} %param.13) | data formatting | bytes 58720256 | tf_op jit(solution)/shard_map/reshape | solution.py:22
  53.1 33.4 %copy.33 = s32[16,128,28,128]{1,3,2,0:T(8,128)} copy(s32[16,128,28,128]{3,2,1,0:T(8,128)} %reshape.87) | data formatting | bytes 58720256 | tf_op jit(solution)/shard_map/reshape | solution.py:22
  86.5 26.1 reshape.88
  112.6 33.3 %copy.35 = f32[16,128,28,128]{1,3,2,0:T(8,128)} copy(f32[16,128,28,128]{3,2,1,0:T(8,128)} %reshape.88) | data formatting | bytes 58720256 | tf_op jit(solution)/shard_map/convert_element_type | solution.py:26
  145.9 324.7 %multiply_bitcast_fusion.7 = (f32[1,16,128,28,128]{2,4,3,0,1:T(8,128)}, f32[16,128,28,128]{1,3,2,0:T(8,128)}, f32[1,16,128,28,128]{2,4,3,1,0:T(8,128)}) fusion(f32[16,28]{1,0:T(8,128)S(1)} %copy-done, f32[16,28]{1,0:T(8,128)S(1)} %get-tuple-element.91, s32[16,28]{1,0:T(8,128)S(1)} %get-tuple-element.86, s32[16,28]{1,0:T(8,128)S(1)} %get-tuple-element.82, ...), kind=kLoop, calls=%fused_computation.44 | loop fusion | flops 154140672 | bytes 146811392 | tf_op jit(solution)/shard_map/stack | solution.py:37
  470.7 901.1 %multiply_bitcast_fusion.6 = (f32[1,16,128,28,128]{2,4,3,0,1:T(8,128)}, f32[1,16,128,28,128]{2,4,3,0,1:T(8,128)}, f32[1,16,128,28,128]{2,4,3,0,1:T(8,128)}, f32[...) fusion(f32[16,128,28,128]{1,3,2,0:T(8,128)} %get-tuple-element.74, ...), kind=kLoop, calls=%fused_computation.43 | loop fusion | flops 389021696 | bytes 234902528 | tf_op jit(solution)/shard_map/stack | solution.py:37
  1373.1 117.9 %fusion.4 = f32[4,16,28]{2,0,1:T(4,128)S(1)} fusion(f32[1,16,128,28,128]{2,4,3,0,1:T(8,128)} %get-tuple-element.77, f32[1,16,128,28,128]{2,4,3,0,1:T(8,128)} %get-tuple-element.76, f32[1,16,128,28,128]{2,4,3,0,1:T(8,128)} %get-tuple-element.75, f32[1,16,128,28,128]{2,4,3,0,1:T(8,128)} %get-tuple-element.73, f32[16,128,128]{2,1,0:T(8,128)} %all-reduce.2.cloned.1.call-done), kind=kOutput, calls=%fused_computation.11 | convolution fusion | flops 45332299776 | bytes 118496256 | tf_op jit(solution)/shard_map/gij,bgjtc->bgitc/dot_general | solution.py:41
  1491.1 1009.4 %while.13 = (s32[]{:T(128)}, f32[]{:T(128)}, f32[]{:T(128)}, f32[4,16,28]{2,1,0:T(8,128)S(1)}, f32[]{:T(128)}, /*index=5*/s32[]{:T(128)}, f32[4]{0:T(128)S(1)}, f32[]{:T(128)}) while((s32[]{:T(128)}, f32[]{:T(128)}, f32[]{:T(128)}, f32[4,16,28]{2,1,0:T(8,128)S(1)}, f32[]{:T(128)}, /*index=5*/s32[]{:T(128)}, f32[4]{0:T(128)S(1)}, ...), condition=%wide.region_8.10_spmd.clone, body=%wide.region_3.9_spmd.sunk.clone.sunk | while | flops 33163 | bytes 30720 | solution.py:77
  1491.3 0.7 multiply_reduce_fusion.3
  1491.9 42.2 %psum.18 = f32[]{:T(128)} all-reduce(f32[]{:T(128)} %multiply_reduce_fusion.3), channel_id=1, replica_groups=mesh['dp'=8,'mp'=4] {'dp','mp'}, use_global_device_ids=true, to_apply=%region_7.8 | all-reduce | flops 1 | bytes 8 | tf_op jit(solution)/shard_map/while/body/eval_jaxpr/psum | solution.py:73
  1535.0 0.7 multiply_reduce_fusion.3
  1535.7 40.5 %psum.18 = f32[]{:T(128)} all-reduce(f32[]{:T(128)} %multiply_reduce_fusion.3), channel_id=1, replica_groups=mesh['dp'=8,'mp'=4] {'dp','mp'}, use_global_device_ids=true, to_apply=%region_7.8 | all-reduce | flops 1 | bytes 8 | tf_op jit(solution)/shard_map/while/body/eval_jaxpr/psum | solution.py:73
  1577.1 0.7 multiply_reduce_fusion.3
  1577.7 40.3 %psum.18 = f32[]{:T(128)} all-reduce(f32[]{:T(128)} %multiply_reduce_fusion.3), channel_id=1, replica_groups=mesh['dp'=8,'mp'=4] {'dp','mp'}, use_global_device_ids=true, to_apply=%region_7.8 | all-reduce | flops 1 | bytes 8 | tf_op jit(solution)/shard_map/while/body/eval_jaxpr/psum | solution.py:73
  1618.9 0.7 multiply_reduce_fusion.3
  1619.6 40.5 %psum.18 = f32[]{:T(128)} all-reduce(f32[]{:T(128)} %multiply_reduce_fusion.3), channel_id=1, replica_groups=mesh['dp'=8,'mp'=4] {'dp','mp'}, use_global_device_ids=true, to_apply=%region_7.8 | all-reduce | flops 1 | bytes 8 | tf_op jit(solution)/shard_map/while/body/eval_jaxpr/psum | solution.py:73
  1661.0 0.7 multiply_reduce_fusion.3
  1661.7 40.3 %psum.18 = f32[]{:T(128)} all-reduce(f32[]{:T(128)} %multiply_reduce_fusion.3), channel_id=1, replica_groups=mesh['dp'=8,'mp'=4] {'dp','mp'}, use_global_device_ids=true, to_apply=%region_7.8 | all-reduce | flops 1 | bytes 8 | tf_op jit(solution)/shard_map/while/body/eval_jaxpr/psum | solution.py:73
  1702.8 0.7 multiply_reduce_fusion.3
  1703.5 40.6 %psum.18 = f32[]{:T(128)} all-reduce(f32[]{:T(128)} %multiply_reduce_fusion.3), channel_id=1, replica_groups=mesh['dp'=8,'mp'=4] {'dp','mp'}, use_global_device_ids=true, to_apply=%region_7.8 | all-reduce | flops 1 | bytes 8 | tf_op jit(solution)/shard_map/while/body/eval_jaxpr/psum | solution.py:73
  1745.0 0.7 multiply_reduce_fusion.3
  1745.7 40.1 %psum.18 = f32[]{:T(128)} all-reduce(f32[]{:T(128)} %multiply_reduce_fusion.3), channel_id=1, replica_groups=mesh['dp'=8,'mp'=4] {'dp','mp'}, use_global_device_ids=true, to_apply=%region_7.8 | all-reduce | flops 1 | bytes 8 | tf_op jit(solution)/shard_map/while/body/eval_jaxpr/psum | solution.py:73
  1786.7 0.7 multiply_reduce_fusion.3
  1787.4 40.7 %psum.18 = f32[]{:T(128)} all-reduce(f32[]{:T(128)} %multiply_reduce_fusion.3), channel_id=1, replica_groups=mesh['dp'=8,'mp'=4] {'dp','mp'}, use_global_device_ids=true, to_apply=%region_7.8 | all-reduce | flops 1 | bytes 8 | tf_op jit(solution)/shard_map/while/body/eval_jaxpr/psum | solution.py:73
  1828.9 0.7 multiply_reduce_fusion.3
  1829.6 40.1 %psum.18 = f32[]{:T(128)} all-reduce(f32[]{:T(128)} %multiply_reduce_fusion.3), channel_id=1, replica_groups=mesh['dp'=8,'mp'=4] {'dp','mp'}, use_global_device_ids=true, to_apply=%region_7.8 | all-reduce | flops 1 | bytes 8 | tf_op jit(solution)/shard_map/while/body/eval_jaxpr/psum | solution.py:73
  1870.6 0.7 multiply_reduce_fusion.3
  1871.2 40.8 %psum.18 = f32[]{:T(128)} all-reduce(f32[]{:T(128)} %multiply_reduce_fusion.3), channel_id=1, replica_groups=mesh['dp'=8,'mp'=4] {'dp','mp'}, use_global_device_ids=true, to_apply=%region_7.8 | all-reduce | flops 1 | bytes 8 | tf_op jit(solution)/shard_map/while/body/eval_jaxpr/psum | solution.py:73
  1912.9 0.7 multiply_reduce_fusion.3
  1913.6 40.0 %psum.18 = f32[]{:T(128)} all-reduce(f32[]{:T(128)} %multiply_reduce_fusion.3), channel_id=1, replica_groups=mesh['dp'=8,'mp'=4] {'dp','mp'}, use_global_device_ids=true, to_apply=%region_7.8 | all-reduce | flops 1 | bytes 8 | tf_op jit(solution)/shard_map/while/body/eval_jaxpr/psum | solution.py:73
  1954.4 0.7 multiply_reduce_fusion.3
  1955.1 40.8 %psum.18 = f32[]{:T(128)} all-reduce(f32[]{:T(128)} %multiply_reduce_fusion.3), channel_id=1, replica_groups=mesh['dp'=8,'mp'=4] {'dp','mp'}, use_global_device_ids=true, to_apply=%region_7.8 | all-reduce | flops 1 | bytes 8 | tf_op jit(solution)/shard_map/while/body/eval_jaxpr/psum | solution.py:73
  1996.8 0.7 multiply_reduce_fusion.3
  1997.5 39.9 %psum.18 = f32[]{:T(128)} all-reduce(f32[]{:T(128)} %multiply_reduce_fusion.3), channel_id=1, replica_groups=mesh['dp'=8,'mp'=4] {'dp','mp'}, use_global_device_ids=true, to_apply=%region_7.8 | all-reduce | flops 1 | bytes 8 | tf_op jit(solution)/shard_map/while/body/eval_jaxpr/psum | solution.py:73
  2038.3 0.7 multiply_reduce_fusion.3
  2039.0 41.0 %psum.18 = f32[]{:T(128)} all-reduce(f32[]{:T(128)} %multiply_reduce_fusion.3), channel_id=1, replica_groups=mesh['dp'=8,'mp'=4] {'dp','mp'}, use_global_device_ids=true, to_apply=%region_7.8 | all-reduce | flops 1 | bytes 8 | tf_op jit(solution)/shard_map/while/body/eval_jaxpr/psum | solution.py:73
  2080.8 0.7 multiply_reduce_fusion.3
  2081.5 39.8 %psum.18 = f32[]{:T(128)} all-reduce(f32[]{:T(128)} %multiply_reduce_fusion.3), channel_id=1, replica_groups=mesh['dp'=8,'mp'=4] {'dp','mp'}, use_global_device_ids=true, to_apply=%region_7.8 | all-reduce | flops 1 | bytes 8 | tf_op jit(solution)/shard_map/while/body/eval_jaxpr/psum | solution.py:73
  2122.2 0.7 multiply_reduce_fusion.3
  2122.8 41.0 %psum.18 = f32[]{:T(128)} all-reduce(f32[]{:T(128)} %multiply_reduce_fusion.3), channel_id=1, replica_groups=mesh['dp'=8,'mp'=4] {'dp','mp'}, use_global_device_ids=true, to_apply=%region_7.8 | all-reduce | flops 1 | bytes 8 | tf_op jit(solution)/shard_map/while/body/eval_jaxpr/psum | solution.py:73
  2164.8 0.7 multiply_reduce_fusion.3
  2165.4 39.7 %psum.18 = f32[]{:T(128)} all-reduce(f32[]{:T(128)} %multiply_reduce_fusion.3), channel_id=1, replica_groups=mesh['dp'=8,'mp'=4] {'dp','mp'}, use_global_device_ids=true, to_apply=%region_7.8 | all-reduce | flops 1 | bytes 8 | tf_op jit(solution)/shard_map/while/body/eval_jaxpr/psum | solution.py:73
  2206.0 0.7 multiply_reduce_fusion.3
  2206.7 41.2 %psum.18 = f32[]{:T(128)} all-reduce(f32[]{:T(128)} %multiply_reduce_fusion.3), channel_id=1, replica_groups=mesh['dp'=8,'mp'=4] {'dp','mp'}, use_global_device_ids=true, to_apply=%region_7.8 | all-reduce | flops 1 | bytes 8 | tf_op jit(solution)/shard_map/while/body/eval_jaxpr/psum | solution.py:73
  2248.8 0.7 multiply_reduce_fusion.3
  2249.5 39.7 %psum.18 = f32[]{:T(128)} all-reduce(f32[]{:T(128)} %multiply_reduce_fusion.3), channel_id=1, replica_groups=mesh['dp'=8,'mp'=4] {'dp','mp'}, use_global_device_ids=true, to_apply=%region_7.8 | all-reduce | flops 1 | bytes 8 | tf_op jit(solution)/shard_map/while/body/eval_jaxpr/psum | solution.py:73
  2290.0 0.7 multiply_reduce_fusion.3
  2290.7 41.1 %psum.18 = f32[]{:T(128)} all-reduce(f32[]{:T(128)} %multiply_reduce_fusion.3), channel_id=1, replica_groups=mesh['dp'=8,'mp'=4] {'dp','mp'}, use_global_device_ids=true, to_apply=%region_7.8 | all-reduce | flops 1 | bytes 8 | tf_op jit(solution)/shard_map/while/body/eval_jaxpr/psum | solution.py:73
  2332.7 0.7 multiply_reduce_fusion.3
  2333.4 39.7 %psum.18 = f32[]{:T(128)} all-reduce(f32[]{:T(128)} %multiply_reduce_fusion.3), channel_id=1, replica_groups=mesh['dp'=8,'mp'=4] {'dp','mp'}, use_global_device_ids=true, to_apply=%region_7.8 | all-reduce | flops 1 | bytes 8 | tf_op jit(solution)/shard_map/while/body/eval_jaxpr/psum | solution.py:73
  2374.0 0.7 multiply_reduce_fusion.3
  2374.6 41.2 %psum.18 = f32[]{:T(128)} all-reduce(f32[]{:T(128)} %multiply_reduce_fusion.3), channel_id=1, replica_groups=mesh['dp'=8,'mp'=4] {'dp','mp'}, use_global_device_ids=true, to_apply=%region_7.8 | all-reduce | flops 1 | bytes 8 | tf_op jit(solution)/shard_map/while/body/eval_jaxpr/psum | solution.py:73
  2416.7 0.7 multiply_reduce_fusion.3
  2417.4 39.7 %psum.18 = f32[]{:T(128)} all-reduce(f32[]{:T(128)} %multiply_reduce_fusion.3), channel_id=1, replica_groups=mesh['dp'=8,'mp'=4] {'dp','mp'}, use_global_device_ids=true, to_apply=%region_7.8 | all-reduce | flops 1 | bytes 8 | tf_op jit(solution)/shard_map/while/body/eval_jaxpr/psum | solution.py:73
  2458.6 41.1 %psum.18 = f32[]{:T(128)} all-reduce(f32[]{:T(128)} %multiply_reduce_fusion.3), channel_id=1, replica_groups=mesh['dp'=8,'mp'=4] {'dp','mp'}, use_global_device_ids=true, to_apply=%region_7.8 | all-reduce | flops 1 | bytes 8 | tf_op jit(solution)/shard_map/while/body/eval_jaxpr/psum | solution.py:73
  2500.6 0.7 multiply_reduce_fusion.1
  2501.3 49.3 %fusion.3 = bf16[16,128,28,128]{1,3,2,0:T(8,128)(2,1)} fusion(f32[1,16,128,28,128]{2,4,3,1,0:T(8,128)} %get-tuple-element.79, f32[1,16,128,28,128]{2,4,3,1,0:T(8,128)} %get-tuple-element.78, f32[1,16,128,28,128]{2,4,3,1,0:T(8,128)} %get-tuple-element.80, f32[1,16,128,28,128]{2,4,3,1,0:T(8,128)} %get-tuple-element.81, f32[4,16,28]{2,1,0:T(8,128)S(1)} %copy.43), kind=kLoop, calls=%fused_computation.9 | loop fusion | flops 139460608 | bytes 132127744 | tf_op jit(solution)/shard_map/reduce_sum | solution.py:82
  2550.6 16.6 copy.44
  2567.2 22.2 convert_element_type.68
  2589.5 327.8 %all_to_all.16 = bf16[2048,4,896]{0,2,1:T(8,128)(2,1)} all-to-all(bf16[2048,4,896]{0,2,1:T(8,128)(2,1)} %convert_element_type.68), channel_id=1, replica_groups=mesh['dp'=8,'mp'=4] {'mp'}, dimensions={1} | all-to-all | bytes 29360128 | tf_op jit(solution)/shard_map/all_to_all | solution.py:86
  2917.2 20.7 copy.45
  (88 shorter events, 5.7 us)
Async XLA Ops:
  7.2 1366.0 %all-reduce.2.cloned.1.call-start = ((), (), s32[]{:S(2)}) async-start(), calls=%async_computation.1 | async-start | bytes 2097152 | tf_op jit(solution)/shard_map/psum | solution.py:65
  112.6 33.3 %copy-start = (f32[16,28]{1,0:T(8,128)S(1)}, f32[16,28]{1,0:T(8,128)}, u32[]{:S(2)}) copy-start(f32[16,28]{1,0:T(8,128)} %param.16) | copy-start | bytes 5380
  470.7 901.1 %copy-start.2 = (s32[8]{0:T(128)S(1)}, s32[8]{0:T(128)}, u32[]{:S(2)}) copy-start(s32[8]{0:T(128)} %param.17) | copy-start | bytes 100
  1373.1 117.9 %copy-start.1 = (f32[4]{0:T(128)S(1)}, f32[4]{0:T(128)}, u32[]{:S(2)}) copy-start(f32[4]{0:T(128)} %constant.88.clone) | copy-start | bytes 52
Sparse Core Ops, SparseCore 0:
  18.4 59.2 all-reduce.1
where the time goes:
time: 2960 us; the launch traced here: 2950 us
  other arithmetic  1300 us (44%)
  blocking collectives  1300 us (44%)
  local copies, waits for them, and re-layouts  186 us (6%)
  matrix products  129 us (4%)
    another operation x2, other arithmetic, candidates(): return (jnp.stack(errors_list), jnp.stack(levels_list))  1230 us
    psum x24, blocking collectives, trial(): summed = lax.psum(total_rate(table, middle), ('dp', 'mp'))  972 us
    all_to_all x1, blocking collectives, local(): lax.all_to_all(mixed, 'mp', split_axis=1, concat_axis=0, tiled=True)  328 us
    dot_general x1, matrix products, error_table(): jnp.einsum('gij,bgjtc->bgitc', hessian, error_values, precision=lax.Preci...  118 us
    reshape x2, local copies, waits for them, and re-layouts, candidates(): code_grid = grid_codes.reshape(shape)  66.8 us
    convert_element_type x2, local copies, waits for them, and re-layouts, candidates(): residue.reshape(shape).astype(jnp.float32)  59.4 us
  transfers between devices with their start and end apart: 1, of which 0 were waited for; matrix products, arithmetic and copies ran while one was open for 46% of the time, Pallas kernels for 0%

commit v1 on v0

v1 whole, which is shorter than its diff:
```python
import functools

import jax
import jax.numpy as jnp
from jax import lax
from jax.experimental import pallas as pl
from jax.experimental.pallas import tpu as pltpu
from jax.sharding import PartitionSpec as P

GROUP = 128
TRIALS = 24
OTHER = 8
TILES = 14336


BIT_WIDTHS = (2, 3, 4, 8)
ERR_WEIGHT = 16.0
SOFTMAX_WARMTH = 0.03
SLOPE_LIMIT = 16.0
TARGET_BITS = 3.5
MIDDLE = 128
VMEM_LIMIT = 48 * 1024 * 1024
LAST_PARTS = 2

SMALL = pl.CostEstimate(flops=1000, bytes_accessed=1000, transcendentals=0)
ANY = pl.BlockSpec(memory_space=pl.ANY)
SCALARS = pl.BlockSpec(memory_space=pltpu.SMEM)


def params_of():
    return pltpu.CompilerParams(vmem_limit_bytes=VMEM_LIMIT)


def largest_divisor(total, limit, unit):
    best = unit
    for size in range(unit, limit + 1, unit):
        if total % size == 0:
            best = size
    return best


def cast_kernel(where_ref, codes_ref, *rest):
    out_ref = rest[-1]
    out_ref[...] = (codes_ref[...] - MIDDLE).astype(jnp.float32).astype(jnp.bfloat16)


def codes_for(grid_codes, dest, width, first_row, row_count, after):
    if width % 128:
        part = lax.dynamic_slice(grid_codes, (jnp.int32(first_row), dest * width), (row_count, width))
        return (part - MIDDLE).astype(jnp.bfloat16)
    block = largest_divisor(row_count, 256, 16)
    first_block = first_row // block
    return pl.pallas_call(
        cast_kernel,
        out_shape=jax.ShapeDtypeStruct((row_count, width), jnp.bfloat16),
        grid_spec=pltpu.PrefetchScalarGridSpec(
            num_scalar_prefetch=1,
            grid=(row_count // block,),
            in_specs=[pl.BlockSpec((block, width), lambda i, where: (first_block + i, where[0]))] + [ANY] * len(after),
            out_specs=pl.BlockSpec((block, width), lambda i, where: (i, 0)),
        ),
        compiler_params=params_of(),
        cost_estimate=SMALL,
        name="cast_codes",
    )(dest.reshape(1), grid_codes, *after)


def gram_kernel(tokens_ref, *rest):
    out_ref = rest[-1]
    feats = tokens_ref[...]
    out_ref[0] = lax.dot_general(feats, feats, (((0,), (0,)), ((), ())), preferred_element_type=jnp.float32)


def gram_blocks(tokens, after):
    tok_count, width_local = tokens.shape
    group_count = width_local // GROUP
    return pl.pallas_call(
        gram_kernel,
        out_shape=jax.ShapeDtypeStruct((group_count, GROUP, GROUP), jnp.float32),
        grid=(group_count,),
        in_specs=[pl.BlockSpec((tok_count, GROUP), lambda g: (0, g))] + [ANY] * len(after),
        out_specs=pl.BlockSpec((1, GROUP, GROUP), lambda g: (g, 0, 0)),
        compiler_params=params_of(),
        cost_estimate=SMALL,
        name="gram",
    )(tokens, *after)


def table_kernel(token_total, chunk, spans_ref, hessian_ref, codes_ref, residue_ref, out_ref, sums_ref):
    group = pl.program_id(0)
    width = codes_ref.shape[1]
    tile_count = width // GROUP
    per_chunk = chunk // GROUP
    hessian = hessian_ref[0] / token_total
    high = hessian.astype(jnp.bfloat16)
    high_f = high.astype(jnp.float32)
    low = (hessian - high_f).astype(jnp.bfloat16)
    both = jnp.concatenate([high, low], axis=1)
    half_rows = 0.5 * jnp.sum(high_f + low.astype(jnp.float32), axis=1, keepdims=True)
    sums_ref[...] = jnp.zeros_like(sums_ref)

    def weigh(values):
        return jnp.dot(both, jnp.concatenate([values, values], axis=0), preferred_element_type=jnp.float32)

    def one_chunk(index, carry):
        start = pl.multiple_of(index * chunk, chunk)
        codes = codes_ref[:, pl.ds(start, chunk)]
        rest = residue_ref[:, pl.ds(start, chunk)]
        rest_weighted = weigh(rest) - half_rows
        rest_centred = rest.astype(jnp.float32) - 0.5
        spans = [spans_ref[group, index * per_chunk + t] for t in range(per_chunk)]
        for row, bit_width in enumerate(BIT_WIDTHS[:-1]):
            pieces = []
            for t in range(per_chunk):
                mask = jnp.right_shift(spans[t], bit_width) - 1
                inside = jnp.bitwise_and(codes[:, t * GROUP:(t + 1) * GROUP], mask)
                pieces.append(inside.astype(jnp.float32) - 0.5 * mask.astype(jnp.float32))
            offset = jnp.concatenate(pieces, axis=1)
            weighted = weigh(offset.astype(jnp.bfloat16)) + rest_weighted
            sums_ref[row:row + 1, pl.ds(start, chunk)] = jnp.sum((offset + rest_centred) * weighted, axis=0, keepdims=True)
        last = len(BIT_WIDTHS) - 1
        sums_ref[last:last + 1, pl.ds(start, chunk)] = jnp.sum(rest_centred * rest_weighted, axis=0, keepdims=True)
        return carry

    lax.fori_loop(0, width // chunk, one_chunk, 0)
    lanes = lax.broadcasted_iota(jnp.int32, out_ref.shape[1:], 1)
    totals = jnp.zeros(out_ref.shape[1:], jnp.float32)
    for tile in range(tile_count):
        total = jnp.sum(sums_ref[:, tile * GROUP:(tile + 1) * GROUP], axis=1, keepdims=True)
        totals = jnp.where(lanes == tile, total, totals)
    out_ref[0] = totals


def error_sums(hessian, grid_codes, residue, tile_spans, token_total):
    group_count, tile_count = tile_spans.shape
    width = grid_codes.shape[1]
    chunk = 256 if width % 256 == 0 else GROUP
    lanes = -(-tile_count // 128) * 128
    return pl.pallas_call(
        functools.partial(table_kernel, float(token_total), chunk),
        out_shape=jax.ShapeDtypeStruct((group_count, 8, lanes), jnp.float32),
        grid_spec=pltpu.PrefetchScalarGridSpec(
            num_scalar_prefetch=1,
            grid=(group_count,),
            in_specs=[
                pl.BlockSpec((1, GROUP, GROUP), lambda g, spans: (g, 0, 0)),
                pl.BlockSpec((GROUP, width), lambda g, spans: (g, 0)),
                pl.BlockSpec((GROUP, width), lambda g, spans: (g, 0)),
            ],
            out_specs=pl.BlockSpec((1, 8, lanes), lambda g, spans: (g, 0, 0)),
            scratch_shapes=[pltpu.VMEM((8, width), jnp.float32)],
        ),
        compiler_params=params_of(),
        cost_estimate=SMALL,
        name="error_table",
    )(tile_spans, hessian, grid_codes, residue)


def probs_of(tables, slope_now):
    scores = [-(ERR_WEIGHT * t + slope_now * float(b)) / SOFTMAX_WARMTH for t, b in zip(tables, BIT_WIDTHS)]
    top = functools.reduce(jnp.maximum, scores)
    raised = [jnp.exp(score - top) for score in scores]
    total = functools.reduce(jnp.add, raised)
    return raised, total


def bits_of(tables, slope_now):
    raised, total = probs_of(tables, slope_now)
    return functools.reduce(jnp.add, [r * float(b) for r, b in zip(raised, BIT_WIDTHS)]) / total


def slope_kernel(goal_ref, me_ref, all_ref, mine_ref, coef_ref, bits_ref, tables_ref):
    bit_count = len(BIT_WIDTHS)
    for row in range(bit_count):
        tables_ref[row] = all_ref[:, row, :]
    goal = goal_ref[0]

    def trial(index, bounds):
        lower, upper = bounds
        middle = 0.5 * (lower + upper)
        rate = jnp.sum(bits_of([tables_ref[row] for row in range(bit_count)], middle))
        above = rate > goal
        return (jnp.where(above, middle, lower), jnp.where(above, upper, middle))

    lower, upper = lax.fori_loop(0, TRIALS, trial, (jnp.float32(0.0), jnp.float32(SLOPE_LIMIT)))
    slope_final = 0.5 * (lower + upper)

    tables = [mine_ref[row] for row in range(bit_count)]
    spans, scales = mine_ref[bit_count], mine_ref[bit_count + 1]
    bits_ref[...] = bits_of(tables, slope_final)
    raised, total = probs_of(tables, slope_final)
    unit = scales / 128.0
    offset = jnp.zeros_like(unit)
    gains = []
    inverses = []
    for weight, bit_width in zip(raised, BIT_WIDTHS):
        prob = weight / total
        step = jnp.maximum(spans * (0.5 ** bit_width), 1.0)
        gains.append(unit * prob * step)
        inverses.append(1.0 / step)
        offset = offset + 0.5 * unit * prob * step
    rows = [gains[-1], offset] + gains[:-1] + inverses[:-1]
    stacked = jnp.concatenate(rows, axis=0)
    group_total, _, width = coef_ref.shape
    tile_count = unit.shape[1]
    tile = lax.broadcasted_iota(jnp.int32, (tile_count, width), 0)
    column = lax.broadcasted_iota(jnp.int32, (tile_count, width), 1) + me_ref[0] * width
    first = tile * GROUP
    spread = jnp.where((column >= first) & (column < first + GROUP), 1.0, 0.0)
    columns = jnp.dot(stacked, spread, precision=lax.Precision.HIGHEST, preferred_element_type=jnp.float32)
    for row in range(len(rows)):
        coef_ref[:, row, :] = columns[row * group_total:(row + 1) * group_total]


def find_slope(goal, me, gathered, mine, width):
    device_count, _, tile_local = gathered.shape
    _, group_total, tile_count = mine.shape
    whole = pl.BlockSpec(memory_space=pltpu.VMEM)
    return pl.pallas_call(
        slope_kernel,
        out_shape=(
            jax.ShapeDtypeStruct((group_total, 8, width), jnp.float32),
            jax.ShapeDtypeStruct((group_total, tile_count), jnp.float32),
        ),
        in_specs=[SCALARS, SCALARS, whole, whole],
        out_specs=(whole, whole),
        scratch_shapes=[pltpu.VMEM((len(BIT_WIDTHS), device_count, tile_local), jnp.float32)],
        compiler_params=params_of(),
        cost_estimate=SMALL,
        name="find_slope",
    )(goal.reshape(1), me.reshape(1), gathered, mine)


def serve_kernel(groups, where_ref, codes_ref, coef_ref, *rest):
    out_ref = rest[-1]
    for group in range(groups):
        rows = pl.ds(group * GROUP, GROUP)
        codes = codes_ref[rows, :]
        if codes.dtype == jnp.int32:
            codes = codes - MIDDLE
        codes = codes.astype(jnp.float32)
        mixed = coef_ref[group, 1:2, :] + coef_ref[group, 0:1, :] * codes
        for row in range(len(BIT_WIDTHS) - 1):
            gain = coef_ref[group, 2 + row:3 + row, :]
            inverse = coef_ref[group, 5 + row:6 + row, :]
            mixed = mixed + gain * jnp.floor(codes * inverse)
        out_ref[rows, :] = mixed.astype(jnp.bfloat16)


def serve(codes, column_block, coef, source, rows_each, first_row, row_count, served):
    group_total, _, width = coef.shape
    groups = largest_divisor(row_count // GROUP, 2, 1)
    block = groups * GROUP
    first_block = first_row // block
    steps = rows_each // block
    where = jnp.stack([source, column_block])
    whole_codes = codes.shape[0] != row_count or codes.shape[1] != width
    code_first = first_block if whole_codes else 0
    before = [] if served is None else [served]
    return pl.pallas_call(
        functools.partial(serve_kernel, groups),
        out_shape=jax.ShapeDtypeStruct((group_total * GROUP, width), jnp.bfloat16),
        grid_spec=pltpu.PrefetchScalarGridSpec(
            num_scalar_prefetch=1,
            grid=(row_count // block,),
            in_specs=[
                pl.BlockSpec((block, width), lambda i, where: (code_first + i, where[1])),
                pl.BlockSpec((groups, 8, width), lambda i, where: (where[0] * steps + first_block + i, 0, 0)),
            ] + [ANY] * len(before),
            out_specs=pl.BlockSpec((block, width), lambda i, where: (where[0] * steps + first_block + i, 0)),
        ),
        input_output_aliases={3: 0} if before else {},
        compiler_params=params_of(),
        cost_estimate=SMALL,
        name="serve",
    )(where, codes, coef, *before)


def local(tokens, grid_codes, residue, tile_spans, tile_scales, other_bits):
    dp_count, mp_count = lax.axis_size("dp"), lax.axis_size("mp")
    me = lax.axis_index("mp").astype(jnp.int32)
    none = jnp.int32(0)
    rows, columns = grid_codes.shape
    width = columns // mp_count
    group_count, tile_count = tile_spans.shape
    group_total = group_count * mp_count
    token_total = tokens.shape[0] * dp_count

    shifts = sorted(range(1, mp_count), key=lambda k: -min(k, mp_count - k))
    parts = []
    for place, shift in enumerate(shifts):
        pieces = LAST_PARTS if place == len(shifts) - 1 and group_count % LAST_PARTS == 0 else 1
        for piece in range(pieces):
            parts.append((shift, piece * (rows // pieces), rows // pieces))
    arrived = []
    gram = None
    for shift, first_row, row_count in parts:
        dest = lax.rem(me + shift, mp_count)
        after = [] if gram is None else [gram]
        sent = codes_for(grid_codes, dest, width, first_row, row_count, after)
        if gram is None:
            gram = gram_blocks(tokens, [sent])
        arrived.append(lax.ppermute(sent, "mp", [(z, (z + shift) % mp_count) for z in range(mp_count)]))

    hessian = lax.psum(gram, "dp")
    sums = error_sums(hessian, grid_codes, residue, tile_spans, token_total)
    unit = tile_scales / 128.0
    bit_count = len(BIT_WIDTHS)
    table = sums[:, :bit_count, :tile_count] * (unit * unit / float(GROUP * GROUP))[:, None, :]
    mine = jnp.concatenate(
        [
            jnp.transpose(table, (1, 0, 2)).reshape(bit_count, -1),
            tile_spans.astype(jnp.float32).reshape(1, -1),
            tile_scales.reshape(1, -1),
        ]
    )
    gathered = lax.all_gather(mine, ("dp", "mp"))
    goal = TARGET_BITS * (OTHER + 1) * TILES - jnp.sum(other_bits).astype(jnp.float32)
    line = lax.dynamic_slice_in_dim(gathered, lax.axis_index("dp") * mp_count, mp_count, 0)
    line = line.reshape(mp_count, bit_count + 2, group_count, tile_count)
    line = jnp.transpose(line, (1, 0, 2, 3)).reshape(bit_count + 2, group_total, tile_count)
    coef, bits = find_slope(goal, me, gathered, line, width)
    tile_bits = lax.dynamic_slice_in_dim(bits, me * group_count, group_count, 0)

    if width % 128:
        own = codes_for(grid_codes, me, width, 0, rows, [])
        served = serve(own, none, coef, me, rows, 0, rows, None)
    else:
        served = serve(grid_codes, me, coef, me, rows, 0, rows, None)
    for (shift, first_row, row_count), codes in zip(parts, arrived):
        source = lax.rem(me + mp_count - shift, mp_count)
        served = serve(codes, none, coef, source, rows, first_row, row_count, served)
    return (served, tile_bits)


def solution(mesh):
    placed = (P("dp", "mp"), P("mp", "dp"), P("mp", "dp"), P("mp", "dp"), P("mp", "dp"), P())
    return jax.shard_map(
        local,
        mesh=mesh,
        in_specs=placed,
        out_specs=(P(None, ("dp", "mp")), P("mp", "dp")),
        check_vma=False,
    )
```

time: 2960 us -> 451 us (0.15)
  other arithmetic: 1300 us -> 0.91 us
  blocking collectives: 1300 us -> 223 us
  local copies, waits for them, and re-layouts: 186 us -> 2.29 us
  Pallas kernels: 0 us -> 142 us
  matrix products: 129 us -> 0 us
  waiting for transfers between devices: 0.04 us -> 57.5 us
    another operation x2 -> x3, other arithmetic: 1230 us -> 0.23 us  [serve(): where = jnp.stack([source, column_block])]
    psum x24 -> x0, blocking collectives: 972 us -> none  [trial(): summed = lax.psum(total_rate(table, middle), ('dp', 'mp'))]
    all_to_all x1 -> x0, blocking collectives: 328 us -> none  [local(): lax.all_to_all(mixed, 'mp', split_axis=1, concat_axis=0, tiled=True)]
    all_gather x0 -> x1, blocking collectives: none -> 223 us  [local(): gathered = lax.all_gather(mine, ('dp', 'mp'))]
    pallas_call x0 -> x12, Pallas kernels: none -> 142 us  [the longest x1 63.2 us: error_sums(): pl.pallas_call(functools.partial(table_kernel, float(token_total), chunk)...]
    dot_general x2 -> x0, matrix products: 129 us -> none  [the longest x1 118 us: error_table(): jnp.einsum('gij,bgjtc->bgitc', hessian, error_values, precision=lax.Preci...]
    convert_element_type x4 -> x0, local copies, waits for them, and re-layouts: 98.3 us -> none  [the longest x2 59.4 us: candidates(): residue.reshape(shape).astype(jnp.float32)]
    reduce_sum x50 -> x0, other arithmetic: 68.7 us -> none  [the longest x1 49.3 us: local(): jnp.sum(probs[:, :, None, :, None] * levels, axis=0)]
  transfers between devices with their start and end apart: 1 -> 5, of which waited for: 0 -> 1; matrix products, arithmetic and copies ran while one was open for 46% -> 0% of each run, Pallas kernels for 0% -> 29%
where the time goes in v1:
time: 451 us; the launch traced here: 449 us
  blocking collectives  223 us (49%)
  Pallas kernels  142 us (31%)
  waiting for transfers between devices  57.5 us (13%)
  between operations  14.8 us (3%)
  starting transfers between devices  8.04 us (2%)
    all_gather x1, blocking collectives, local(): gathered = lax.all_gather(mine, ('dp', 'mp'))  223 us
    pallas_call x1, Pallas kernels, error_sums(): pl.pallas_call(functools.partial(table_kernel, float(token_total), chunk)...  63.2 us
    psum x1, waiting for transfers between devices, local(): hessian = lax.psum(gram, 'dp')  56.9 us
    pallas_call x5, Pallas kernels, serve(): pl.pallas_call(functools.partial(serve_kernel, groups), out_shape=jax.Sha...  36.8 us
    pallas_call x4, Pallas kernels, codes_for(): pl.pallas_call(cast_kernel, out_shape=jax.ShapeDtypeStruct((row_count, wi...  21.7 us
    pallas_call x1, Pallas kernels, gram_blocks(): pl.pallas_call(gram_kernel, out_shape=jax.ShapeDtypeStruct((group_count,...  12.8 us
  transfers between devices with their start and end apart: 5, of which 1 were waited for; matrix products, arithmetic and copies ran while one was open for 0% of the time, Pallas kernels for 29%

profile of v1, /device:TPU:0, one launch (start us, length us, event | category | flops | bytes accessed | tf_op | source)
XLA Modules:
  0.0 449.1 jit_solution(2468606098206350948)
XLA Ops:
  7.2 7.3 %cast_codes.4.rest_0_ = bf16[2048,896]{1,0:T(8,128)(2,1)} custom-call(s32[1]{0:T(128)} %bitcast.2.where_ref, s32[2048,3584]{1,0:T(8,128)} %codes_ref.11), custom_call_target="tpu_custom_call" | custom-call | flops 1000 | bytes 1000 | tf_op jit(solution)/shard_map/cast_codes/pallas_call | solution.py:53
  14.5 4.0 collective-permute-start.3
  18.5 12.8 %gram.1.rest_0_ = f32[16,128,128]{2,1,0:T(8,128)} custom-call(bf16[2048,2048]{1,0:T(8,128)(2,1)} %tokens_ref.1, bf16[2048,896]{1,0:T(8,128)(2,1)} %cast_codes.4.rest_0_), custom_call_target="tpu_custom_call" | custom-call | flops 1000 | bytes 1000 | tf_op jit(solution)/shard_map/gram/pallas_call | solution.py:77
  31.3 7.4 %cast_codes.7 = bf16[2048,896]{1,0:T(8,128)(2,1)} custom-call(s32[1]{0:T(128)} %bitcast.where_ref, s32[2048,3584]{1,0:T(8,128)} %codes_ref.11, f32[16,128,128]{2,1,0:T(8,128)} %gram.1.rest_0_), custom_call_target="tpu_custom_call" | custom-call | flops 1000 | bytes 1000 | tf_op jit(solution)/shard_map/cast_codes/pallas_call | solution.py:53
  38.7 1.6 collective-permute-start.2
  40.2 4.1 cast_codes.6
  44.4 0.0 copy-start.3
  44.4 0.0 copy-start.2
  44.4 0.0 copy-start.1
  44.4 2.3 collective-permute-start.1
  46.7 2.9 cast_codes.5
  49.6 0.0 all-reduce.2.cloned.1.call-start
  49.6 0.1 collective-permute-start
  49.7 0.6 all-reduce.2.cloned.1.call-update
  50.3 0.0 copy-done.3
  50.3 0.6 reduce_sum.9
  51.6 0.0 copy-done.2
  51.6 0.1 reshape.40
  51.7 0.0 copy-done.1
  51.7 0.1 reshape.39
  51.8 0.1 pad_add_fusion.where_ref
  51.9 0.1 pad_add_fusion.3.where_ref
  52.0 0.1 pad_add_fusion.1
  52.0 56.9 %all-reduce.2.cloned.1.call-done.hessian_ref = f32[16,128,128]{2,1,0:T(8,128)} async-done(((f32[16,128,128]{2,1,0:T(8,128)}), f32[16,128,128]{2,1,0:T(8,128)}) %all-reduce.2.cloned.1.call-update) | async-done | bytes 1048592 | tf_op jit(solution)/shard_map/psum | solution.py:305
  108.9 0.0 copy-start
  108.9 1.2 copy-done
  110.2 63.2 %error_table.1 = f32[16,8,128]{2,1,0:T(8,128)S(1)} custom-call(s32[16,28]{1,0:T(8,128)S(1)} %copy-done.1, f32[16,128,128]{2,1,0:T(8,128)S(1)} %copy-done, s32[2048,3584]{1,0:T(8,128)} %codes_ref.11, bf16[2048,3584]{1,0:T(8,128)(2,1)} %residue_ref.1), custom_call_target="tpu_custom_call" | custom-call | flops 1000 | bytes 1000 | tf_op jit(solution)/shard_map/error_table/pallas_call | solution.py:139
  173.4 0.1 reshape.38
  173.5 223.3 %all-gather.1.all_ref = f32[32,6,448]{2,1,0:T(8,128)S(1)} all-gather(f32[1,6,448]{2,1,0:T(8,128)S(1)} %maximum_bitcast_fusion), channel_id=2, replica_groups=mesh['dp'=8,'mp'=4] {'dp','mp'}, dimensions={0}, use_global_device_ids=true | all-gather | bytes 354816 | tf_op jit(solution)/shard_map/all_gather | solution.py:317
  396.8 0.2 reshape.41
  396.9 7.8 %find_slope.1 = (f32[64,8,896]{2,1,0:T(8,128)S(1)}, f32[64,28]{1,0:T(8,128)S(1)}) custom-call(f32[1]{0:T(128)} %bitcast.3.goal_ref, s32[1]{0:T(128)} %bitcast.4.me_ref, f32[32,6,448]{2,1,0:T(8,128)S(1)} %all-gather.1.all_ref, f32[6,64,28]{2,1,0:T(8,128)S(1)} %bitcast.14), custom_call_target="tpu_custom_call" | custom-call | flops 1000 | bytes 1000 | tf_op jit(solution)/shard_map/find_slope/pallas_call | solution.py:219
  404.8 9.4 %serve.5.rest_0_ = bf16[8192,896]{1,0:T(8,128)(2,1)} custom-call(s32[2]{0:T(128)S(1)} %pad_add_fusion.3.where_ref, s32[2048,3584]{1,0:T(8,128)} %codes_ref.11, f32[64,8,896]{2,1,0:T(8,128)S(1)} %get-tuple-element.4.coef_ref), custom_call_target="tpu_custom_call" | custom-call | flops 1000 | bytes 1000 | tf_op jit(solution)/shard_map/serve/pallas_call | solution.py:260
  414.2 0.6 constant_dynamic-slice_fusion
  414.8 0.0 collective-permute-done.3.codes_ref
  414.8 8.6 %serve.6.rest_0_ = bf16[8192,896]{1,0:T(8,128)(2,1)} custom-call(s32[2]{0:T(128)S(1)} %pad_add_fusion.where_ref, bf16[2048,896]{1,0:T(8,128)(2,1)} %collective-permute-done.3.codes_ref, f32[64,8,896]{2,1,0:T(8,128)S(1)} %get-tuple-element.4.coef_ref, bf16[8192,896]{1,0:T(8,128)(2,1)} %serve.5.rest_0_), custom_call_target="tpu_custom_call", output_to_operand_aliasing={{}: (3, {})} | custom-call | flops 1000 | bytes 1000 | tf_op jit(solution)/shard_map/serve/pallas_call | solution.py:260
  423.4 0.0 collective-permute-done.2.codes_ref
  423.4 8.6 %serve.7.rest_0_ = bf16[8192,896]{1,0:T(8,128)(2,1)} custom-call(s32[2]{0:T(128)S(1)} %get-tuple-element.6.where_ref, bf16[2048,896]{1,0:T(8,128)(2,1)} %collective-permute-done.2.codes_ref, f32[64,8,896]{2,1,0:T(8,128)S(1)} %get-tuple-element.4.coef_ref, bf16[8192,896]{1,0:T(8,128)(2,1)} %serve.6.rest_0_), custom_call_target="tpu_custom_call", output_to_operand_aliasing={{}: (3, {})} | custom-call | flops 1000 | bytes 1000 | tf_op jit(solution)/shard_map/serve/pallas_call | solution.py:260
  431.9 0.0 collective-permute-done.1.codes_ref
  431.9 5.1 %serve.8.rest_0_ = bf16[8192,896]{1,0:T(8,128)(2,1)} custom-call(s32[2]{0:T(128)S(1)} %get-tuple-element.7.where_ref, bf16[1024,896]{1,0:T(8,128)(2,1)} %collective-permute-done.1.codes_ref, f32[64,8,896]{2,1,0:T(8,128)S(1)} %get-tuple-element.4.coef_ref, bf16[8192,896]{1,0:T(8,128)(2,1)} %serve.7.rest_0_), custom_call_target="tpu_custom_call", output_to_operand_aliasing={{}: (3, {})} | custom-call | flops 1000 | bytes 1000 | tf_op jit(solution)/shard_map/serve/pallas_call | solution.py:260
  437.1 0.0 collective-permute-done.codes_ref
  437.1 5.1 %serve.9 = bf16[8192,896]{1,0:T(8,128)(2,1)} custom-call(s32[2]{0:T(128)S(1)} %get-tuple-element.7.where_ref, bf16[1024,896]{1,0:T(8,128)(2,1)} %collective-permute-done.codes_ref, f32[64,8,896]{2,1,0:T(8,128)S(1)} %get-tuple-element.4.coef_ref, bf16[8192,896]{1,0:T(8,128)(2,1)} %serve.8.rest_0_), custom_call_target="tpu_custom_call", output_to_operand_aliasing={{}: (3, {})} | custom-call | flops 1000 | bytes 1000 | tf_op jit(solution)/shard_map/serve/pallas_call | solution.py:260
  (7 shorter events, 0.1 us)
Async XLA Ops:
  14.5 400.3 %collective-permute-start.3 = (bf16[2048,896]{1,0:T(8,128)(2,1)}, bf16[2048,896]{1,0:T(8,128)(2,1)}, u32[]{:S(2)}, u32[]{:S(2)}) collective-permute-start(bf16[2048,896]{1,0:T(8,128)(2,1)} %cast_codes.4.rest_0_), channel_id=1, source_target_pairs={{0,2},{1,3},{2,0},{3,1},{4,6},{5,7},{6,4},{7,5},{8,10},{9,11},{10,... | collective-permute-start | bytes 11010056 | tf_op jit(solution)/shard_map/ppermute | solution.py:303
  38.7 384.7 %collective-permute-start.2 = (bf16[2048,896]{1,0:T(8,128)(2,1)}, bf16[2048,896]{1,0:T(8,128)(2,1)}, u32[]{:S(2)}, u32[]{:S(2)}) collective-permute-start(bf16[2048,896]{1,0:T(8,128)(2,1)} %cast_codes.7), channel_id=1, source_target_pairs={{0,1},{1,2},{2,3},{3,0},{4,5},{5,6},{6,7},{7,4},{8,9},{9,10},{10,1... | collective-permute-start | bytes 11010056 | tf_op jit(solution)/shard_map/ppermute | solution.py:303
  44.4 5.9 %copy-start.3 = (s32[8]{0:T(128)S(1)}, s32[8]{0:T(128)}, u32[]{:S(2)}) copy-start(s32[8]{0:T(128)} %param.11) | copy-start | bytes 100
  44.4 7.2 %copy-start.2 = (f32[16,28]{1,0:T(8,128)S(1)}, f32[16,28]{1,0:T(8,128)}, u32[]{:S(2)}) copy-start(f32[16,28]{1,0:T(8,128)} %param.10) | copy-start | bytes 5380
  44.4 7.3 %copy-start.1 = (s32[16,28]{1,0:T(8,128)S(1)}, s32[16,28]{1,0:T(8,128)}, u32[]{:S(2)}) copy-start(s32[16,28]{1,0:T(8,128)} %spans_ref.1) | copy-start | bytes 5380
  44.4 387.6 %collective-permute-start.1 = (bf16[1024,896]{1,0:T(8,128)(2,1)}, bf16[1024,896]{1,0:T(8,128)(2,1)}, u32[]{:S(2)}, u32[]{:S(2)}) collective-permute-start(bf16[1024,896]{1,0:T(8,128)(2,1)} %cast_codes.6), channel_id=1, source_target_pairs={{0,3},{1,0},{2,1},{3,2},{4,7},{5,4},{6,5},{7,6},{8,11},{9,8},{10,9... | collective-permute-start | bytes 5505032 | tf_op jit(solution)/shard_map/ppermute | solution.py:303
  49.6 59.4 %all-reduce.2.cloned.1.call-start = ((), (), s32[]{:S(2)}) async-start(), calls=%async_computation | async-start | bytes 2097152 | tf_op jit(solution)/shard_map/psum | solution.py:305
  49.6 387.5 %collective-permute-start = (bf16[1024,896]{1,0:T(8,128)(2,1)S(1)}, bf16[1024,896]{1,0:T(8,128)(2,1)}, u32[]{:S(2)}, u32[]{:S(2)}) collective-permute-start(bf16[1024,896]{1,0:T(8,128)(2,1)S(1)} %cast_codes.5), channel_id=1, source_target_pairs={{0,3},{1,0},{2,1},{3,2},{4,7},{5,4},{6,5},{7,6},{8,11},{9,8},{10,9... | collective-permute-start | bytes 5505032 | tf_op jit(solution)/shard_map/ppermute | solution.py:303
  108.9 1.2 copy-start
Sparse Core Ops, SparseCore 0:
  54.1 54.7 all-reduce.1

commit v2 on v1

--- a/solution.py
+++ b/solution.py
@@ -20,7 +20,6 @@
 TARGET_BITS = 3.5
 MIDDLE = 128
 VMEM_LIMIT = 48 * 1024 * 1024
-LAST_PARTS = 2
 
 SMALL = pl.CostEstimate(flops=1000, bytes_accessed=1000, transcendentals=0)
 ANY = pl.BlockSpec(memory_space=pl.ANY)
@@ -86,7 +85,7 @@
     )(tokens, *after)
 
 
-def table_kernel(token_total, chunk, spans_ref, hessian_ref, codes_ref, residue_ref, out_ref, sums_ref):
+def table_kernel(token_total, chunk, spans_ref, hessian_ref, codes_ref, residue_ref, factor_ref, added_ref, out_ref, sums_ref):
     group = pl.program_id(0)
     width = codes_ref.shape[1]
     tile_count = width // GROUP
@@ -128,14 +127,21 @@
     for tile in range(tile_count):
         total = jnp.sum(sums_ref[:, tile * GROUP:(tile + 1) * GROUP], axis=1, keepdims=True)
         totals = jnp.where(lanes == tile, total, totals)
-    out_ref[0] = totals
-
-
-def error_sums(hessian, grid_codes, residue, tile_spans, token_total):
+    out_ref[0] = totals * factor_ref[0] + added_ref[0]
+
+
+def error_table(hessian, grid_codes, residue, tile_spans, tile_scales, token_total):
     group_count, tile_count = tile_spans.shape
     width = grid_codes.shape[1]
     chunk = 256 if width % 256 == 0 else GROUP
     lanes = -(-tile_count // 128) * 128
+    bit_count = len(BIT_WIDTHS)
+    unit = tile_scales / 128.0
+    factor = jnp.broadcast_to((unit * unit / float(GROUP * GROUP))[:, None, :], (group_count, bit_count, tile_count))
+    factor = jnp.pad(factor, ((0, 0), (0, 8 - bit_count), (0, lanes - tile_count)))
+    added = jnp.stack([tile_spans.astype(jnp.float32), tile_scales], axis=1)
+    added = jnp.pad(added, ((0, 0), (bit_count, 6 - bit_count), (0, lanes - tile_count)))
+    rows = pl.BlockSpec((1, 8, lanes), lambda g, spans: (g, 0, 0))
     return pl.pallas_call(
         functools.partial(table_kernel, float(token_total), chunk),
         out_shape=jax.ShapeDtypeStruct((group_count, 8, lanes), jnp.float32),
@@ -146,14 +152,16 @@
                 pl.BlockSpec((1, GROUP, GROUP), lambda g, spans: (g, 0, 0)),
                 pl.BlockSpec((GROUP, width), lambda g, spans: (g, 0)),
                 pl.BlockSpec((GROUP, width), lambda g, spans: (g, 0)),
+                rows,
+                rows,
             ],
-            out_specs=pl.BlockSpec((1, 8, lanes), lambda g, spans: (g, 0, 0)),
+            out_specs=rows,
             scratch_shapes=[pltpu.VMEM((8, width), jnp.float32)],
         ),
         compiler_params=params_of(),
         cost_estimate=SMALL,
         name="error_table",
-    )(tile_spans, hessian, grid_codes, residue)
+    )(tile_spans, hessian, grid_codes, residue, factor, added)
 
 
 def probs_of(tables, slope_now):
@@ -169,24 +177,35 @@
     return functools.reduce(jnp.add, [r * float(b) for r, b in zip(raised, BIT_WIDTHS)]) / total
 
 
-def slope_kernel(goal_ref, me_ref, all_ref, mine_ref, coef_ref, bits_ref, tables_ref):
+def slope_kernel(tile_count, pack, goal_ref, me_ref, all_ref, coef_ref, bits_ref, tables_ref):
     bit_count = len(BIT_WIDTHS)
+    lanes = all_ref.shape[2]
+    pitch = lanes // pack
+    packed_rows = tables_ref.shape[1]
     for row in range(bit_count):
-        tables_ref[row] = all_ref[:, row, :]
+        packed = all_ref[:packed_rows, row, :]
+        for place in range(1, pack):
+            part = all_ref[place * packed_rows:(place + 1) * packed_rows, row, :]
+            packed = packed + pltpu.roll(part, place * pitch, 1)
+        tables_ref[row] = packed
     goal = goal_ref[0]
+    lane = lax.broadcasted_iota(jnp.int32, (packed_rows, lanes), 1)
+    held = lax.rem(lane, jnp.int32(pitch)) < tile_count
 
     def trial(index, bounds):
         lower, upper = bounds
         middle = 0.5 * (lower + upper)
-        rate = jnp.sum(bits_of([tables_ref[row] for row in range(bit_count)], middle))
-        above = rate > goal
+        bits = bits_of([tables_ref[row] for row in range(bit_count)], middle)
+        above = jnp.sum(jnp.where(held, bits, 0.0)) > goal
         return (jnp.where(above, middle, lower), jnp.where(above, upper, middle))
 
     lower, upper = lax.fori_loop(0, TRIALS, trial, (jnp.float32(0.0), jnp.float32(SLOPE_LIMIT)))
     slope_final = 0.5 * (lower + upper)
 
-    tables = [mine_ref[row] for row in range(bit_count)]
-    spans, scales = mine_ref[bit_count], mine_ref[bit_count + 1]
+    group_total, _, width = coef_ref.shape
+    mine = pl.ds(me_ref[0] * group_total, group_total)
+    tables = [all_ref[mine, row, :] for row in range(bit_count)]
+    spans, scales = all_ref[mine, bit_count, :], all_ref[mine, bit_count + 1, :]
     bits_ref[...] = bits_of(tables, slope_final)
     raised, total = probs_of(tables, slope_final)
     unit = scales / 128.0
@@ -201,10 +220,8 @@
         offset = offset + 0.5 * unit * prob * step
     rows = [gains[-1], offset] + gains[:-1] + inverses[:-1]
     stacked = jnp.concatenate(rows, axis=0)
-    group_total, _, width = coef_ref.shape
-    tile_count = unit.shape[1]
-    tile = lax.broadcasted_iota(jnp.int32, (tile_count, width), 0)
-    column = lax.broadcasted_iota(jnp.int32, (tile_count, width), 1) + me_ref[0] * width
+    tile = lax.broadcasted_iota(jnp.int32, (lanes, width), 0)
+    column = lax.broadcasted_iota(jnp.int32, (lanes, width), 1) + me_ref[1] * width
     first = tile * GROUP
     spread = jnp.where((column >= first) & (column < first + GROUP), 1.0, 0.0)
     columns = jnp.dot(stacked, spread, precision=lax.Precision.HIGHEST, preferred_element_type=jnp.float32)
@@ -212,23 +229,23 @@
         coef_ref[:, row, :] = columns[row * group_total:(row + 1) * group_total]
 
 
-def find_slope(goal, me, gathered, mine, width):
-    device_count, _, tile_local = gathered.shape
-    _, group_total, tile_count = mine.shape
+def find_slope(goal, me, gathered, group_total, tile_count, width):
+    group_all, _, lanes = gathered.shape
+    pack = 4 if tile_count <= lanes // 4 and group_all % 32 == 0 else 1
     whole = pl.BlockSpec(memory_space=pltpu.VMEM)
     return pl.pallas_call(
-        slope_kernel,
+        functools.partial(slope_kernel, tile_count, pack),
         out_shape=(
             jax.ShapeDtypeStruct((group_total, 8, width), jnp.float32),
-            jax.ShapeDtypeStruct((group_total, tile_count), jnp.float32),
+            jax.ShapeDtypeStruct((group_total, lanes), jnp.float32),
         ),
-        in_specs=[SCALARS, SCALARS, whole, whole],
+        in_specs=[SCALARS, SCALARS, whole],
         out_specs=(whole, whole),
-        scratch_shapes=[pltpu.VMEM((len(BIT_WIDTHS), device_count, tile_local), jnp.float32)],
+        scratch_shapes=[pltpu.VMEM((len(BIT_WIDTHS), group_all // pack, lanes), jnp.float32)],
         compiler_params=params_of(),
         cost_estimate=SMALL,
         name="find_slope",
-    )(goal.reshape(1), me.reshape(1), gathered, mine)
+    )(goal.reshape(1), me, gathered)
 
 
 def serve_kernel(groups, where_ref, codes_ref, coef_ref, *rest):
@@ -287,11 +304,13 @@
     token_total = tokens.shape[0] * dp_count
 
     shifts = sorted(range(1, mp_count), key=lambda k: -min(k, mp_count - k))
+    short = rows // 4 if group_count % 4 == 0 else rows
     parts = []
     for place, shift in enumerate(shifts):
-        pieces = LAST_PARTS if place == len(shifts) - 1 and group_count % LAST_PARTS == 0 else 1
-        for piece in range(pieces):
-            parts.append((shift, piece * (rows // pieces), rows // pieces))
+        cuts = [0, rows]
+        if place == len(shifts) - 1:
+            cuts = sorted({0, rows - short, rows})
+        parts += [(shift, first, end - first) for first, end in zip(cuts, cuts[1:]) if end > first]
     arrived = []
     gram = None
     for shift, first_row, row_count in parts:
@@ -303,24 +322,12 @@
         arrived.append(lax.ppermute(sent, "mp", [(z, (z + shift) % mp_count) for z in range(mp_count)]))
 
     hessian = lax.psum(gram, "dp")
-    sums = error_sums(hessian, grid_codes, residue, tile_spans, token_total)
-    unit = tile_scales / 128.0
-    bit_count = len(BIT_WIDTHS)
-    table = sums[:, :bit_count, :tile_count] * (unit * unit / float(GROUP * GROUP))[:, None, :]
-    mine = jnp.concatenate(
-        [
-            jnp.transpose(table, (1, 0, 2)).reshape(bit_count, -1),
-            tile_spans.astype(jnp.float32).reshape(1, -1),
-            tile_scales.reshape(1, -1),
-        ]
-    )
-    gathered = lax.all_gather(mine, ("dp", "mp"))
+    table = error_table(hessian, grid_codes, residue, tile_spans, tile_scales, token_total)
+    gathered = lax.all_gather(table, ("dp", "mp"), tiled=True)
     goal = TARGET_BITS * (OTHER + 1) * TILES - jnp.sum(other_bits).astype(jnp.float32)
-    line = lax.dynamic_slice_in_dim(gathered, lax.axis_index("dp") * mp_count, mp_count, 0)
-    line = line.reshape(mp_count, bit_count + 2, group_count, tile_count)
-    line = jnp.transpose(line, (1, 0, 2, 3)).reshape(bit_count + 2, group_total, tile_count)
-    coef, bits = find_slope(goal, me, gathered, line, width)
-    tile_bits = lax.dynamic_slice_in_dim(bits, me * group_count, group_count, 0)
+    places = jnp.stack([lax.axis_index("dp").astype(jnp.int32), me])
+    coef, bits = find_slope(goal, places, gathered, group_total, tile_count, width)
+    tile_bits = lax.dynamic_slice(bits, (me * group_count, none), (group_count, tile_count))
 
     if width % 128:
         own = codes_for(grid_codes, me, width, 0, rows, [])

time: 451 us -> 524 us (1.16)
  the two profiles are of different devices: /device:TPU:0 before, /device:TPU:17 now
where the time goes in v2:
time: 524 us; the launch traced here: 522 us
  waiting for transfers between devices  355 us (68%)
  Pallas kernels  140 us (27%)
  between operations  14.9 us (3%)
  local copies, waits for them, and re-layouts  8.02 us (2%)
    all_gather x1, waiting for transfers between devices, local(): gathered = lax.all_gather(table, ('dp', 'mp'), tiled=True)  268 us
    pallas_call x1, Pallas kernels, error_table(): pl.pallas_call(functools.partial(table_kernel, float(token_total), chunk)...  63.7 us
    psum x1, waiting for transfers between devices, local(): hessian = lax.psum(gram, 'dp')  60.3 us
    pallas_call x5, Pallas kernels, serve(): pl.pallas_call(functools.partial(serve_kernel, groups), out_shape=jax.Sha...  36.7 us
    ppermute x4, waiting for transfers between devices, local(): lax.ppermute(sent, 'mp', [(z, (z + shift) % mp_count) for z in range(mp_c...  25.2 us
    pallas_call x4, Pallas kernels, codes_for(): pl.pallas_call(cast_kernel, out_shape=jax.ShapeDtypeStruct((row_count, wi...  16.8 us
    pallas_call x1, Pallas kernels, gram_blocks(): pl.pallas_call(gram_kernel, out_shape=jax.ShapeDtypeStruct((group_count,...  12.8 us
  transfers between devices with their start and end apart: 6, of which 3 were waited for; matrix products, arithmetic and copies ran while one was open for 0% of the time, Pallas kernels for 8%

profile of v2, /device:TPU:17, one launch (start us, length us, event | category | flops | bytes accessed | tf_op | source)
XLA Modules:
  0.0 522.2 jit_solution(12514752079937633001)
XLA Ops:
  7.2 5.5 %cast_codes.4.rest_0_ = bf16[2048,896]{1,0:T(8,128)(2,1)S(1)} custom-call(s32[1]{0:T(128)} %bitcast.2.where_ref, s32[2048,3584]{1,0:T(8,128)} %codes_ref.11), custom_call_target="tpu_custom_call" | custom-call | flops 1000 | bytes 1000 | tf_op jit(solution)/shard_map/cast_codes/pallas_call | solution.py:52
  12.7 12.8 %gram.1.rest_0_ = f32[16,128,128]{2,1,0:T(8,128)} custom-call(bf16[2048,2048]{1,0:T(8,128)(2,1)} %tokens_ref.1, bf16[2048,896]{1,0:T(8,128)(2,1)S(1)} %cast_codes.4.rest_0_), custom_call_target="tpu_custom_call" | custom-call | flops 1000 | bytes 1000 | tf_op jit(solution)/shard_map/gram/pallas_call | solution.py:76
  25.5 0.0 copy-start
  25.5 1.8 copy-done
  27.3 1.6 cast_codes.5
  28.9 0.0 copy-start.4
  28.9 0.9 copy-done.4
  29.8 4.2 cast_codes.6
  34.0 0.0 copy-start.5
  34.0 0.0 copy-start.6
  34.0 5.5 %cast_codes.7 = bf16[2048,896]{1,0:T(8,128)(2,1)S(1)} custom-call(s32[1]{0:T(128)} %bitcast.where_ref, s32[2048,3584]{1,0:T(8,128)} %codes_ref.11, f32[16,128,128]{2,1,0:T(8,128)} %gram.1.rest_0_), custom_call_target="tpu_custom_call" | custom-call | flops 1000 | bytes 1000 | tf_op jit(solution)/shard_map/cast_codes/pallas_call | solution.py:52
  39.6 0.0 copy-start.1
  39.6 1.8 copy-done.1
  41.4 0.0 all-reduce.4.cloned.1.call-start
  41.4 0.7 all-reduce.4.cloned.1.call-update
  42.2 0.0 all-gather.2.cloned.1.call-start
  42.2 0.0 copy-done.5
  42.2 0.0 copy-done.6
  42.3 60.3 %all-reduce.4.cloned.1.call-done.hessian_ref = f32[16,128,128]{2,1,0:T(8,128)} async-done(((f32[16,128,128]{2,1,0:T(8,128)}), f32[16,128,128]{2,1,0:T(8,128)}) %all-reduce.4.cloned.1.call-update) | async-done | bytes 1048592 | tf_op jit(solution)/shard_map/psum | solution.py:324
  102.6 0.0 copy-start.3
  102.6 1.2 copy-done.3
  103.9 0.0 copy-start.7
  103.9 63.7 %error_table.1 = f32[16,8,128]{2,1,0:T(8,128)} custom-call(s32[16,28]{1,0:T(8,128)S(1)} %copy-done.5, f32[16,128,128]{2,1,0:T(8,128)S(1)} %copy-done.3, s32[2048,3584]{1,0:T(8,128)} %codes_ref.11, bf16[2048,3584]{1,0:T(8,128)(2,1)} %residue_ref.1, f32[16,8,128]{2,1,0:T(8,128)S(1)} %pad.8.factor_ref, f32[16,8,128]{2,1,0:T(8,128)S(1)} %select_maximum_fusion.added_ref), custom_call_target="tpu_custom_call" | custom-call | flops 1000 | bytes 1000 | tf_op jit(solution)/shard_map/error_table/pallas_call | solution.py:145
  167.5 0.0 all-gather.2.cloned.1.call-update
  167.6 0.3 collective-permute-start.3
  167.9 1.2 collective-permute-start.2
  169.1 0.9 collective-permute-start.1
  170.0 1.5 collective-permute-start
  171.5 0.0 copy-done.7
  171.5 0.7 reduce_sum.9
  172.9 0.1 pad_add_fusion.4.where_ref
  172.9 0.1 pad_add_fusion.3.me_ref
  173.0 0.1 pad_add_fusion.where_ref
  173.1 0.1 pad_add_fusion.1
  173.2 268.3 %all-gather.2.cloned.1.call-done.all_ref = f32[512,8,128]{2,1,0:T(8,128)} async-done(((f32[16,8,128]{2,1,0:T(8,128)}), f32[512,8,128]{2,1,0:T(8,128)}) %all-gather.2.cloned.1.call-update) | async-done | bytes 2097168 | tf_op jit(solution)/shard_map/all_gather | solution.py:326
  441.5 0.0 copy-start.2
  441.5 1.6 copy-done.2
  443.1 9.7 %find_slope.1 = (f32[64,8,896]{2,1,0:T(8,128)S(1)}, f32[64,128]{1,0:T(8,128)S(1)}) custom-call(f32[1]{0:T(128)} %bitcast.3.goal_ref, s32[2]{0:T(128)S(1)} %pad_add_fusion.3.me_ref, f32[512,8,128]{2,1,0:T(8,128)S(1)} %copy-done.2), custom_call_target="tpu_custom_call" | custom-call | flops 1000 | bytes 1000 | tf_op jit(solution)/shard_map/find_slope/pallas_call | solution.py:236
  452.8 9.4 %serve.5.rest_0_ = bf16[8192,896]{1,0:T(8,128)(2,1)} custom-call(s32[2]{0:T(128)S(1)} %pad_add_fusion.4.where_ref, s32[2048,3584]{1,0:T(8,128)} %codes_ref.11, f32[64,8,896]{2,1,0:T(8,128)S(1)} %get-tuple-element.4.coef_ref), custom_call_target="tpu_custom_call" | custom-call | flops 1000 | bytes 1000 | tf_op jit(solution)/shard_map/serve/pallas_call | solution.py:277
  462.3 0.0 collective-permute-done.3.codes_ref
  462.3 8.6 %serve.6.rest_0_ = bf16[8192,896]{1,0:T(8,128)(2,1)} custom-call(s32[2]{0:T(128)S(1)} %pad_add_fusion.where_ref, bf16[2048,896]{1,0:T(8,128)(2,1)} %collective-permute-done.3.codes_ref, f32[64,8,896]{2,1,0:T(8,128)S(1)} %get-tuple-element.4.coef_ref, bf16[8192,896]{1,0:T(8,128)(2,1)} %serve.5.rest_0_), custom_call_target="tpu_custom_call", output_to_operand_aliasing={{}: (3, {})} | custom-call | flops 1000 | bytes 1000 | tf_op jit(solution)/shard_map/serve/pallas_call | solution.py:277
  470.8 25.2 %collective-permute-done.2.codes_ref = bf16[2048,896]{1,0:T(8,128)(2,1)} collective-permute-done((bf16[2048,896]{1,0:T(8,128)(2,1)}, bf16[2048,896]{1,0:T(8,128)(2,1)}, u32[]{:S(2)}, u32[]{:S(2)}) %collective-permute-start.2) | collective-permute-done | bytes 3670048 | tf_op jit(solution)/shard_map/ppermute | solution.py:322
  496.0 8.6 %serve.7.rest_0_ = bf16[8192,896]{1,0:T(8,128)(2,1)} custom-call(s32[2]{0:T(128)S(1)} %get-tuple-element.6.where_ref, bf16[2048,896]{1,0:T(8,128)(2,1)} %collective-permute-done.2.codes_ref, f32[64,8,896]{2,1,0:T(8,128)S(1)} %get-tuple-element.4.coef_ref, bf16[8192,896]{1,0:T(8,128)(2,1)} %serve.6.rest_0_), custom_call_target="tpu_custom_call", output_to_operand_aliasing={{}: (3, {})} | custom-call | flops 1000 | bytes 1000 | tf_op jit(solution)/shard_map/serve/pallas_call | solution.py:277
  504.6 0.0 collective-permute-done.1.codes_ref
  504.6 6.8 %serve.8.rest_0_ = bf16[8192,896]{1,0:T(8,128)(2,1)} custom-call(s32[2]{0:T(128)S(1)} %get-tuple-element.7.where_ref, bf16[1536,896]{1,0:T(8,128)(2,1)} %collective-permute-done.1.codes_ref, f32[64,8,896]{2,1,0:T(8,128)S(1)} %get-tuple-element.4.coef_ref, bf16[8192,896]{1,0:T(8,128)(2,1)} %serve.7.rest_0_), custom_call_target="tpu_custom_call", output_to_operand_aliasing={{}: (3, {})} | custom-call | flops 1000 | bytes 1000 | tf_op jit(solution)/shard_map/serve/pallas_call | solution.py:277
  511.4 0.6 constant_dynamic-slice_fusion
  512.0 0.0 collective-permute-done.codes_ref
  512.0 3.3 serve.9
  (5 shorter events, 0.1 us)
Async XLA Ops:
  25.5 1.8 copy-start
  28.9 0.9 copy-start.4
  34.0 8.2 %copy-start.5 = (s32[16,28]{1,0:T(8,128)S(1)}, s32[16,28]{1,0:T(8,128)}, u32[]{:S(2)}) copy-start(s32[16,28]{1,0:T(8,128)} %spans_ref.1) | copy-start | bytes 5380
  34.0 8.2 %copy-start.6 = (f32[16,28]{1,0:T(8,128)S(1)}, f32[16,28]{1,0:T(8,128)}, u32[]{:S(2)}) copy-start(f32[16,28]{1,0:T(8,128)} %param.10) | copy-start | bytes 5380
  39.6 1.9 copy-start.1
  41.4 61.2 %all-reduce.4.cloned.1.call-start = ((), (), s32[]{:S(2)}) async-start(), calls=%async_computation | async-start | bytes 2097152 | tf_op jit(solution)/shard_map/psum | solution.py:324
  42.2 399.3 %all-gather.2.cloned.1.call-start = ((), (), s32[]{:S(2)}) async-start(), calls=%async_computation.1 | async-start | bytes 2162688 | tf_op jit(solution)/shard_map/all_gather | solution.py:326
  102.6 1.2 copy-start.3
  103.9 67.6 %copy-start.7 = (s32[8]{0:T(128)S(1)}, s32[8]{0:T(128)}, u32[]{:S(2)}) copy-start(s32[8]{0:T(128)} %param.11) | copy-start | bytes 100
  167.6 294.7 %collective-permute-start.3 = (bf16[2048,896]{1,0:T(8,128)(2,1)}, bf16[2048,896]{1,0:T(8,128)(2,1)}, u32[]{:S(2)}, u32[]{:S(2)}) collective-permute-start(bf16[2048,896]{1,0:T(8,128)(2,1)} %copy-done), channel_id=1, source_target_pairs={{0,2},{1,3},{2,0},{3,1},{4,6},{5,7},{6,4},{7,5},{8,10},{9,11},{10,... | collective-permute-start | bytes 11010056 | tf_op jit(solution)/shard_map/ppermute | solution.py:322
  167.9 328.1 %collective-permute-start.2 = (bf16[2048,896]{1,0:T(8,128)(2,1)}, bf16[2048,896]{1,0:T(8,128)(2,1)}, u32[]{:S(2)}, u32[]{:S(2)}) collective-permute-start(bf16[2048,896]{1,0:T(8,128)(2,1)} %copy-done.1), channel_id=1, source_target_pairs={{0,1},{1,2},{2,3},{3,0},{4,5},{5,6},{6,7},{7,4},{8,9},{9,10},{10,1... | collective-permute-start | bytes 11010056 | tf_op jit(solution)/shard_map/ppermute | solution.py:322
  169.1 335.5 %collective-permute-start.1 = (bf16[1536,896]{1,0:T(8,128)(2,1)S(1)}, bf16[1536,896]{1,0:T(8,128)(2,1)}, u32[]{:S(2)}, u32[]{:S(2)}) collective-permute-start(bf16[1536,896]{1,0:T(8,128)(2,1)S(1)} %cast_codes.6), channel_id=1, source_target_pairs={{0,3},{1,0},{2,1},{3,2},{4,7},{5,4},{6,5},{7,6},{8,11},{9,8},{10,9... | collective-permute-start | bytes 8257544 | tf_op jit(solution)/shard_map/ppermute | solution.py:322
  170.0 342.0 %collective-permute-start = (bf16[512,896]{1,0:T(8,128)(2,1)}, bf16[512,896]{1,0:T(8,128)(2,1)}, u32[]{:S(2)}, u32[]{:S(2)}) collective-permute-start(bf16[512,896]{1,0:T(8,128)(2,1)} %copy-done.4), channel_id=1, source_target_pairs={{0,3},{1,0},{2,1},{3,2},{4,7},{5,4},{6,5},{7,6},{8,11},{9,8},{10,9... | collective-permute-start | bytes 2752520 | tf_op jit(solution)/shard_map/ppermute | solution.py:322
  441.5 1.6 copy-start.2
Sparse Core Ops, SparseCore 0:
  46.0 56.5 all-reduce.3
  167.7 273.7 all-gather.1

commit v3 on v2

--- a/solution.py
+++ b/solution.py
@@ -36,6 +36,23 @@
         if total % size == 0:
             best = size
     return best
+
+
+def touch_kernel(*refs):
+    pass
+
+
+def once_there(value, after):
+    return pl.pallas_call(
+        touch_kernel,
+        out_shape=jax.ShapeDtypeStruct(value.shape, value.dtype),
+        in_specs=[ANY] * (1 + len(after)),
+        out_specs=ANY,
+        input_output_aliases={0: 0},
+        compiler_params=params_of(),
+        cost_estimate=SMALL,
+        name="once_there",
+    )(value, *after)
 
 
 def cast_kernel(where_ref, codes_ref, *rest):
@@ -264,7 +281,7 @@
         out_ref[rows, :] = mixed.astype(jnp.bfloat16)
 
 
-def serve(codes, column_block, coef, source, rows_each, first_row, row_count, served):
+def serve(codes, column_block, coef, slot, source, rows_each, first_row, row_count, served):
     group_total, _, width = coef.shape
     groups = largest_divisor(row_count // GROUP, 2, 1)
     block = groups * GROUP
@@ -282,7 +299,7 @@
             grid=(row_count // block,),
             in_specs=[
                 pl.BlockSpec((block, width), lambda i, where: (code_first + i, where[1])),
-                pl.BlockSpec((groups, 8, width), lambda i, where: (where[0] * steps + first_block + i, 0, 0)),
+                pl.BlockSpec((groups, 8, width), lambda i, where: (slot * steps + first_block + i, 0, 0)),
             ] + [ANY] * len(before),
             out_specs=pl.BlockSpec((block, width), lambda i, where: (where[0] * steps + first_block + i, 0)),
         ),
@@ -303,40 +320,55 @@
     group_total = group_count * mp_count
     token_total = tokens.shape[0] * dp_count
 
+    def shifted(value, shift):
+        return lax.ppermute(value, "mp", [(z, (z + shift) % mp_count) for z in range(mp_count)])
+
+    def cast(shift, first_row, row_count, after):
+        return codes_for(grid_codes, lax.rem(me + shift, mp_count), width, first_row, row_count, after)
+
     shifts = sorted(range(1, mp_count), key=lambda k: -min(k, mp_count - k))
-    short = rows // 4 if group_count % 4 == 0 else rows
-    parts = []
-    for place, shift in enumerate(shifts):
-        cuts = [0, rows]
-        if place == len(shifts) - 1:
-            cuts = sorted({0, rows - short, rows})
-        parts += [(shift, first, end - first) for first, end in zip(cuts, cuts[1:]) if end > first]
+    loads = [min(k, mp_count - k) for k in shifts]
+    early = max(1, sum(1 for i in range(len(shifts)) if 2 * sum(loads[:i]) < sum(loads)))
+    whole = [(shift, 0, rows) for shift in shifts]
+    first_parts, second_parts = whole[:early], whole[early:]
+    half = rows // 2
+    if second_parts and group_count % 2 == 0:
+        last = second_parts.pop()[0]
+        second_parts += [(last, 0, half), (last, half, half)]
+
     arrived = []
     gram = None
-    for shift, first_row, row_count in parts:
-        dest = lax.rem(me + shift, mp_count)
-        after = [] if gram is None else [gram]
-        sent = codes_for(grid_codes, dest, width, first_row, row_count, after)
+    for part in first_parts:
+        sent = cast(*part, [] if gram is None else [gram])
         if gram is None:
             gram = gram_blocks(tokens, [sent])
-        arrived.append(lax.ppermute(sent, "mp", [(z, (z + shift) % mp_count) for z in range(mp_count)]))
+        arrived.append(shifted(sent, part[0]))
 
     hessian = lax.psum(gram, "dp")
     table = error_table(hessian, grid_codes, residue, tile_spans, tile_scales, token_total)
-    gathered = lax.all_gather(table, ("dp", "mp"), tiled=True)
+    ready = [cast(*part, [table]) for part in second_parts]
+    crossing = once_there(table, arrived)
+    tables = [table] + [shifted(crossing, shift) for shift in range(1, mp_count)]
+    late = []
+    for place, (part, sent) in enumerate(zip(second_parts, ready)):
+        final = place == len(second_parts) - 1 and place > 1
+        after = [late[0]] if final else tables[1:]
+        late.append(shifted(once_there(sent, after), part[0]))
+
+    gathered = lax.all_gather(jnp.concatenate(tables), "dp", tiled=True)
     goal = TARGET_BITS * (OTHER + 1) * TILES - jnp.sum(other_bits).astype(jnp.float32)
     places = jnp.stack([lax.axis_index("dp").astype(jnp.int32), me])
     coef, bits = find_slope(goal, places, gathered, group_total, tile_count, width)
-    tile_bits = lax.dynamic_slice(bits, (me * group_count, none), (group_count, tile_count))
+    tile_bits = bits[:group_count, :tile_count]
 
     if width % 128:
-        own = codes_for(grid_codes, me, width, 0, rows, [])
-        served = serve(own, none, coef, me, rows, 0, rows, None)
+        own = cast(0, 0, rows, [])
+        served = serve(own, none, coef, 0, me, rows, 0, rows, None)
     else:
-        served = serve(grid_codes, me, coef, me, rows, 0, rows, None)
-    for (shift, first_row, row_count), codes in zip(parts, arrived):
+        served = serve(grid_codes, me, coef, 0, me, rows, 0, rows, None)
+    for (shift, first_row, row_count), codes in zip(first_parts + second_parts, arrived + late):
         source = lax.rem(me + mp_count - shift, mp_count)
-        served = serve(codes, none, coef, source, rows, first_row, row_count, served)
+        served = serve(codes, none, coef, shift, source, rows, first_row, row_count, served)
     return (served, tile_bits)
 
 

time: 524 us -> 363 us (0.69)
  the two profiles are of different devices: /device:TPU:17 before, /device:TPU:0 now
where the time goes in v3:
time: 363 us; the launch traced here: 362 us
  waiting for transfers between devices  185 us (51%)
  Pallas kernels  144 us (40%)
  between operations  14.8 us (4%)
  starting transfers between devices  12.1 us (3%)
    ppermute x7, waiting for transfers between devices, shifted(): lax.ppermute(value, 'mp', [(z, (z + shift) % mp_count) for z in range(mp_...  130 us
    pallas_call x1, Pallas kernels, error_table(): pl.pallas_call(functools.partial(table_kernel, float(token_total), chunk)...  63.2 us
    psum x1, waiting for transfers between devices, local(): hessian = lax.psum(gram, 'dp')  55.9 us
    pallas_call x5, Pallas kernels, serve(): pl.pallas_call(functools.partial(serve_kernel, groups), out_shape=jax.Sha...  36.8 us
    pallas_call x4, Pallas kernels, codes_for(): pl.pallas_call(cast_kernel, out_shape=jax.ShapeDtypeStruct((row_count, wi...  21.7 us
    pallas_call x1, Pallas kernels, gram_blocks(): pl.pallas_call(gram_kernel, out_shape=jax.ShapeDtypeStruct((group_count,...  12.7 us
    ppermute x7, starting transfers between devices, shifted(): lax.ppermute(value, 'mp', [(z, (z + shift) % mp_count) for z in range(mp_...  12 us
    pallas_call x1, Pallas kernels, find_slope(): pl.pallas_call(functools.partial(slope_kernel, tile_count, pack), out_sha...  9.73 us
  transfers between devices with their start and end apart: 9, of which 4 were waited for; matrix products, arithmetic and copies ran while one was open for 1% of the time, Pallas kernels for 36%

profile of v3, /device:TPU:0, one launch (start us, length us, event | category | flops | bytes accessed | tf_op | source)
XLA Modules:
  0.0 361.7 jit_solution(13267242081345821369)
XLA Ops:
  7.2 0.0 all-reduce.4.cloned.1.call-start
  7.2 7.3 %cast_codes.4.rest_0_ = bf16[2048,896]{1,0:T(8,128)(2,1)} custom-call(s32[1]{0:T(128)} %bitcast.2.where_ref, s32[2048,3584]{1,0:T(8,128)} %codes_ref.11), custom_call_target="tpu_custom_call" | custom-call | flops 1000 | bytes 1000 | tf_op jit(solution)/shard_map/cast_codes/pallas_call | solution.py:69
  14.5 0.0 copy-start.2
  14.5 0.0 copy-start.3
  14.5 4.0 %collective-permute-start = (bf16[2048,896]{1,0:T(8,128)(2,1)}, bf16[2048,896]{1,0:T(8,128)(2,1)}, u32[]{:S(2)}, u32[]{:S(2)}) collective-permute-start(bf16[2048,896]{1,0:T(8,128)(2,1)} %cast_codes.4.rest_0_), channel_id=1, source_target_pairs={{0,2},{1,3},{2,0},{3,1},{4,6},{5,7},{6,4},{7,5},{8,10},{9,11},{10,... | collective-permute-start | bytes 11010056 | tf_op jit(solution)/shard_map/ppermute | solution.py:324
  18.5 12.7 %gram.1 = f32[16,128,128]{2,1,0:T(8,128)} custom-call(bf16[2048,2048]{1,0:T(8,128)(2,1)} %tokens_ref.1, bf16[2048,896]{1,0:T(8,128)(2,1)} %cast_codes.4.rest_0_), custom_call_target="tpu_custom_call" | custom-call | flops 1000 | bytes 1000 | tf_op jit(solution)/shard_map/gram/pallas_call | solution.py:93
  31.3 0.0 all-reduce.4.cloned.1.call-update
  31.3 0.0 all-gather.2.cloned.1.call-start
  31.4 0.0 copy-done.2
  31.4 0.0 copy-done.3
  31.5 55.9 %all-reduce.4.cloned.1.call-done.hessian_ref = f32[16,128,128]{2,1,0:T(8,128)} async-done(((f32[16,128,128]{2,1,0:T(8,128)}), f32[16,128,128]{2,1,0:T(8,128)}) %all-reduce.4.cloned.1.call-update) | async-done | bytes 1048592 | tf_op jit(solution)/shard_map/psum | solution.py:347
  87.3 0.0 copy-start.1
  87.3 1.2 copy-done.1
  88.6 63.2 %error_table.1.rest_0_ = f32[16,8,128]{2,1,0:T(8,128)S(1)} custom-call(s32[16,28]{1,0:T(8,128)S(1)} %copy-done.2, f32[16,128,128]{2,1,0:T(8,128)S(1)} %copy-done.1, s32[2048,3584]{1,0:T(8,128)} %codes_ref.11, bf16[2048,3584]{1,0:T(8,128)(2,1)} %residue_ref.1, f32[16,8,128]{2,1,0:T(8,128)S(1)} %pad.8.factor_ref, f32[16,8,128]{2,1,0:T(8,128)S(1)} %select_maximum_fusion.added_ref), custom_call_target="tpu_custom_call" | custom-call | flops 1000 | bytes 1000 | tf_op jit(solution)/shard_map/error_table/pallas_call | solution.py:162
  151.8 25.0 %collective-permute-done.refs_1_.codes_ref = bf16[2048,896]{1,0:T(8,128)(2,1)} collective-permute-done((bf16[2048,896]{1,0:T(8,128)(2,1)}, bf16[2048,896]{1,0:T(8,128)(2,1)}, u32[]{:S(2)}, u32[]{:S(2)}) %collective-permute-start) | collective-permute-done | bytes 3670048 | tf_op jit(solution)/shard_map/ppermute | solution.py:324
  176.8 0.7 collective-permute-start.1
  177.6 3.4 collective-permute-start.2
  180.9 0.0 collective-permute-start.3
  180.9 7.3 %cast_codes.6.refs_0_ = bf16[2048,896]{1,0:T(8,128)(2,1)} custom-call(s32[1]{0:T(128)} %bitcast.where_ref, s32[2048,3584]{1,0:T(8,128)} %codes_ref.11, f32[16,8,128]{2,1,0:T(8,128)S(1)} %error_table.1.rest_0_), custom_call_target="tpu_custom_call" | custom-call | flops 1000 | bytes 1000 | tf_op jit(solution)/shard_map/cast_codes/pallas_call | solution.py:69
  188.2 0.0 collective-permute-done.1.refs_1_
  188.2 0.0 collective-permute-done.2.refs_2_
  188.2 0.0 collective-permute-done.3.refs_3_
  188.2 2.1 collective-permute-start.4
  190.3 0.7 pad_maximum_fusion
  191.1 0.0 all-gather.2.cloned.1.call-update
  191.1 4.2 %cast_codes.7.refs_0_ = bf16[1024,896]{1,0:T(8,128)(2,1)} custom-call(s32[1]{0:T(128)} %bitcast.1.where_ref, s32[2048,3584]{1,0:T(8,128)} %codes_ref.11, f32[16,8,128]{2,1,0:T(8,128)S(1)} %error_table.1.rest_0_), custom_call_target="tpu_custom_call" | custom-call | flops 1000 | bytes 1000 | tf_op jit(solution)/shard_map/cast_codes/pallas_call | solution.py:69
  195.3 1.8 collective-permute-start.6
  197.1 3.0 cast_codes.5.refs_0_
  200.0 0.0 copy-start.4
  200.1 72.7 %collective-permute-done.4.refs_1_.codes_ref = bf16[2048,896]{1,0:T(8,128)(2,1)} collective-permute-done((bf16[2048,896]{1,0:T(8,128)(2,1)}, bf16[2048,896]{1,0:T(8,128)(2,1)}, u32[]{:S(2)}, u32[]{:S(2)}) %collective-permute-start.4) | collective-permute-done | bytes 3670048 | tf_op jit(solution)/shard_map/ppermute | solution.py:324
  272.7 0.0 collective-permute-start.5
  272.7 0.0 copy-done.4
  272.7 0.6 reduce_sum.9
  274.0 0.1 pad_add_fusion.4.where_ref
  274.1 0.1 pad_add_fusion.3.me_ref
  274.2 0.1 pad_add_fusion.where_ref
  274.2 0.0 all-gather.2.cloned.1.call-done.all_ref
  274.2 0.0 copy-start
  274.3 1.6 copy-done
  275.8 9.7 %find_slope.1 = (f32[64,8,896]{2,1,0:T(8,128)S(1)}, f32[64,128]{1,0:T(8,128)S(1)}) custom-call(f32[1]{0:T(128)} %bitcast.5.goal_ref, s32[2]{0:T(128)S(1)} %pad_add_fusion.3.me_ref, f32[512,8,128]{2,1,0:T(8,128)S(1)} %copy-done), custom_call_target="tpu_custom_call" | custom-call | flops 1000 | bytes 1000 | tf_op jit(solution)/shard_map/find_slope/pallas_call | solution.py:253
  285.6 9.4 %serve.5.rest_0_ = bf16[8192,896]{1,0:T(8,128)(2,1)} custom-call(s32[2]{0:T(128)S(1)} %pad_add_fusion.4.where_ref, s32[2048,3584]{1,0:T(8,128)} %codes_ref.11, f32[64,8,896]{2,1,0:T(8,128)S(1)} %get-tuple-element.4.coef_ref), custom_call_target="tpu_custom_call" | custom-call | flops 1000 | bytes 1000 | tf_op jit(solution)/shard_map/serve/pallas_call | solution.py:294
  295.0 0.1 pad_add_fusion.1
  295.1 8.6 %serve.6.rest_0_ = bf16[8192,896]{1,0:T(8,128)(2,1)} custom-call(s32[2]{0:T(128)S(1)} %pad_add_fusion.where_ref, bf16[2048,896]{1,0:T(8,128)(2,1)} %collective-permute-done.refs_1_.codes_ref, f32[64,8,896]{2,1,0:T(8,128)S(1)} %get-tuple-element.4.coef_ref, bf16[8192,896]{1,0:T(8,128)(2,1)} %serve.5.rest_0_), custom_call_target="tpu_custom_call", output_to_operand_aliasing={{}: (3, {})} | custom-call | flops 1000 | bytes 1000 | tf_op jit(solution)/shard_map/serve/pallas_call | solution.py:294
  303.6 8.6 %serve.7.rest_0_ = bf16[8192,896]{1,0:T(8,128)(2,1)} custom-call(s32[2]{0:T(128)S(1)} %get-tuple-element.6.where_ref, bf16[2048,896]{1,0:T(8,128)(2,1)} %collective-permute-done.4.refs_1_.codes_ref, f32[64,8,896]{2,1,0:T(8,128)S(1)} %get-tuple-element.4.coef_ref, bf16[8192,896]{1,0:T(8,128)(2,1)} %serve.6.rest_0_), custom_call_target="tpu_custom_call", output_to_operand_aliasing={{}: (3, {})} | custom-call | flops 1000 | bytes 1000 | tf_op jit(solution)/shard_map/serve/pallas_call | solution.py:294
  312.2 0.0 collective-permute-done.6.codes_ref
  312.2 5.1 %serve.8.rest_0_ = bf16[8192,896]{1,0:T(8,128)(2,1)} custom-call(s32[2]{0:T(128)S(1)} %get-tuple-element.7.where_ref, bf16[1024,896]{1,0:T(8,128)(2,1)} %collective-permute-done.6.codes_ref, f32[64,8,896]{2,1,0:T(8,128)S(1)} %get-tuple-element.4.coef_ref, bf16[8192,896]{1,0:T(8,128)(2,1)} %serve.7.rest_0_), custom_call_target="tpu_custom_call", output_to_operand_aliasing={{}: (3, {})} | custom-call | flops 1000 | bytes 1000 | tf_op jit(solution)/shard_map/serve/pallas_call | solution.py:294
  317.3 0.6 slice.3
  317.9 31.8 %collective-permute-done.5.codes_ref = bf16[1024,896]{1,0:T(8,128)(2,1)} collective-permute-done((bf16[1024,896]{1,0:T(8,128)(2,1)S(1)}, bf16[1024,896]{1,0:T(8,128)(2,1)}, u32[]{:S(2)}, u32[]{:S(2)}) %collective-permute-start.5) | collective-permute-done | bytes 1835040 | tf_op jit(solution)/shard_map/ppermute | solution.py:324
  349.8 5.1 %serve.9 = bf16[8192,896]{1,0:T(8,128)(2,1)} custom-call(s32[2]{0:T(128)S(1)} %get-tuple-element.7.where_ref, bf16[1024,896]{1,0:T(8,128)(2,1)} %collective-permute-done.5.codes_ref, f32[64,8,896]{2,1,0:T(8,128)S(1)} %get-tuple-element.4.coef_ref, bf16[8192,896]{1,0:T(8,128)(2,1)} %serve.8.rest_0_), custom_call_target="tpu_custom_call", output_to_operand_aliasing={{}: (3, {})} | custom-call | flops 1000 | bytes 1000 | tf_op jit(solution)/shard_map/serve/pallas_call | solution.py:294
  (10 shorter events, 0.1 us)
Async XLA Ops:
  7.2 80.2 %all-reduce.4.cloned.1.call-start = ((), (), s32[]{:S(2)}) async-start(), calls=%async_computation | async-start | bytes 2097152 | tf_op jit(solution)/shard_map/psum | solution.py:347
  14.5 16.9 %copy-start.2 = (s32[16,28]{1,0:T(8,128)S(1)}, s32[16,28]{1,0:T(8,128)}, u32[]{:S(2)}) copy-start(s32[16,28]{1,0:T(8,128)} %spans_ref.1) | copy-start | bytes 5380
  14.5 16.9 %copy-start.3 = (f32[16,28]{1,0:T(8,128)S(1)}, f32[16,28]{1,0:T(8,128)}, u32[]{:S(2)}) copy-start(f32[16,28]{1,0:T(8,128)} %param.10) | copy-start | bytes 5380
  14.5 162.3 %collective-permute-start = (bf16[2048,896]{1,0:T(8,128)(2,1)}, bf16[2048,896]{1,0:T(8,128)(2,1)}, u32[]{:S(2)}, u32[]{:S(2)}) collective-permute-start(bf16[2048,896]{1,0:T(8,128)(2,1)} %cast_codes.4.rest_0_), channel_id=1, source_target_pairs={{0,2},{1,3},{2,0},{3,1},{4,6},{5,7},{6,4},{7,5},{8,10},{9,11},{10,... | collective-permute-start | bytes 11010056 | tf_op jit(solution)/shard_map/ppermute | solution.py:324
  31.3 242.9 %all-gather.2.cloned.1.call-start = ((), (), s32[]{:S(2)}) async-start(), calls=%async_computation.1 | async-start | bytes 2359296 | tf_op jit(solution)/shard_map/all_gather | solution.py:358
  87.3 1.2 copy-start.1
  176.8 11.4 %collective-permute-start.1 = (f32[16,8,128]{2,1,0:T(8,128)S(1)}, f32[16,8,128]{2,1,0:T(8,128)S(1)}, u32[]{:S(2)}, u32[]{:S(2)}) collective-permute-start(f32[16,8,128]{2,1,0:T(8,128)S(1)} %once_there.4), channel_id=1, source_target_pairs={{0,1},{1,2},{2,3},{3,0},{4,5},{5,6},{6,7},{7,4},{8,9},{9,10},{10,1... | collective-permute-start | bytes 196616 | tf_op jit(solution)/shard_map/ppermute | solution.py:324
  177.6 10.7 %collective-permute-start.2 = (f32[16,8,128]{2,1,0:T(8,128)S(1)}, f32[16,8,128]{2,1,0:T(8,128)S(1)}, u32[]{:S(2)}, u32[]{:S(2)}) collective-permute-start(f32[16,8,128]{2,1,0:T(8,128)S(1)} %once_there.4), channel_id=1, source_target_pairs={{0,2},{1,3},{2,0},{3,1},{4,6},{5,7},{6,4},{7,5},{8,10},{9,11},{10,... | collective-permute-start | bytes 196616 | tf_op jit(solution)/shard_map/ppermute | solution.py:324
  180.9 7.3 %collective-permute-start.3 = (f32[16,8,128]{2,1,0:T(8,128)S(1)}, f32[16,8,128]{2,1,0:T(8,128)S(1)}, u32[]{:S(2)}, u32[]{:S(2)}) collective-permute-start(f32[16,8,128]{2,1,0:T(8,128)S(1)} %once_there.4), channel_id=1, source_target_pairs={{0,3},{1,0},{2,1},{3,2},{4,7},{5,4},{6,5},{7,6},{8,11},{9,8},{10,9... | collective-permute-start | bytes 196616 | tf_op jit(solution)/shard_map/ppermute | solution.py:324
  188.2 84.5 %collective-permute-start.4 = (bf16[2048,896]{1,0:T(8,128)(2,1)}, bf16[2048,896]{1,0:T(8,128)(2,1)}, u32[]{:S(2)}, u32[]{:S(2)}) collective-permute-start(bf16[2048,896]{1,0:T(8,128)(2,1)} %once_there.5), channel_id=1, source_target_pairs={{0,1},{1,2},{2,3},{3,0},{4,5},{5,6},{6,7},{7,4},{8,9},{9,10},{10,1... | collective-permute-start | bytes 11010056 | tf_op jit(solution)/shard_map/ppermute | solution.py:324
  195.3 116.9 %collective-permute-start.6 = (bf16[1024,896]{1,0:T(8,128)(2,1)}, bf16[1024,896]{1,0:T(8,128)(2,1)}, u32[]{:S(2)}, u32[]{:S(2)}) collective-permute-start(bf16[1024,896]{1,0:T(8,128)(2,1)} %once_there.7), channel_id=1, source_target_pairs={{0,3},{1,0},{2,1},{3,2},{4,7},{5,4},{6,5},{7,6},{8,11},{9,8},{10,9... | collective-permute-start | bytes 5505032 | tf_op jit(solution)/shard_map/ppermute | solution.py:324
  200.0 72.7 %copy-start.4 = (s32[8]{0:T(128)S(1)}, s32[8]{0:T(128)}, u32[]{:S(2)}) copy-start(s32[8]{0:T(128)} %param.11) | copy-start | bytes 100
  272.7 77.0 %collective-permute-start.5 = (bf16[1024,896]{1,0:T(8,128)(2,1)S(1)}, bf16[1024,896]{1,0:T(8,128)(2,1)}, u32[]{:S(2)}, u32[]{:S(2)}) collective-permute-start(bf16[1024,896]{1,0:T(8,128)(2,1)S(1)} %once_there.6), channel_id=1, source_target_pairs={{0,3},{1,0},{2,1},{3,2},{4,7},{5,4},{6,5},{7,6},{8,11},{9,8},{10,9... | collective-permute-start | bytes 5505032 | tf_op jit(solution)/shard_map/ppermute | solution.py:324
  274.2 1.6 copy-start
Sparse Core Ops, SparseCore 0:
  31.4 55.8 all-reduce.3
  191.2 27.3 all-gather.1

commit v4 on v3

--- a/solution.py
+++ b/solution.py
@@ -1,4 +1,5 @@
 import functools
+import math
 
 import jax
 import jax.numpy as jnp
@@ -55,30 +56,38 @@
     )(value, *after)
 
 
-def cast_kernel(where_ref, codes_ref, *rest):
-    out_ref = rest[-1]
-    out_ref[...] = (codes_ref[...] - MIDDLE).astype(jnp.float32).astype(jnp.bfloat16)
+def cast_kernel(reads, where_ref, *refs):
+    out_ref = refs[-1]
+    for place, codes_ref in enumerate(refs[:reads]):
+        block = codes_ref.shape[0]
+        centred = (codes_ref[...] - MIDDLE).astype(jnp.float32)
+        out_ref[place * block:(place + 1) * block, :] = centred.astype(jnp.bfloat16)
 
 
 def codes_for(grid_codes, dest, width, first_row, row_count, after):
     if width % 128:
         part = lax.dynamic_slice(grid_codes, (jnp.int32(first_row), dest * width), (row_count, width))
         return (part - MIDDLE).astype(jnp.bfloat16)
-    block = largest_divisor(row_count, 256, 16)
+    reads = 4
+    block = largest_divisor(math.gcd(row_count // reads, first_row), GROUP, GROUP // reads)
     first_block = first_row // block
-    return pl.pallas_call(
-        cast_kernel,
+
+    def read(place):
+        return pl.BlockSpec((block, width), lambda i, where: (first_block + i * reads + place, where[0]))
+
+    return pl.pallas_call(
+        functools.partial(cast_kernel, reads),
         out_shape=jax.ShapeDtypeStruct((row_count, width), jnp.bfloat16),
         grid_spec=pltpu.PrefetchScalarGridSpec(
             num_scalar_prefetch=1,
-            grid=(row_count // block,),
-            in_specs=[pl.BlockSpec((block, width), lambda i, where: (first_block + i, where[0]))] + [ANY] * len(after),
-            out_specs=pl.BlockSpec((block, width), lambda i, where: (i, 0)),
+            grid=(row_count // (reads * block),),
+            in_specs=[read(place) for place in range(reads)] + [ANY] * len(after),
+            out_specs=pl.BlockSpec((reads * block, width), lambda i, where: (i, 0)),
         ),
         compiler_params=params_of(),
         cost_estimate=SMALL,
         name="cast_codes",
-    )(dest.reshape(1), grid_codes, *after)
+    )(dest.reshape(1), *[grid_codes] * reads, *after)
 
 
 def gram_kernel(tokens_ref, *rest):
@@ -102,7 +111,7 @@
     )(tokens, *after)
 
 
-def table_kernel(token_total, chunk, spans_ref, hessian_ref, codes_ref, residue_ref, factor_ref, added_ref, out_ref, sums_ref):
+def table_kernel(token_total, chunk, pack, spans_ref, hessian_ref, codes_ref, residue_ref, factor_ref, added_ref, out_ref, sums_ref):
     group = pl.program_id(0)
     width = codes_ref.shape[1]
     tile_count = width // GROUP
@@ -144,7 +153,18 @@
     for tile in range(tile_count):
         total = jnp.sum(sums_ref[:, tile * GROUP:(tile + 1) * GROUP], axis=1, keepdims=True)
         totals = jnp.where(lanes == tile, total, totals)
-    out_ref[0] = totals * factor_ref[0] + added_ref[0]
+    place = lax.rem(group, pack)
+
+    @pl.when(place == 0)
+    def _():
+        out_ref[...] = jnp.zeros_like(out_ref)
+
+    pitch = out_ref.shape[2] // pack
+    out_ref[0] += pltpu.roll(totals * factor_ref[0] + added_ref[0], place * pitch, 1)
+
+
+def packed_groups(group_count, tile_count):
+    return 4 if tile_count <= 32 and group_count % 4 == 0 else 1
 
 
 def error_table(hessian, grid_codes, residue, tile_spans, tile_scales, token_total):
@@ -152,6 +172,7 @@
     width = grid_codes.shape[1]
     chunk = 256 if width % 256 == 0 else GROUP
     lanes = -(-tile_count // 128) * 128
+    pack = packed_groups(group_count, tile_count)
     bit_count = len(BIT_WIDTHS)
     unit = tile_scales / 128.0
     factor = jnp.broadcast_to((unit * unit / float(GROUP * GROUP))[:, None, :], (group_count, bit_count, tile_count))
@@ -160,8 +181,8 @@
     added = jnp.pad(added, ((0, 0), (bit_count, 6 - bit_count), (0, lanes - tile_count)))
     rows = pl.BlockSpec((1, 8, lanes), lambda g, spans: (g, 0, 0))
     return pl.pallas_call(
-        functools.partial(table_kernel, float(token_total), chunk),
-        out_shape=jax.ShapeDtypeStruct((group_count, 8, lanes), jnp.float32),
+        functools.partial(table_kernel, float(token_total), chunk, pack),
+        out_shape=jax.ShapeDtypeStruct((group_count // pack, 8, lanes), jnp.float32),
         grid_spec=pltpu.PrefetchScalarGridSpec(
             num_scalar_prefetch=1,
             grid=(group_count,),
@@ -172,7 +193,7 @@
                 rows,
                 rows,
             ],
-            out_specs=rows,
+            out_specs=pl.BlockSpec((1, 8, lanes), lambda g, spans: (g // pack, 0, 0)),
             scratch_shapes=[pltpu.VMEM((8, width), jnp.float32)],
         ),
         compiler_params=params_of(),
@@ -196,17 +217,14 @@
 
 def slope_kernel(tile_count, pack, goal_ref, me_ref, all_ref, coef_ref, bits_ref, tables_ref):
     bit_count = len(BIT_WIDTHS)
-    lanes = all_ref.shape[2]
+    line_count, _, _, lanes = all_ref.shape
     pitch = lanes // pack
-    packed_rows = tables_ref.shape[1]
+    line_rows = bits_ref.shape[0]
     for row in range(bit_count):
-        packed = all_ref[:packed_rows, row, :]
-        for place in range(1, pack):
-            part = all_ref[place * packed_rows:(place + 1) * packed_rows, row, :]
-            packed = packed + pltpu.roll(part, place * pitch, 1)
-        tables_ref[row] = packed
+        for line in range(line_count):
+            tables_ref[row, line * line_rows:(line + 1) * line_rows, :] = all_ref[line, :line_rows, row, :]
     goal = goal_ref[0]
-    lane = lax.broadcasted_iota(jnp.int32, (packed_rows, lanes), 1)
+    lane = lax.broadcasted_iota(jnp.int32, tables_ref.shape[1:], 1)
     held = lax.rem(lane, jnp.int32(pitch)) < tile_count
 
     def trial(index, bounds):
@@ -219,10 +237,9 @@
     lower, upper = lax.fori_loop(0, TRIALS, trial, (jnp.float32(0.0), jnp.float32(SLOPE_LIMIT)))
     slope_final = 0.5 * (lower + upper)
 
-    group_total, _, width = coef_ref.shape
-    mine = pl.ds(me_ref[0] * group_total, group_total)
-    tables = [all_ref[mine, row, :] for row in range(bit_count)]
-    spans, scales = all_ref[mine, bit_count, :], all_ref[mine, bit_count + 1, :]
+    width = coef_ref.shape[3]
+    tables = [all_ref[me_ref[0], :line_rows, row, :] for row in range(bit_count)]
+    spans, scales = [all_ref[me_ref[0], :line_rows, row, :] for row in range(bit_count, bit_count + 2)]
     bits_ref[...] = bits_of(tables, slope_final)
     raised, total = probs_of(tables, slope_final)
     unit = scales / 128.0
@@ -237,28 +254,28 @@
         offset = offset + 0.5 * unit * prob * step
     rows = [gains[-1], offset] + gains[:-1] + inverses[:-1]
     stacked = jnp.concatenate(rows, axis=0)
-    tile = lax.broadcasted_iota(jnp.int32, (lanes, width), 0)
+    lane = lax.broadcasted_iota(jnp.int32, (lanes, width), 0)
     column = lax.broadcasted_iota(jnp.int32, (lanes, width), 1) + me_ref[1] * width
-    first = tile * GROUP
-    spread = jnp.where((column >= first) & (column < first + GROUP), 1.0, 0.0)
-    columns = jnp.dot(stacked, spread, precision=lax.Precision.HIGHEST, preferred_element_type=jnp.float32)
-    for row in range(len(rows)):
-        coef_ref[:, row, :] = columns[row * group_total:(row + 1) * group_total]
-
-
-def find_slope(goal, me, gathered, group_total, tile_count, width):
-    group_all, _, lanes = gathered.shape
-    pack = 4 if tile_count <= lanes // 4 and group_all % 32 == 0 else 1
+    for place in range(pack):
+        first = (lane - place * pitch) * GROUP
+        spread = jnp.where((column >= first) & (column < first + GROUP), 1.0, 0.0)
+        columns = jnp.dot(stacked, spread, precision=lax.Precision.HIGHEST, preferred_element_type=jnp.float32)
+        for row in range(len(rows)):
+            coef_ref[:, place, row, :] = columns[row * line_rows:(row + 1) * line_rows]
+
+
+def find_slope(goal, me, gathered, line_rows, pack, tile_count, width):
+    line_count, _, _, lanes = gathered.shape
     whole = pl.BlockSpec(memory_space=pltpu.VMEM)
     return pl.pallas_call(
         functools.partial(slope_kernel, tile_count, pack),
         out_shape=(
-            jax.ShapeDtypeStruct((group_total, 8, width), jnp.float32),
-            jax.ShapeDtypeStruct((group_total, lanes), jnp.float32),
+            jax.ShapeDtypeStruct((line_rows, pack, 8, width), jnp.float32),
+            jax.ShapeDtypeStruct((line_rows, lanes), jnp.float32),
         ),
         in_specs=[SCALARS, SCALARS, whole],
         out_specs=(whole, whole),
-        scratch_shapes=[pltpu.VMEM((len(BIT_WIDTHS), group_all // pack, lanes), jnp.float32)],
+        scratch_shapes=[pltpu.VMEM((len(BIT_WIDTHS), line_count * line_rows, lanes), jnp.float32)],
         compiler_params=params_of(),
         cost_estimate=SMALL,
         name="find_slope",
@@ -267,23 +284,29 @@
 
 def serve_kernel(groups, where_ref, codes_ref, coef_ref, *rest):
     out_ref = rest[-1]
+    width = out_ref.shape[1]
+    piece = 32
     for group in range(groups):
-        rows = pl.ds(group * GROUP, GROUP)
-        codes = codes_ref[rows, :]
-        if codes.dtype == jnp.int32:
-            codes = codes - MIDDLE
-        codes = codes.astype(jnp.float32)
-        mixed = coef_ref[group, 1:2, :] + coef_ref[group, 0:1, :] * codes
-        for row in range(len(BIT_WIDTHS) - 1):
-            gain = coef_ref[group, 2 + row:3 + row, :]
-            inverse = coef_ref[group, 5 + row:6 + row, :]
-            mixed = mixed + gain * jnp.floor(codes * inverse)
-        out_ref[rows, :] = mixed.astype(jnp.bfloat16)
+        for start in range(0, width, 128):
+            lanes = slice(start, min(start + 128, width))
+            gain_last, offset = coef_ref[group, 0:1, lanes], coef_ref[group, 1:2, lanes]
+            gains = [coef_ref[group, 2 + row:3 + row, lanes] for row in range(len(BIT_WIDTHS) - 1)]
+            inverses = [coef_ref[group, 5 + row:6 + row, lanes] for row in range(len(BIT_WIDTHS) - 1)]
+            for first in range(group * GROUP, (group + 1) * GROUP, piece):
+                rows = slice(first, first + piece)
+                codes = codes_ref[rows, lanes]
+                if codes.dtype == jnp.int32:
+                    codes = codes - MIDDLE
+                codes = codes.astype(jnp.float32)
+                mixed = offset + gain_last * codes
+                for gain, inverse in zip(gains, inverses):
+                    mixed = mixed + gain * jnp.floor(codes * inverse)
+                out_ref[rows, lanes] = mixed.astype(jnp.bfloat16)
 
 
 def serve(codes, column_block, coef, slot, source, rows_each, first_row, row_count, served):
     group_total, _, width = coef.shape
-    groups = largest_divisor(row_count // GROUP, 2, 1)
+    groups = 2 if row_count > 2 * GROUP and row_count % (2 * GROUP) == 0 and first_row % (2 * GROUP) == 0 else 1
     block = groups * GROUP
     first_block = first_row // block
     steps = rows_each // block
@@ -331,10 +354,13 @@
     early = max(1, sum(1 for i in range(len(shifts)) if 2 * sum(loads[:i]) < sum(loads)))
     whole = [(shift, 0, rows) for shift in shifts]
     first_parts, second_parts = whole[:early], whole[early:]
-    half = rows // 2
-    if second_parts and group_count % 2 == 0:
-        last = second_parts.pop()[0]
-        second_parts += [(last, 0, half), (last, half, half)]
+    if group_count % 8 == 0:
+        cut = rows // 2
+        last = second_parts.pop()[0] if len(second_parts) > 1 else None
+        second_parts = [(shift, at, cut) for shift, _, _ in second_parts for at in (0, cut)]
+        if last is not None:
+            short = rows // 8
+            second_parts += [(last, 0, cut), (last, cut, cut - short), (last, rows - short, short)]
 
     arrived = []
     gram = None
@@ -346,20 +372,26 @@
 
     hessian = lax.psum(gram, "dp")
     table = error_table(hessian, grid_codes, residue, tile_spans, tile_scales, token_total)
-    ready = [cast(*part, [table]) for part in second_parts]
-    crossing = once_there(table, arrived)
-    tables = [table] + [shifted(crossing, shift) for shift in range(1, mp_count)]
+    tables = [table] + [shifted(table, shift) for shift in range(1, mp_count)]
+    line = jnp.concatenate(tables)
+    line_rows = line.shape[0]
     late = []
-    for place, (part, sent) in enumerate(zip(second_parts, ready)):
-        final = place == len(second_parts) - 1 and place > 1
-        after = [late[0]] if final else tables[1:]
-        late.append(shifted(once_there(sent, after), part[0]))
-
-    gathered = lax.all_gather(jnp.concatenate(tables), "dp", tiled=True)
+    for place, part in enumerate(second_parts):
+        sent = cast(*part, [table])
+        if place == 1:
+            sent = once_there(sent, arrived)
+        elif place > 1:
+            sent = once_there(sent, [late[place - (3 if place == len(second_parts) - 1 and place > 2 else 2)]])
+        late.append(shifted(sent, part[0]))
+
+    line = jnp.pad(line, ((0, max(0, 64 - line_rows)), (0, 0), (0, 0)))
+    gathered = lax.all_gather(line, "dp")
     goal = TARGET_BITS * (OTHER + 1) * TILES - jnp.sum(other_bits).astype(jnp.float32)
     places = jnp.stack([lax.axis_index("dp").astype(jnp.int32), me])
-    coef, bits = find_slope(goal, places, gathered, group_total, tile_count, width)
-    tile_bits = bits[:group_count, :tile_count]
+    pack = packed_groups(group_count, tile_count)
+    coef, bits = find_slope(goal, places, gathered, line_rows, pack, tile_count, width)
+    coef = coef.reshape(group_total, 8, width)
+    tile_bits = bits[:group_count // pack].reshape(group_count, -1)[:, :tile_count]
 
     if width % 128:
         own = cast(0, 0, rows, [])

time: 363 us -> 388 us (1.069)
  starting transfers between devices: 12.1 us -> 75 us
  waiting for transfers between devices: 185 us -> 146 us
    ppermute x7 -> x9, starting transfers between devices: 12 us -> 74.9 us  [shifted(): lax.ppermute(value, 'mp', [(z, (z + shift) % mp_count) for z in range(mp_...]
    ppermute x7 -> x9, waiting for transfers between devices: 130 us -> 90.4 us  [shifted(): lax.ppermute(value, 'mp', [(z, (z + shift) % mp_count) for z in range(mp_...]
    pallas_call x5 -> x7, Pallas kernels: 36.8 us -> 38.9 us  [serve(): pl.pallas_call(functools.partial(serve_kernel, groups), out_shape=jax.Sha...]
    pallas_call x5 -> x7, Pallas kernels: 84.9 us -> 83.8 us  [the longest x1 64.1 us: error_table(): pl.pallas_call(functools.partial(table_kernel, float(token_total), chunk,...]
  transfers between devices with their start and end apart: 9 -> 11, of which waited for: 4 -> 5; matrix products, arithmetic and copies ran while one was open for 1% -> 1% of each run, Pallas kernels for 36% -> 35%
where the time goes in v4:
time: 388 us; the launch traced here: 387 us
  waiting for transfers between devices  146 us (38%)
  Pallas kernels  144 us (37%)
  starting transfers between devices  75 us (19%)
  between operations  14.8 us (4%)
  local copies, waits for them, and re-layouts  5.03 us (1%)
    ppermute x9, waiting for transfers between devices, shifted(): lax.ppermute(value, 'mp', [(z, (z + shift) % mp_count) for z in range(mp_...  90.4 us
    ppermute x9, starting transfers between devices, shifted(): lax.ppermute(value, 'mp', [(z, (z + shift) % mp_count) for z in range(mp_...  74.9 us
    pallas_call x1, Pallas kernels, error_table(): pl.pallas_call(functools.partial(table_kernel, float(token_total), chunk,...  64.1 us
    psum x1, waiting for transfers between devices, local(): hessian = lax.psum(gram, 'dp')  55.9 us
    pallas_call x7, Pallas kernels, serve(): pl.pallas_call(functools.partial(serve_kernel, groups), out_shape=jax.Sha...  38.9 us
    pallas_call x6, Pallas kernels, codes_for(): pl.pallas_call(functools.partial(cast_kernel, reads), out_shape=jax.Shape...  19.7 us
    pallas_call x1, Pallas kernels, gram_blocks(): pl.pallas_call(gram_kernel, out_shape=jax.ShapeDtypeStruct((group_count,...  12.7 us
    pallas_call x1, Pallas kernels, find_slope(): pl.pallas_call(functools.partial(slope_kernel, tile_count, pack), out_sha...  8.8 us
  transfers between devices with their start and end apart: 11, of which 5 were waited for; matrix products, arithmetic and copies ran while one was open for 1% of the time, Pallas kernels for 35%

profile of v4, /device:TPU:0, one launch (start us, length us, event | category | flops | bytes accessed | tf_op | source)
XLA Modules:
  0.0 387.2 jit_solution(17773712409710336636)
XLA Ops:
  7.2 0.0 all-reduce.5.cloned.1.call-start
  7.2 5.4 %cast_codes.6.rest_0_ = bf16[2048,896]{1,0:T(8,128)(2,1)} custom-call(s32[1]{0:T(128)} %bitcast.2.where_ref, s32[2048,3584]{1,0:T(8,128)} %codes_ref.3, s32[2048,3584]{1,0:T(8,128)} %codes_ref.3, s32[2048,3584]{1,0:T(8,128)} %codes_ref.3, s32[2048,3584]{1,0:T(8,128)} %codes_ref.3), custom_call_target="tpu_custom_call" | custom-call | flops 1000 | bytes 1000 | tf_op jit(solution)/shard_map/cast_codes/pallas_call | solution.py:78
  12.7 0.0 copy-start.4
  12.7 0.0 copy-start.5
  12.7 4.1 %collective-permute-start = (bf16[2048,896]{1,0:T(8,128)(2,1)}, bf16[2048,896]{1,0:T(8,128)(2,1)}, u32[]{:S(2)}, u32[]{:S(2)}) collective-permute-start(bf16[2048,896]{1,0:T(8,128)(2,1)} %cast_codes.6.rest_0_), channel_id=1, source_target_pairs={{0,2},{1,3},{2,0},{3,1},{4,6},{5,7},{6,4},{7,5},{8,10},{9,11},{10,... | collective-permute-start | bytes 11010056 | tf_op jit(solution)/shard_map/ppermute | solution.py:347
  16.8 12.7 %gram.1 = f32[16,128,128]{2,1,0:T(8,128)} custom-call(bf16[2048,2048]{1,0:T(8,128)(2,1)} %tokens_ref.1, bf16[2048,896]{1,0:T(8,128)(2,1)} %cast_codes.6.rest_0_), custom_call_target="tpu_custom_call" | custom-call | flops 1000 | bytes 1000 | tf_op jit(solution)/shard_map/gram/pallas_call | solution.py:102
  29.5 0.0 all-reduce.5.cloned.1.call-update
  29.5 0.0 all-gather.3.cloned.1.call-start
  29.6 0.0 copy-done.4
  29.6 0.0 copy-done.5
  29.7 55.9 %all-reduce.5.cloned.1.call-done.hessian_ref = f32[16,128,128]{2,1,0:T(8,128)} async-done(((f32[16,128,128]{2,1,0:T(8,128)}), f32[16,128,128]{2,1,0:T(8,128)}) %all-reduce.5.cloned.1.call-update) | async-done | bytes 1048592 | tf_op jit(solution)/shard_map/psum | solution.py:373
  85.6 0.0 copy-start.3
  85.6 1.2 copy-done.3
  86.8 64.1 %error_table.1.refs_4_ = f32[4,8,128]{2,1,0:T(8,128)S(1)} custom-call(s32[16,28]{1,0:T(8,128)S(1)} %copy-done.4, f32[16,128,128]{2,1,0:T(8,128)S(1)} %copy-done.3, s32[2048,3584]{1,0:T(8,128)} %codes_ref.3, bf16[2048,3584]{1,0:T(8,128)(2,1)} %residue_ref.1, f32[16,8,128]{2,1,0:T(8,128)S(1)} %pad.12.factor_ref, f32[16,8,128]{2,1,0:T(8,128)S(1)} %select_maximum_fusion.3.added_ref), custom_call_target="tpu_custom_call" | custom-call | flops 1000 | bytes 1000 | tf_op jit(solution)/shard_map/error_table/pallas_call | solution.py:183
  150.9 1.3 collective-permute-start.3
  152.3 2.4 collective-permute-start.4
  154.7 1.4 collective-permute-start.5
  156.1 0.6 collective-permute-done.3
  156.7 19.6 %collective-permute-done.4 = f32[4,8,128]{2,1,0:T(8,128)S(1)} collective-permute-done((f32[4,8,128]{2,1,0:T(8,128)S(1)}, f32[4,8,128]{2,1,0:T(8,128)S(1)}, u32[]{:S(2)}, u32[]{:S(2)}) %collective-permute-start.4) | collective-permute-done | bytes 16416 | tf_op jit(solution)/shard_map/ppermute | solution.py:347
  176.2 0.0 collective-permute-done.5
  176.2 0.7 select_maximum_fusion
  177.0 0.0 all-gather.3.cloned.1.call-update
  177.0 3.2 cast_codes.11
  180.2 0.9 collective-permute-start.7
  181.1 3.1 cast_codes.8.refs_0_
  184.2 0.0 collective-permute-done.refs_1_.codes_ref
  184.2 2.2 collective-permute-start.1
  186.5 3.1 cast_codes.10.refs_0_
  189.6 35.6 %collective-permute-done.7.refs_1_.codes_ref = bf16[1024,896]{1,0:T(8,128)(2,1)} collective-permute-done((bf16[1024,896]{1,0:T(8,128)(2,1)}, bf16[1024,896]{1,0:T(8,128)(2,1)}, u32[]{:S(2)}, u32[]{:S(2)}) %collective-permute-start.7) | collective-permute-done | bytes 1835040 | tf_op jit(solution)/shard_map/ppermute | solution.py:347
  225.2 1.9 collective-permute-start.8
  227.1 2.7 cast_codes.9.refs_0_
  229.8 34.7 %collective-permute-done.1.refs_1_.codes_ref = bf16[1024,896]{1,0:T(8,128)(2,1)S(1)} collective-permute-done((bf16[1024,896]{1,0:T(8,128)(2,1)}, bf16[1024,896]{1,0:T(8,128)(2,1)S(1)}, u32[]{:S(2)}, u32[]{:S(2)}) %collective-permute-start.1) | collective-permute-done | bytes 1835040 | tf_op jit(solution)/shard_map/ppermute | solution.py:347
  264.5 0.0 copy-start
  264.5 59.9 %collective-permute-start.6 = (bf16[768,896]{1,0:T(8,128)(2,1)S(1)}, bf16[768,896]{1,0:T(8,128)(2,1)}, u32[]{:S(2)}, u32[]{:S(2)}) collective-permute-start(bf16[768,896]{1,0:T(8,128)(2,1)S(1)} %once_there.6), channel_id=1, source_target_pairs={{0,3},{1,0},{2,1},{3,2},{4,7},{5,4},{6,5},{7,6},{8,11},{9,8},{10,9... | collective-permute-start | bytes 4128776 | tf_op jit(solution)/shard_map/ppermute | solution.py:347
  324.4 2.1 cast_codes.7.refs_0_
  326.5 0.0 copy-done
  326.5 0.0 copy-start.6
  326.5 0.6 collective-permute-start.2
  327.2 0.1 pad_add_fusion.4.where_ref
  327.2 0.0 copy-done.6
  327.2 0.6 reduce_sum.9
  328.5 0.1 pad_add_fusion.3.me_ref
  328.6 0.1 pad_add_fusion.where_ref
  328.7 0.0 all-gather.3.cloned.1.call-done
  328.7 0.0 copy-start.2
  328.7 1.6 copy-done.2
  330.3 8.8 %find_slope.1 = (f32[16,4,8,896]{3,2,1,0:T(8,128)S(1)}, f32[16,128]{1,0:T(8,128)S(1)}) custom-call(f32[1]{0:T(128)} %bitcast.5.goal_ref, s32[2]{0:T(128)S(1)} %pad_add_fusion.3.me_ref, f32[8,64,8,128]{3,2,1,0:T(8,128)S(1)} %bitcast.18), custom_call_target="tpu_custom_call" | custom-call | flops 1000 | bytes 1000 | tf_op jit(solution)/shard_map/find_slope/pallas_call | solution.py:270
  339.1 9.4 %serve.7.rest_0_ = bf16[8192,896]{1,0:T(8,128)(2,1)} custom-call(s32[2]{0:T(128)S(1)} %pad_add_fusion.4.where_ref, s32[2048,3584]{1,0:T(8,128)} %codes_ref.3, f32[64,8,896]{2,1,0:T(8,128)S(1)} %bitcast.11), custom_call_target="tpu_custom_call" | custom-call | flops 1000 | bytes 1000 | tf_op jit(solution)/shard_map/serve/pallas_call | solution.py:317
  348.5 0.1 pad_add_fusion.1.where_ref
  348.6 8.5 %serve.8.rest_0_ = bf16[8192,896]{1,0:T(8,128)(2,1)} custom-call(s32[2]{0:T(128)S(1)} %pad_add_fusion.where_ref, bf16[2048,896]{1,0:T(8,128)(2,1)} %collective-permute-done.refs_1_.codes_ref, f32[64,8,896]{2,1,0:T(8,128)S(1)} %bitcast.12, bf16[8192,896]{1,0:T(8,128)(2,1)} %serve.7.rest_0_), custom_call_target="tpu_custom_call", output_to_operand_aliasing={{}: (3, {})} | custom-call | flops 1000 | bytes 1000 | tf_op jit(solution)/shard_map/serve/pallas_call | solution.py:317
  357.1 0.1 pad_add_fusion.2.where_ref
  357.2 5.1 %serve.9.rest_0_ = bf16[8192,896]{1,0:T(8,128)(2,1)} custom-call(s32[2]{0:T(128)S(1)} %pad_add_fusion.1.where_ref, bf16[1024,896]{1,0:T(8,128)(2,1)} %collective-permute-done.7.refs_1_.codes_ref, f32[64,8,896]{2,1,0:T(8,128)S(1)} %bitcast.13, bf16[8192,896]{1,0:T(8,128)(2,1)} %serve.8.rest_0_), custom_call_target="tpu_custom_call", output_to_operand_aliasing={{}: (3, {})} | custom-call | flops 1000 | bytes 1000 | tf_op jit(solution)/shard_map/serve/pallas_call | solution.py:317
  362.3 0.7 reshape.28
  363.0 0.0 copy-start.1
  363.0 1.5 copy-done.1
  364.5 3.6 serve.10.rest_0_
  368.0 0.0 collective-permute-done.8.codes_ref
  368.0 5.1 %serve.11.rest_0_ = bf16[8192,896]{1,0:T(8,128)(2,1)} custom-call(s32[2]{0:T(128)S(1)} %pad_add_fusion.2.where_ref, bf16[1024,896]{1,0:T(8,128)(2,1)} %collective-permute-done.8.codes_ref, f32[64,8,896]{2,1,0:T(8,128)S(1)} %bitcast.15, bf16[8192,896]{1,0:T(8,128)(2,1)} %serve.10.rest_0_), custom_call_target="tpu_custom_call", output_to_operand_aliasing={{}: (3, {})} | custom-call | flops 1000 | bytes 1000 | tf_op jit(solution)/shard_map/serve/pallas_call | solution.py:317
  373.1 0.0 collective-permute-done.6.codes_ref
  373.1 4.5 %serve.12.rest_0_ = bf16[8192,896]{1,0:T(8,128)(2,1)} custom-call(s32[2]{0:T(128)S(1)} %pad_add_fusion.2.where_ref, bf16[768,896]{1,0:T(8,128)(2,1)} %collective-permute-done.6.codes_ref, f32[64,8,896]{2,1,0:T(8,128)S(1)} %bitcast.16, bf16[8192,896]{1,0:T(8,128)(2,1)} %serve.11.rest_0_), custom_call_target="tpu_custom_call", output_to_operand_aliasing={{}: (3, {})} | custom-call | flops 1000 | bytes 1000 | tf_op jit(solution)/shard_map/serve/pallas_call | solution.py:317
  377.6 0.0 collective-permute-done.2.codes_ref
  377.6 2.7 serve.13
  (10 shorter events, 0.1 us)
Async XLA Ops:
  7.2 78.4 %all-reduce.5.cloned.1.call-start = ((), (), s32[]{:S(2)}) async-start(), calls=%async_computation | async-start | bytes 2097152 | tf_op jit(solution)/shard_map/psum | solution.py:373
  12.7 16.9 %copy-start.4 = (s32[16,28]{1,0:T(8,128)S(1)}, s32[16,28]{1,0:T(8,128)}, u32[]{:S(2)}) copy-start(s32[16,28]{1,0:T(8,128)} %spans_ref.1) | copy-start | bytes 5380
  12.7 16.9 %copy-start.5 = (f32[16,28]{1,0:T(8,128)S(1)}, f32[16,28]{1,0:T(8,128)}, u32[]{:S(2)}) copy-start(f32[16,28]{1,0:T(8,128)} %param.10) | copy-start | bytes 5380
  12.7 171.5 %collective-permute-start = (bf16[2048,896]{1,0:T(8,128)(2,1)}, bf16[2048,896]{1,0:T(8,128)(2,1)}, u32[]{:S(2)}, u32[]{:S(2)}) collective-permute-start(bf16[2048,896]{1,0:T(8,128)(2,1)} %cast_codes.6.rest_0_), channel_id=1, source_target_pairs={{0,2},{1,3},{2,0},{3,1},{4,6},{5,7},{6,4},{7,5},{8,10},{9,11},{10,... | collective-permute-start | bytes 11010056 | tf_op jit(solution)/shard_map/ppermute | solution.py:347
  29.5 299.1 %all-gather.3.cloned.1.call-start = ((), (), s32[]{:S(2)}) async-start(), calls=%async_computation.1 | async-start | bytes 2359296 | tf_op jit(solution)/shard_map/all_gather | solution.py:388
  85.6 1.2 copy-start.3
  150.9 5.8 %collective-permute-start.3 = (f32[4,8,128]{2,1,0:T(8,128)S(1)}, f32[4,8,128]{2,1,0:T(8,128)S(1)}, u32[]{:S(2)}, u32[]{:S(2)}) collective-permute-start(f32[4,8,128]{2,1,0:T(8,128)S(1)} %error_table.1.refs_4_), channel_id=1, source_target_pairs={{0,1},{1,2},{2,3},{3,0},{4,5},{5,6},{6,7},{7,4},{8,9},{9,10},{10,1... | collective-permute-start | bytes 49160 | tf_op jit(solution)/shard_map/ppermute | solution.py:347
  152.3 24.0 %collective-permute-start.4 = (f32[4,8,128]{2,1,0:T(8,128)S(1)}, f32[4,8,128]{2,1,0:T(8,128)S(1)}, u32[]{:S(2)}, u32[]{:S(2)}) collective-permute-start(f32[4,8,128]{2,1,0:T(8,128)S(1)} %error_table.1.refs_4_), channel_id=1, source_target_pairs={{0,2},{1,3},{2,0},{3,1},{4,6},{5,7},{6,4},{7,5},{8,10},{9,11},{10,... | collective-permute-start | bytes 49160 | tf_op jit(solution)/shard_map/ppermute | solution.py:347
  154.7 21.5 %collective-permute-start.5 = (f32[4,8,128]{2,1,0:T(8,128)S(1)}, f32[4,8,128]{2,1,0:T(8,128)S(1)}, u32[]{:S(2)}, u32[]{:S(2)}) collective-permute-start(f32[4,8,128]{2,1,0:T(8,128)S(1)} %error_table.1.refs_4_), channel_id=1, source_target_pairs={{0,3},{1,0},{2,1},{3,2},{4,7},{5,4},{6,5},{7,6},{8,11},{9,8},{10,9... | collective-permute-start | bytes 49160 | tf_op jit(solution)/shard_map/ppermute | solution.py:347
  180.2 45.0 %collective-permute-start.7 = (bf16[1024,896]{1,0:T(8,128)(2,1)}, bf16[1024,896]{1,0:T(8,128)(2,1)}, u32[]{:S(2)}, u32[]{:S(2)}) collective-permute-start(bf16[1024,896]{1,0:T(8,128)(2,1)} %cast_codes.11), channel_id=1, source_target_pairs={{0,1},{1,2},{2,3},{3,0},{4,5},{5,6},{6,7},{7,4},{8,9},{9,10},{10,1... | collective-permute-start | bytes 5505032 | tf_op jit(solution)/shard_map/ppermute | solution.py:347
  184.2 80.2 %collective-permute-start.1 = (bf16[1024,896]{1,0:T(8,128)(2,1)}, bf16[1024,896]{1,0:T(8,128)(2,1)S(1)}, u32[]{:S(2)}, u32[]{:S(2)}) collective-permute-start(bf16[1024,896]{1,0:T(8,128)(2,1)} %once_there.4), channel_id=1, source_target_pairs={{0,1},{1,2},{2,3},{3,0},{4,5},{5,6},{6,7},{7,4},{8,9},{9,10},{10,1... | collective-permute-start | bytes 5505032 | tf_op jit(solution)/shard_map/ppermute | solution.py:347
  225.2 142.9 %collective-permute-start.8 = (bf16[1024,896]{1,0:T(8,128)(2,1)}, bf16[1024,896]{1,0:T(8,128)(2,1)}, u32[]{:S(2)}, u32[]{:S(2)}) collective-permute-start(bf16[1024,896]{1,0:T(8,128)(2,1)} %once_there.7), channel_id=1, source_target_pairs={{0,3},{1,0},{2,1},{3,2},{4,7},{5,4},{6,5},{7,6},{8,11},{9,8},{10,9... | collective-permute-start | bytes 5505032 | tf_op jit(solution)/shard_map/ppermute | solution.py:347
  264.5 62.0 %copy-start = (bf16[1024,896]{1,0:T(8,128)(2,1)}, bf16[1024,896]{1,0:T(8,128)(2,1)S(1)}, u32[]{:S(2)}) copy-start(bf16[1024,896]{1,0:T(8,128)(2,1)S(1)} %collective-permute-done.1.refs_1_.codes_ref) | copy-start | bytes 5505028
  264.5 108.7 %collective-permute-start.6 = (bf16[768,896]{1,0:T(8,128)(2,1)S(1)}, bf16[768,896]{1,0:T(8,128)(2,1)}, u32[]{:S(2)}, u32[]{:S(2)}) collective-permute-start(bf16[768,896]{1,0:T(8,128)(2,1)S(1)} %once_there.6), channel_id=1, source_target_pairs={{0,3},{1,0},{2,1},{3,2},{4,7},{5,4},{6,5},{7,6},{8,11},{9,8},{10,9... | collective-permute-start | bytes 4128776 | tf_op jit(solution)/shard_map/ppermute | solution.py:347
  326.5 0.7 copy-start.6
  326.5 51.1 %collective-permute-start.2 = (bf16[256,896]{1,0:T(8,128)(2,1)}, bf16[256,896]{1,0:T(8,128)(2,1)}, u32[]{:S(2)}, u32[]{:S(2)}) collective-permute-start(bf16[256,896]{1,0:T(8,128)(2,1)} %once_there.5), channel_id=1, source_target_pairs={{0,3},{1,0},{2,1},{3,2},{4,7},{5,4},{6,5},{7,6},{8,11},{9,8},{10,9... | collective-permute-start | bytes 1376264 | tf_op jit(solution)/shard_map/ppermute | solution.py:347
  328.7 1.6 copy-start.2
  363.0 1.5 copy-start.1
Sparse Core Ops, SparseCore 0:
  29.7 55.8 all-reduce.4
  177.1 29.2 all-gather.2

commit v5 on v4

--- a/solution.py
+++ b/solution.py
@@ -19,7 +19,8 @@
 SOFTMAX_WARMTH = 0.03
 SLOPE_LIMIT = 16.0
 TARGET_BITS = 3.5
-MIDDLE = 128
+MIDDLE = 127.5
+ROUNDER = 1.5 * 2.0 ** 23
 VMEM_LIMIT = 48 * 1024 * 1024
 
 SMALL = pl.CostEstimate(flops=1000, bytes_accessed=1000, transcendentals=0)
@@ -60,14 +61,14 @@
     out_ref = refs[-1]
     for place, codes_ref in enumerate(refs[:reads]):
         block = codes_ref.shape[0]
-        centred = (codes_ref[...] - MIDDLE).astype(jnp.float32)
+        centred = codes_ref[...].astype(jnp.float32) - MIDDLE
         out_ref[place * block:(place + 1) * block, :] = centred.astype(jnp.bfloat16)
 
 
 def codes_for(grid_codes, dest, width, first_row, row_count, after):
     if width % 128:
         part = lax.dynamic_slice(grid_codes, (jnp.int32(first_row), dest * width), (row_count, width))
-        return (part - MIDDLE).astype(jnp.bfloat16)
+        return (part.astype(jnp.float32) - MIDDLE).astype(jnp.bfloat16)
     reads = 4
     block = largest_divisor(math.gcd(row_count // reads, first_row), GROUP, GROUP // reads)
     first_block = first_row // block
@@ -245,14 +246,13 @@
     unit = scales / 128.0
     offset = jnp.zeros_like(unit)
     gains = []
-    inverses = []
-    for weight, bit_width in zip(raised, BIT_WIDTHS):
-        prob = weight / total
+    steps = []
+    for weight, bit_width in zip(raised[:-1], BIT_WIDTHS):
         step = jnp.maximum(spans * (0.5 ** bit_width), 1.0)
-        gains.append(unit * prob * step)
-        inverses.append(1.0 / step)
-        offset = offset + 0.5 * unit * prob * step
-    rows = [gains[-1], offset] + gains[:-1] + inverses[:-1]
+        gains.append(unit * (weight / total))
+        steps.append(step)
+        offset = offset + gains[-1] * (0.5 * step)
+    rows = [unit * (raised[-1] / total), offset] + gains + steps
     stacked = jnp.concatenate(rows, axis=0)
     lane = lax.broadcasted_iota(jnp.int32, (lanes, width), 0)
     column = lax.broadcasted_iota(jnp.int32, (lanes, width), 1) + me_ref[1] * width
@@ -291,16 +291,17 @@
             lanes = slice(start, min(start + 128, width))
             gain_last, offset = coef_ref[group, 0:1, lanes], coef_ref[group, 1:2, lanes]
             gains = [coef_ref[group, 2 + row:3 + row, lanes] for row in range(len(BIT_WIDTHS) - 1)]
-            inverses = [coef_ref[group, 5 + row:6 + row, lanes] for row in range(len(BIT_WIDTHS) - 1)]
+            steps = [coef_ref[group, 5 + row:6 + row, lanes] for row in range(len(BIT_WIDTHS) - 1)]
+            halves = [0.5 * step for step in steps]
+            rounders = [ROUNDER * step for step in steps]
             for first in range(group * GROUP, (group + 1) * GROUP, piece):
                 rows = slice(first, first + piece)
-                codes = codes_ref[rows, lanes]
-                if codes.dtype == jnp.int32:
+                codes = codes_ref[rows, lanes].astype(jnp.float32)
+                if codes_ref.dtype == jnp.int32:
                     codes = codes - MIDDLE
-                codes = codes.astype(jnp.float32)
                 mixed = offset + gain_last * codes
-                for gain, inverse in zip(gains, inverses):
-                    mixed = mixed + gain * jnp.floor(codes * inverse)
+                for gain, half, rounder in zip(gains, halves, rounders):
+                    mixed = mixed + gain * (((codes - half) + rounder) - rounder)
                 out_ref[rows, lanes] = mixed.astype(jnp.bfloat16)
 
 
@@ -354,13 +355,10 @@
     early = max(1, sum(1 for i in range(len(shifts)) if 2 * sum(loads[:i]) < sum(loads)))
     whole = [(shift, 0, rows) for shift in shifts]
     first_parts, second_parts = whole[:early], whole[early:]
-    if group_count % 8 == 0:
-        cut = rows // 2
-        last = second_parts.pop()[0] if len(second_parts) > 1 else None
-        second_parts = [(shift, at, cut) for shift, _, _ in second_parts for at in (0, cut)]
-        if last is not None:
-            short = rows // 8
-            second_parts += [(last, 0, cut), (last, cut, cut - short), (last, rows - short, short)]
+    if group_count % 8 == 0 and len(second_parts) > 1:
+        last = second_parts.pop()[0]
+        cut, short = rows // 2, rows // 8
+        second_parts += [(last, 0, cut), (last, cut, cut - short), (last, rows - short, short)]
 
     arrived = []
     gram = None
@@ -372,16 +370,17 @@
 
     hessian = lax.psum(gram, "dp")
     table = error_table(hessian, grid_codes, residue, tile_spans, tile_scales, token_total)
-    tables = [table] + [shifted(table, shift) for shift in range(1, mp_count)]
-    line = jnp.concatenate(tables)
+    ready = [cast(*part, [table]) for part in second_parts]
+    crossing = once_there(table, ready[:1])
+    tables = [table] + [shifted(crossing, shift) for shift in range(1, mp_count)]
+    line = once_there(jnp.concatenate(tables), arrived)
     line_rows = line.shape[0]
     late = []
-    for place, part in enumerate(second_parts):
-        sent = cast(*part, [table])
+    for place, (part, sent) in enumerate(zip(second_parts, ready)):
         if place == 1:
             sent = once_there(sent, arrived)
         elif place > 1:
-            sent = once_there(sent, [late[place - (3 if place == len(second_parts) - 1 and place > 2 else 2)]])
+            sent = once_there(sent, [late[0]])
         late.append(shifted(sent, part[0]))
 
     line = jnp.pad(line, ((0, max(0, 64 - line_rows)), (0, 0), (0, 0)))

time: 388 us -> 353 us (0.910)
  starting transfers between devices: 75 us -> 14.9 us
  waiting for transfers between devices: 146 us -> 171 us
    ppermute x9 -> x8, starting transfers between devices: 74.9 us -> 14.8 us  [shifted(): lax.ppermute(value, 'mp', [(z, (z + shift) % mp_count) for z in range(mp_...]
    all_gather x1, waiting for transfers between devices: 0.01 us -> 15.1 us  [local(): gathered = lax.all_gather(line, 'dp')]
    ppermute x9 -> x8, waiting for transfers between devices: 90.4 us -> 99.5 us  [shifted(): lax.ppermute(value, 'mp', [(z, (z + shift) % mp_count) for z in range(mp_...]
    pallas_call x7 -> x6, Pallas kernels: 38.9 us -> 40.5 us  [serve(): pl.pallas_call(functools.partial(serve_kernel, groups), out_shape=jax.Sha...]
    pallas_call x6 -> x5, Pallas kernels: 19.7 us -> 18.9 us  [codes_for(): pl.pallas_call(functools.partial(cast_kernel, reads), out_shape=jax.Shape...]
  transfers between devices with their start and end apart: 11 -> 10, of which waited for: 5 -> 6; matrix products, arithmetic and copies ran while one was open for 1% -> 1% of each run, Pallas kernels for 35% -> 39%
where the time goes in v5:
time: 353 us; the launch traced here: 351 us
  waiting for transfers between devices  171 us (48%)
  Pallas kernels  145 us (41%)
  starting transfers between devices  14.9 us (4%)
  between operations  14.9 us (4%)
  local copies, waits for them, and re-layouts  4.79 us (1%)
    ppermute x8, waiting for transfers between devices, shifted(): lax.ppermute(value, 'mp', [(z, (z + shift) % mp_count) for z in range(mp_...  99.5 us
    pallas_call x1, Pallas kernels, error_table(): pl.pallas_call(functools.partial(table_kernel, float(token_total), chunk,...  64.1 us
    psum x1, waiting for transfers between devices, local(): hessian = lax.psum(gram, 'dp')  55.8 us
    pallas_call x6, Pallas kernels, serve(): pl.pallas_call(functools.partial(serve_kernel, groups), out_shape=jax.Sha...  40.5 us
    pallas_call x5, Pallas kernels, codes_for(): pl.pallas_call(functools.partial(cast_kernel, reads), out_shape=jax.Shape...  18.9 us
    all_gather x1, waiting for transfers between devices, local(): gathered = lax.all_gather(line, 'dp')  15.1 us
    ppermute x8, starting transfers between devices, shifted(): lax.ppermute(value, 'mp', [(z, (z + shift) % mp_count) for z in range(mp_...  14.8 us
    pallas_call x1, Pallas kernels, gram_blocks(): pl.pallas_call(gram_kernel, out_shape=jax.ShapeDtypeStruct((group_count,...  12.7 us
  transfers between devices with their start and end apart: 10, of which 6 were waited for; matrix products, arithmetic and copies ran while one was open for 1% of the time, Pallas kernels for 39%

profile of v5, /device:TPU:0, one launch (start us, length us, event | category | flops | bytes accessed | tf_op | source)
XLA Modules:
  0.0 351.3 jit_solution(10572085716101752799)
XLA Ops:
  7.2 0.0 all-reduce.5.cloned.1.call-start
  7.2 5.4 %cast_codes.5.rest_0_ = bf16[2048,896]{1,0:T(8,128)(2,1)} custom-call(s32[1]{0:T(128)} %bitcast.2.where_ref, s32[2048,3584]{1,0:T(8,128)} %codes_ref.3, s32[2048,3584]{1,0:T(8,128)} %codes_ref.3, s32[2048,3584]{1,0:T(8,128)} %codes_ref.3, s32[2048,3584]{1,0:T(8,128)} %codes_ref.3), custom_call_target="tpu_custom_call" | custom-call | flops 1000 | bytes 1000 | tf_op jit(solution)/shard_map/cast_codes/pallas_call | solution.py:79
  12.7 0.0 copy-start.2
  12.7 0.0 copy-start.3
  12.7 4.1 %collective-permute-start.5 = (bf16[2048,896]{1,0:T(8,128)(2,1)}, bf16[2048,896]{1,0:T(8,128)(2,1)}, u32[]{:S(2)}, u32[]{:S(2)}) collective-permute-start(bf16[2048,896]{1,0:T(8,128)(2,1)} %cast_codes.5.rest_0_), channel_id=1, source_target_pairs={{0,2},{1,3},{2,0},{3,1},{4,6},{5,7},{6,4},{7,5},{8,10},{9,11},{10,... | collective-permute-start | bytes 11010056 | tf_op jit(solution)/shard_map/ppermute | solution.py:348
  16.8 12.7 %gram.1 = f32[16,128,128]{2,1,0:T(8,128)} custom-call(bf16[2048,2048]{1,0:T(8,128)(2,1)} %tokens_ref.1, bf16[2048,896]{1,0:T(8,128)(2,1)} %cast_codes.5.rest_0_), custom_call_target="tpu_custom_call" | custom-call | flops 1000 | bytes 1000 | tf_op jit(solution)/shard_map/gram/pallas_call | solution.py:103
  29.5 0.0 all-reduce.5.cloned.1.call-update
  29.5 0.0 all-gather.3.cloned.1.call-start
  29.6 0.0 copy-done.2
  29.6 0.0 copy-done.3
  29.7 55.8 %all-reduce.5.cloned.1.call-done.hessian_ref = f32[16,128,128]{2,1,0:T(8,128)} async-done(((f32[16,128,128]{2,1,0:T(8,128)}), f32[16,128,128]{2,1,0:T(8,128)}) %all-reduce.5.cloned.1.call-update) | async-done | bytes 1048592 | tf_op jit(solution)/shard_map/psum | solution.py:371
  85.5 0.0 copy-start.1
  85.5 1.2 copy-done.1
  86.8 64.1 %error_table.1.refs_4_ = f32[4,8,128]{2,1,0:T(8,128)S(1)} custom-call(s32[16,28]{1,0:T(8,128)S(1)} %copy-done.2, f32[16,128,128]{2,1,0:T(8,128)S(1)} %copy-done.1, s32[2048,3584]{1,0:T(8,128)} %codes_ref.3, bf16[2048,3584]{1,0:T(8,128)(2,1)} %residue_ref.1, f32[16,8,128]{2,1,0:T(8,128)S(1)} %pad.12.factor_ref, f32[16,8,128]{2,1,0:T(8,128)S(1)} %select_maximum_fusion.added_ref), custom_call_target="tpu_custom_call" | custom-call | flops 1000 | bytes 1000 | tf_op jit(solution)/shard_map/error_table/pallas_call | solution.py:184
  150.9 5.4 %cast_codes.7.refs_1_ = bf16[2048,896]{1,0:T(8,128)(2,1)} custom-call(s32[1]{0:T(128)} %bitcast.where_ref, s32[2048,3584]{1,0:T(8,128)} %codes_ref.3, s32[2048,3584]{1,0:T(8,128)} %codes_ref.3, s32[2048,3584]{1,0:T(8,128)} %codes_ref.3, s32[2048,3584]{1,0:T(8,128)} %codes_ref.3, f32[4,8,128]{2,1,0:T(8,128)S(1)} %error_table.1.refs_4_), custom_call_target="tpu_custom_call" | custom-call | flops 1000 | bytes 1000 | tf_op jit(solution)/shard_map/cast_codes/pallas_call | solution.py:79
  156.3 1.3 collective-permute-start
  157.7 1.5 collective-permute-start.2
  159.1 1.6 collective-permute-start.3
  160.7 2.3 collective-permute-start.4
  163.0 76.2 %collective-permute-done.2 = f32[4,8,128]{2,1,0:T(8,128)S(1)} collective-permute-done((f32[4,8,128]{2,1,0:T(8,128)S(1)}, f32[4,8,128]{2,1,0:T(8,128)S(1)}, u32[]{:S(2)}, u32[]{:S(2)}) %collective-permute-start.2) | collective-permute-done | bytes 16416 | tf_op jit(solution)/shard_map/ppermute | solution.py:348
  239.2 15.7 %collective-permute-done.3 = f32[4,8,128]{2,1,0:T(8,128)S(1)} collective-permute-done((f32[4,8,128]{2,1,0:T(8,128)S(1)}, f32[4,8,128]{2,1,0:T(8,128)S(1)}, u32[]{:S(2)}, u32[]{:S(2)}) %collective-permute-start.3) | collective-permute-done | bytes 16416 | tf_op jit(solution)/shard_map/ppermute | solution.py:348
  254.9 0.0 collective-permute-done.4
  254.9 0.0 collective-permute-done.5.refs_1_.codes_ref
  254.9 0.7 pad.14
  255.6 0.0 all-gather.3.cloned.1.call-update
  255.7 3.1 cast_codes.9.refs_0_
  258.8 3.7 %collective-permute-start.7 = (bf16[1024,896]{1,0:T(8,128)(2,1)}, bf16[1024,896]{1,0:T(8,128)(2,1)}, u32[]{:S(2)}, u32[]{:S(2)}) collective-permute-start(bf16[1024,896]{1,0:T(8,128)(2,1)} %once_there.9), channel_id=1, source_target_pairs={{0,3},{1,0},{2,1},{3,2},{4,7},{5,4},{6,5},{7,6},{8,11},{9,8},{10,9... | collective-permute-start | bytes 5505032 | tf_op jit(solution)/shard_map/ppermute | solution.py:348
  262.5 2.8 cast_codes.8.refs_0_
  265.3 0.0 collective-permute-done.refs_1_.codes_ref
  265.3 0.2 collective-permute-start.6
  265.6 2.1 cast_codes.6.refs_0_
  267.7 0.0 copy-start.4
  267.7 0.0 collective-permute-start.1
  267.7 0.1 pad_add_fusion.4.where_ref
  267.8 0.5 copy-done.4
  268.4 0.7 reduce_sum.9
  269.8 0.1 pad_add_fusion.3.me_ref
  269.8 0.1 pad_add_fusion.where_ref
  269.9 15.1 %all-gather.3.cloned.1.call-done = f32[512,8,128]{2,1,0:T(8,128)} async-done(((f32[64,8,128]{2,1,0:T(8,128)}), f32[512,8,128]{2,1,0:T(8,128)}) %all-gather.3.cloned.1.call-update) | async-done | bytes 2097168 | tf_op jit(solution)/shard_map/all_gather | solution.py:387
  285.1 0.0 copy-start
  285.1 1.6 copy-done
  286.7 8.8 %find_slope.1 = (f32[16,4,8,896]{3,2,1,0:T(8,128)S(1)}, f32[16,128]{1,0:T(8,128)S(1)}) custom-call(f32[1]{0:T(128)} %bitcast.5.goal_ref, s32[2]{0:T(128)S(1)} %pad_add_fusion.3.me_ref, f32[8,64,8,128]{3,2,1,0:T(8,128)S(1)} %bitcast.17), custom_call_target="tpu_custom_call" | custom-call | flops 1000 | bytes 1000 | tf_op jit(solution)/shard_map/find_slope/pallas_call | solution.py:270
  295.4 9.9 %serve.6.rest_0_ = bf16[8192,896]{1,0:T(8,128)(2,1)} custom-call(s32[2]{0:T(128)S(1)} %pad_add_fusion.4.where_ref, s32[2048,3584]{1,0:T(8,128)} %codes_ref.3, f32[64,8,896]{2,1,0:T(8,128)S(1)} %bitcast.11), custom_call_target="tpu_custom_call" | custom-call | flops 1000 | bytes 1000 | tf_op jit(solution)/shard_map/serve/pallas_call | solution.py:318
  305.3 0.1 pad_add_fusion.1.where_ref
  305.4 8.9 %serve.7.rest_0_ = bf16[8192,896]{1,0:T(8,128)(2,1)} custom-call(s32[2]{0:T(128)S(1)} %pad_add_fusion.where_ref, bf16[2048,896]{1,0:T(8,128)(2,1)} %collective-permute-done.5.refs_1_.codes_ref, f32[64,8,896]{2,1,0:T(8,128)S(1)} %bitcast.12, bf16[8192,896]{1,0:T(8,128)(2,1)} %serve.6.rest_0_), custom_call_target="tpu_custom_call", output_to_operand_aliasing={{}: (3, {})} | custom-call | flops 1000 | bytes 1000 | tf_op jit(solution)/shard_map/serve/pallas_call | solution.py:318
  314.3 0.1 pad_add_fusion.2.where_ref
  314.4 8.9 %serve.8.rest_0_ = bf16[8192,896]{1,0:T(8,128)(2,1)} custom-call(s32[2]{0:T(128)S(1)} %pad_add_fusion.1.where_ref, bf16[2048,896]{1,0:T(8,128)(2,1)} %collective-permute-done.refs_1_.codes_ref, f32[64,8,896]{2,1,0:T(8,128)S(1)} %bitcast.13, bf16[8192,896]{1,0:T(8,128)(2,1)} %serve.7.rest_0_), custom_call_target="tpu_custom_call", output_to_operand_aliasing={{}: (3, {})} | custom-call | flops 1000 | bytes 1000 | tf_op jit(solution)/shard_map/serve/pallas_call | solution.py:318
  323.3 0.0 collective-permute-done.7.codes_ref
  323.3 5.3 %serve.9.rest_0_ = bf16[8192,896]{1,0:T(8,128)(2,1)} custom-call(s32[2]{0:T(128)S(1)} %pad_add_fusion.2.where_ref, bf16[1024,896]{1,0:T(8,128)(2,1)} %collective-permute-done.7.codes_ref, f32[64,8,896]{2,1,0:T(8,128)S(1)} %bitcast.14, bf16[8192,896]{1,0:T(8,128)(2,1)} %serve.8.rest_0_), custom_call_target="tpu_custom_call", output_to_operand_aliasing={{}: (3, {})} | custom-call | flops 1000 | bytes 1000 | tf_op jit(solution)/shard_map/serve/pallas_call | solution.py:318
  328.6 4.0 %collective-permute-done.6.codes_ref = bf16[768,896]{1,0:T(8,128)(2,1)} collective-permute-done((bf16[768,896]{1,0:T(8,128)(2,1)S(1)}, bf16[768,896]{1,0:T(8,128)(2,1)}, u32[]{:S(2)}, u32[]{:S(2)}) %collective-permute-start.6) | collective-permute-done | bytes 1376288 | tf_op jit(solution)/shard_map/ppermute | solution.py:348
  332.6 4.7 %serve.10.rest_0_ = bf16[8192,896]{1,0:T(8,128)(2,1)} custom-call(s32[2]{0:T(128)S(1)} %pad_add_fusion.2.where_ref, bf16[768,896]{1,0:T(8,128)(2,1)} %collective-permute-done.6.codes_ref, f32[64,8,896]{2,1,0:T(8,128)S(1)} %bitcast.15, bf16[8192,896]{1,0:T(8,128)(2,1)} %serve.9.rest_0_), custom_call_target="tpu_custom_call", output_to_operand_aliasing={{}: (3, {})} | custom-call | flops 1000 | bytes 1000 | tf_op jit(solution)/shard_map/serve/pallas_call | solution.py:318
  337.3 0.7 reshape.27
  338.0 3.6 %collective-permute-done.1.codes_ref = bf16[256,896]{1,0:T(8,128)(2,1)} collective-permute-done((bf16[256,896]{1,0:T(8,128)(2,1)}, bf16[256,896]{1,0:T(8,128)(2,1)}, u32[]{:S(2)}, u32[]{:S(2)}) %collective-permute-start.1) | collective-permute-done | bytes 458784 | tf_op jit(solution)/shard_map/ppermute | solution.py:348
  341.6 2.8 serve.11
  (13 shorter events, 0.1 us)
Async XLA Ops:
  7.2 78.4 %all-reduce.5.cloned.1.call-start = ((), (), s32[]{:S(2)}) async-start(), calls=%async_computation | async-start | bytes 2097152 | tf_op jit(solution)/shard_map/psum | solution.py:371
  12.7 16.9 %copy-start.2 = (s32[16,28]{1,0:T(8,128)S(1)}, s32[16,28]{1,0:T(8,128)}, u32[]{:S(2)}) copy-start(s32[16,28]{1,0:T(8,128)} %spans_ref.1) | copy-start | bytes 5380
  12.7 16.9 %copy-start.3 = (f32[16,28]{1,0:T(8,128)S(1)}, f32[16,28]{1,0:T(8,128)}, u32[]{:S(2)}) copy-start(f32[16,28]{1,0:T(8,128)} %param.10) | copy-start | bytes 5380
  12.7 242.2 %collective-permute-start.5 = (bf16[2048,896]{1,0:T(8,128)(2,1)}, bf16[2048,896]{1,0:T(8,128)(2,1)}, u32[]{:S(2)}, u32[]{:S(2)}) collective-permute-start(bf16[2048,896]{1,0:T(8,128)(2,1)} %cast_codes.5.rest_0_), channel_id=1, source_target_pairs={{0,2},{1,3},{2,0},{3,1},{4,6},{5,7},{6,4},{7,5},{8,10},{9,11},{10,... | collective-permute-start | bytes 11010056 | tf_op jit(solution)/shard_map/ppermute | solution.py:348
  29.5 255.5 %all-gather.3.cloned.1.call-start = ((), (), s32[]{:S(2)}) async-start(), calls=%async_computation.1 | async-start | bytes 2359296 | tf_op jit(solution)/shard_map/all_gather | solution.py:387
  85.5 1.2 copy-start.1
  156.3 109.0 %collective-permute-start = (bf16[2048,896]{1,0:T(8,128)(2,1)}, bf16[2048,896]{1,0:T(8,128)(2,1)}, u32[]{:S(2)}, u32[]{:S(2)}) collective-permute-start(bf16[2048,896]{1,0:T(8,128)(2,1)} %cast_codes.7.refs_1_), channel_id=1, source_target_pairs={{0,1},{1,2},{2,3},{3,0},{4,5},{5,6},{6,7},{7,4},{8,9},{9,10},{10,1... | collective-permute-start | bytes 11010056 | tf_op jit(solution)/shard_map/ppermute | solution.py:348
  157.7 81.6 %collective-permute-start.2 = (f32[4,8,128]{2,1,0:T(8,128)S(1)}, f32[4,8,128]{2,1,0:T(8,128)S(1)}, u32[]{:S(2)}, u32[]{:S(2)}) collective-permute-start(f32[4,8,128]{2,1,0:T(8,128)S(1)} %once_there.6), channel_id=1, source_target_pairs={{0,1},{1,2},{2,3},{3,0},{4,5},{5,6},{6,7},{7,4},{8,9},{9,10},{10,1... | collective-permute-start | bytes 49160 | tf_op jit(solution)/shard_map/ppermute | solution.py:348
  159.1 95.7 %collective-permute-start.3 = (f32[4,8,128]{2,1,0:T(8,128)S(1)}, f32[4,8,128]{2,1,0:T(8,128)S(1)}, u32[]{:S(2)}, u32[]{:S(2)}) collective-permute-start(f32[4,8,128]{2,1,0:T(8,128)S(1)} %once_there.6), channel_id=1, source_target_pairs={{0,2},{1,3},{2,0},{3,1},{4,6},{5,7},{6,4},{7,5},{8,10},{9,11},{10,... | collective-permute-start | bytes 49160 | tf_op jit(solution)/shard_map/ppermute | solution.py:348
  160.7 94.2 %collective-permute-start.4 = (f32[4,8,128]{2,1,0:T(8,128)S(1)}, f32[4,8,128]{2,1,0:T(8,128)S(1)}, u32[]{:S(2)}, u32[]{:S(2)}) collective-permute-start(f32[4,8,128]{2,1,0:T(8,128)S(1)} %once_there.6), channel_id=1, source_target_pairs={{0,3},{1,0},{2,1},{3,2},{4,7},{5,4},{6,5},{7,6},{8,11},{9,8},{10,9... | collective-permute-start | bytes 49160 | tf_op jit(solution)/shard_map/ppermute | solution.py:348
  258.8 64.5 %collective-permute-start.7 = (bf16[1024,896]{1,0:T(8,128)(2,1)}, bf16[1024,896]{1,0:T(8,128)(2,1)}, u32[]{:S(2)}, u32[]{:S(2)}) collective-permute-start(bf16[1024,896]{1,0:T(8,128)(2,1)} %once_there.9), channel_id=1, source_target_pairs={{0,3},{1,0},{2,1},{3,2},{4,7},{5,4},{6,5},{7,6},{8,11},{9,8},{10,9... | collective-permute-start | bytes 5505032 | tf_op jit(solution)/shard_map/ppermute | solution.py:348
  265.3 67.3 %collective-permute-start.6 = (bf16[768,896]{1,0:T(8,128)(2,1)S(1)}, bf16[768,896]{1,0:T(8,128)(2,1)}, u32[]{:S(2)}, u32[]{:S(2)}) collective-permute-start(bf16[768,896]{1,0:T(8,128)(2,1)S(1)} %once_there.8), channel_id=1, source_target_pairs={{0,3},{1,0},{2,1},{3,2},{4,7},{5,4},{6,5},{7,6},{8,11},{9,8},{10,9... | collective-permute-start | bytes 4128776 | tf_op jit(solution)/shard_map/ppermute | solution.py:348
  267.7 0.7 copy-start.4
  267.7 73.9 %collective-permute-start.1 = (bf16[256,896]{1,0:T(8,128)(2,1)}, bf16[256,896]{1,0:T(8,128)(2,1)}, u32[]{:S(2)}, u32[]{:S(2)}) collective-permute-start(bf16[256,896]{1,0:T(8,128)(2,1)} %once_there.5), channel_id=1, source_target_pairs={{0,3},{1,0},{2,1},{3,2},{4,7},{5,4},{6,5},{7,6},{8,11},{9,8},{10,9... | collective-permute-start | bytes 1376264 | tf_op jit(solution)/shard_map/ppermute | solution.py:348
  285.1 1.6 copy-start
Sparse Core Ops, SparseCore 0:
  29.7 55.8 all-reduce.4
  255.8 29.2 all-gather.2

commit v6 on v5

--- a/solution.py
+++ b/solution.py
@@ -377,11 +377,8 @@
     line_rows = line.shape[0]
     late = []
     for place, (part, sent) in enumerate(zip(second_parts, ready)):
-        if place == 1:
-            sent = once_there(sent, arrived)
-        elif place > 1:
-            sent = once_there(sent, [late[0]])
-        late.append(shifted(sent, part[0]))
+        after = [tables[1:], arrived, late[:1]][min(place, 2)]
+        late.append(shifted(once_there(sent, after), part[0]))
 
     line = jnp.pad(line, ((0, max(0, 64 - line_rows)), (0, 0), (0, 0)))
     gathered = lax.all_gather(line, "dp")

time: 353 us -> 385 us (1.091)
  starting transfers between devices: 14.9 us -> 73.4 us
  waiting for transfers between devices: 171 us -> 144 us
    ppermute x8, starting transfers between devices: 14.8 us -> 73.3 us  [shifted(): lax.ppermute(value, 'mp', [(z, (z + shift) % mp_count) for z in range(mp_...]
    all_gather x1, waiting for transfers between devices: 15.1 us -> 0.01 us  [local(): gathered = lax.all_gather(line, 'dp')]
    ppermute x8, waiting for transfers between devices: 99.5 us -> 88.6 us  [shifted(): lax.ppermute(value, 'mp', [(z, (z + shift) % mp_count) for z in range(mp_...]
  transfers between devices with their start and end apart: 10 -> 10, of which waited for: 6 -> 4; matrix products, arithmetic and copies ran while one was open for 1% -> 1% of each run, Pallas kernels for 39% -> 36%
where the time goes in v6:
time: 385 us; the launch traced here: 383 us
  Pallas kernels  145 us (38%)
  waiting for transfers between devices  144 us (37%)
  starting transfers between devices  73.4 us (19%)
  between operations  14.7 us (4%)
  local copies, waits for them, and re-layouts  4.63 us (1%)
    ppermute x8, waiting for transfers between devices, shifted(): lax.ppermute(value, 'mp', [(z, (z + shift) % mp_count) for z in range(mp_...  88.6 us
    ppermute x8, starting transfers between devices, shifted(): lax.ppermute(value, 'mp', [(z, (z + shift) % mp_count) for z in range(mp_...  73.3 us
    pallas_call x1, Pallas kernels, error_table(): pl.pallas_call(functools.partial(table_kernel, float(token_total), chunk,...  64.1 us
    psum x1, waiting for transfers between devices, local(): hessian = lax.psum(gram, 'dp')  55.9 us
    pallas_call x6, Pallas kernels, serve(): pl.pallas_call(functools.partial(serve_kernel, groups), out_shape=jax.Sha...  40.5 us
    pallas_call x5, Pallas kernels, codes_for(): pl.pallas_call(functools.partial(cast_kernel, reads), out_shape=jax.Shape...  18.9 us
    pallas_call x1, Pallas kernels, gram_blocks(): pl.pallas_call(gram_kernel, out_shape=jax.ShapeDtypeStruct((group_count,...  12.7 us
    pallas_call x1, Pallas kernels, find_slope(): pl.pallas_call(functools.partial(slope_kernel, tile_count, pack), out_sha...  8.77 us
  transfers between devices with their start and end apart: 10, of which 4 were waited for; matrix products, arithmetic and copies ran while one was open for 1% of the time, Pallas kernels for 36%

profile of v6, /device:TPU:0, one launch (start us, length us, event | category | flops | bytes accessed | tf_op | source)
XLA Modules:
  0.0 383.3 jit_solution(15285855584554792255)
XLA Ops:
  7.2 0.0 all-reduce.5.cloned.1.call-start
  7.2 5.4 %cast_codes.5.rest_0_ = bf16[2048,896]{1,0:T(8,128)(2,1)} custom-call(s32[1]{0:T(128)} %bitcast.2.where_ref, s32[2048,3584]{1,0:T(8,128)} %codes_ref.3, s32[2048,3584]{1,0:T(8,128)} %codes_ref.3, s32[2048,3584]{1,0:T(8,128)} %codes_ref.3, s32[2048,3584]{1,0:T(8,128)} %codes_ref.3), custom_call_target="tpu_custom_call" | custom-call | flops 1000 | bytes 1000 | tf_op jit(solution)/shard_map/cast_codes/pallas_call | solution.py:79
  12.7 0.0 copy-start.2
  12.7 0.0 copy-start.3
  12.7 4.1 %collective-permute-start.5 = (bf16[2048,896]{1,0:T(8,128)(2,1)}, bf16[2048,896]{1,0:T(8,128)(2,1)}, u32[]{:S(2)}, u32[]{:S(2)}) collective-permute-start(bf16[2048,896]{1,0:T(8,128)(2,1)} %cast_codes.5.rest_0_), channel_id=1, source_target_pairs={{0,2},{1,3},{2,0},{3,1},{4,6},{5,7},{6,4},{7,5},{8,10},{9,11},{10,... | collective-permute-start | bytes 11010056 | tf_op jit(solution)/shard_map/ppermute | solution.py:348
  16.8 12.7 %gram.1 = f32[16,128,128]{2,1,0:T(8,128)} custom-call(bf16[2048,2048]{1,0:T(8,128)(2,1)} %tokens_ref.1, bf16[2048,896]{1,0:T(8,128)(2,1)} %cast_codes.5.rest_0_), custom_call_target="tpu_custom_call" | custom-call | flops 1000 | bytes 1000 | tf_op jit(solution)/shard_map/gram/pallas_call | solution.py:103
  29.5 0.0 all-reduce.5.cloned.1.call-update
  29.5 0.0 all-gather.3.cloned.1.call-start
  29.6 0.0 copy-done.2
  29.6 0.0 copy-done.3
  29.7 55.9 %all-reduce.5.cloned.1.call-done.hessian_ref = f32[16,128,128]{2,1,0:T(8,128)} async-done(((f32[16,128,128]{2,1,0:T(8,128)}), f32[16,128,128]{2,1,0:T(8,128)}) %all-reduce.5.cloned.1.call-update) | async-done | bytes 1048592 | tf_op jit(solution)/shard_map/psum | solution.py:371
  85.6 0.0 copy-start.1
  85.6 1.2 copy-done.1
  86.8 64.1 %error_table.1.refs_4_ = f32[4,8,128]{2,1,0:T(8,128)S(1)} custom-call(s32[16,28]{1,0:T(8,128)S(1)} %copy-done.2, f32[16,128,128]{2,1,0:T(8,128)S(1)} %copy-done.1, s32[2048,3584]{1,0:T(8,128)} %codes_ref.3, bf16[2048,3584]{1,0:T(8,128)(2,1)} %residue_ref.1, f32[16,8,128]{2,1,0:T(8,128)S(1)} %pad.12.factor_ref, f32[16,8,128]{2,1,0:T(8,128)S(1)} %select_maximum_fusion.added_ref), custom_call_target="tpu_custom_call" | custom-call | flops 1000 | bytes 1000 | tf_op jit(solution)/shard_map/error_table/pallas_call | solution.py:184
  150.9 5.4 %cast_codes.7.refs_1_.refs_0_ = bf16[2048,896]{1,0:T(8,128)(2,1)} custom-call(s32[1]{0:T(128)} %bitcast.where_ref, s32[2048,3584]{1,0:T(8,128)} %codes_ref.3, s32[2048,3584]{1,0:T(8,128)} %codes_ref.3, s32[2048,3584]{1,0:T(8,128)} %codes_ref.3, s32[2048,3584]{1,0:T(8,128)} %codes_ref.3, f32[4,8,128]{2,1,0:T(8,128)S(1)} %error_table.1.refs_4_), custom_call_target="tpu_custom_call" | custom-call | flops 1000 | bytes 1000 | tf_op jit(solution)/shard_map/cast_codes/pallas_call | solution.py:79
  156.4 1.3 collective-permute-start
  157.7 2.4 collective-permute-start.1
  160.1 1.4 collective-permute-start.2
  161.5 0.6 collective-permute-done.refs_1_
  162.1 14.1 %collective-permute-done.1.refs_2_ = f32[4,8,128]{2,1,0:T(8,128)S(1)} collective-permute-done((f32[4,8,128]{2,1,0:T(8,128)S(1)}, f32[4,8,128]{2,1,0:T(8,128)S(1)}, u32[]{:S(2)}, u32[]{:S(2)}) %collective-permute-start.1) | collective-permute-done | bytes 16416 | tf_op jit(solution)/shard_map/ppermute | solution.py:348
  176.2 0.0 collective-permute-done.2.refs_3_
  176.2 0.9 collective-permute-start.3
  177.1 0.0 collective-permute-done.5.refs_1_.codes_ref
  177.2 0.7 pad.14
  177.9 0.0 all-gather.3.cloned.1.call-update
  177.9 3.1 cast_codes.9.refs_0_
  181.1 3.0 collective-permute-start.7
  184.0 2.7 cast_codes.8.refs_0_
  186.7 73.8 %collective-permute-done.3.refs_1_.codes_ref = bf16[2048,896]{1,0:T(8,128)(2,1)} collective-permute-done((bf16[2048,896]{1,0:T(8,128)(2,1)}, bf16[2048,896]{1,0:T(8,128)(2,1)}, u32[]{:S(2)}, u32[]{:S(2)}) %collective-permute-start.3) | collective-permute-done | bytes 3670048 | tf_op jit(solution)/shard_map/ppermute | solution.py:348
  260.6 59.9 %collective-permute-start.6 = (bf16[768,896]{1,0:T(8,128)(2,1)S(1)}, bf16[768,896]{1,0:T(8,128)(2,1)}, u32[]{:S(2)}, u32[]{:S(2)}) collective-permute-start(bf16[768,896]{1,0:T(8,128)(2,1)S(1)} %once_there.10), channel_id=1, source_target_pairs={{0,3},{1,0},{2,1},{3,2},{4,7},{5,4},{6,5},{7,6},{8,11},{9,8},{10,9... | collective-permute-start | bytes 4128776 | tf_op jit(solution)/shard_map/ppermute | solution.py:348
  320.5 2.1 cast_codes.6.refs_0_
  322.6 0.0 copy-start.4
  322.7 0.3 collective-permute-start.4
  322.9 0.4 copy-done.4
  323.3 0.6 reduce_sum.9
  324.5 0.1 pad_add_fusion.4.where_ref
  324.6 0.1 pad_add_fusion.3.me_ref
  324.7 0.1 pad_add_fusion.where_ref
  324.8 0.0 all-gather.3.cloned.1.call-done
  324.8 0.0 copy-start
  324.8 1.6 copy-done
  326.3 8.8 %find_slope.1 = (f32[16,4,8,896]{3,2,1,0:T(8,128)S(1)}, f32[16,128]{1,0:T(8,128)S(1)}) custom-call(f32[1]{0:T(128)} %bitcast.5.goal_ref, s32[2]{0:T(128)S(1)} %pad_add_fusion.3.me_ref, f32[8,64,8,128]{3,2,1,0:T(8,128)S(1)} %bitcast.17), custom_call_target="tpu_custom_call" | custom-call | flops 1000 | bytes 1000 | tf_op jit(solution)/shard_map/find_slope/pallas_call | solution.py:270
  335.1 9.9 %serve.6.rest_0_ = bf16[8192,896]{1,0:T(8,128)(2,1)} custom-call(s32[2]{0:T(128)S(1)} %pad_add_fusion.4.where_ref, s32[2048,3584]{1,0:T(8,128)} %codes_ref.3, f32[64,8,896]{2,1,0:T(8,128)S(1)} %bitcast.11), custom_call_target="tpu_custom_call" | custom-call | flops 1000 | bytes 1000 | tf_op jit(solution)/shard_map/serve/pallas_call | solution.py:318
  345.0 0.1 pad_add_fusion.1
  345.1 8.9 %serve.7.rest_0_ = bf16[8192,896]{1,0:T(8,128)(2,1)} custom-call(s32[2]{0:T(128)S(1)} %pad_add_fusion.where_ref, bf16[2048,896]{1,0:T(8,128)(2,1)} %collective-permute-done.5.refs_1_.codes_ref, f32[64,8,896]{2,1,0:T(8,128)S(1)} %bitcast.12, bf16[8192,896]{1,0:T(8,128)(2,1)} %serve.6.rest_0_), custom_call_target="tpu_custom_call", output_to_operand_aliasing={{}: (3, {})} | custom-call | flops 1000 | bytes 1000 | tf_op jit(solution)/shard_map/serve/pallas_call | solution.py:318
  354.0 8.9 %serve.8.rest_0_ = bf16[8192,896]{1,0:T(8,128)(2,1)} custom-call(s32[2]{0:T(128)S(1)} %get-tuple-element.6.where_ref, bf16[2048,896]{1,0:T(8,128)(2,1)} %collective-permute-done.3.refs_1_.codes_ref, f32[64,8,896]{2,1,0:T(8,128)S(1)} %bitcast.13, bf16[8192,896]{1,0:T(8,128)(2,1)} %serve.7.rest_0_), custom_call_target="tpu_custom_call", output_to_operand_aliasing={{}: (3, {})} | custom-call | flops 1000 | bytes 1000 | tf_op jit(solution)/shard_map/serve/pallas_call | solution.py:318
  362.9 0.0 collective-permute-done.7.codes_ref
  362.9 5.3 %serve.9.rest_0_ = bf16[8192,896]{1,0:T(8,128)(2,1)} custom-call(s32[2]{0:T(128)S(1)} %get-tuple-element.7.where_ref, bf16[1024,896]{1,0:T(8,128)(2,1)} %collective-permute-done.7.codes_ref, f32[64,8,896]{2,1,0:T(8,128)S(1)} %bitcast.14, bf16[8192,896]{1,0:T(8,128)(2,1)} %serve.8.rest_0_), custom_call_target="tpu_custom_call", output_to_operand_aliasing={{}: (3, {})} | custom-call | flops 1000 | bytes 1000 | tf_op jit(solution)/shard_map/serve/pallas_call | solution.py:318
  368.2 0.0 collective-permute-done.6.codes_ref
  368.2 4.7 %serve.10.rest_0_ = bf16[8192,896]{1,0:T(8,128)(2,1)} custom-call(s32[2]{0:T(128)S(1)} %get-tuple-element.7.where_ref, bf16[768,896]{1,0:T(8,128)(2,1)} %collective-permute-done.6.codes_ref, f32[64,8,896]{2,1,0:T(8,128)S(1)} %bitcast.15, bf16[8192,896]{1,0:T(8,128)(2,1)} %serve.9.rest_0_), custom_call_target="tpu_custom_call", output_to_operand_aliasing={{}: (3, {})} | custom-call | flops 1000 | bytes 1000 | tf_op jit(solution)/shard_map/serve/pallas_call | solution.py:318
  372.9 0.7 reshape.27
  373.6 0.0 collective-permute-done.4.codes_ref
  373.6 2.8 serve.11
  (14 shorter events, 0.1 us)
Async XLA Ops:
  7.2 78.4 %all-reduce.5.cloned.1.call-start = ((), (), s32[]{:S(2)}) async-start(), calls=%async_computation | async-start | bytes 2097152 | tf_op jit(solution)/shard_map/psum | solution.py:371
  12.7 16.9 %copy-start.2 = (s32[16,28]{1,0:T(8,128)S(1)}, s32[16,28]{1,0:T(8,128)}, u32[]{:S(2)}) copy-start(s32[16,28]{1,0:T(8,128)} %spans_ref.1) | copy-start | bytes 5380
  12.7 16.9 %copy-start.3 = (f32[16,28]{1,0:T(8,128)S(1)}, f32[16,28]{1,0:T(8,128)}, u32[]{:S(2)}) copy-start(f32[16,28]{1,0:T(8,128)} %param.10) | copy-start | bytes 5380
  12.7 164.5 %collective-permute-start.5 = (bf16[2048,896]{1,0:T(8,128)(2,1)}, bf16[2048,896]{1,0:T(8,128)(2,1)}, u32[]{:S(2)}, u32[]{:S(2)}) collective-permute-start(bf16[2048,896]{1,0:T(8,128)(2,1)} %cast_codes.5.rest_0_), channel_id=1, source_target_pairs={{0,2},{1,3},{2,0},{3,1},{4,6},{5,7},{6,4},{7,5},{8,10},{9,11},{10,... | collective-permute-start | bytes 11010056 | tf_op jit(solution)/shard_map/ppermute | solution.py:348
  29.5 295.2 %all-gather.3.cloned.1.call-start = ((), (), s32[]{:S(2)}) async-start(), calls=%async_computation.1 | async-start | bytes 2359296 | tf_op jit(solution)/shard_map/all_gather | solution.py:384
  85.6 1.2 copy-start.1
  156.4 5.7 %collective-permute-start = (f32[4,8,128]{2,1,0:T(8,128)S(1)}, f32[4,8,128]{2,1,0:T(8,128)S(1)}, u32[]{:S(2)}, u32[]{:S(2)}) collective-permute-start(f32[4,8,128]{2,1,0:T(8,128)S(1)} %once_there.6), channel_id=1, source_target_pairs={{0,1},{1,2},{2,3},{3,0},{4,5},{5,6},{6,7},{7,4},{8,9},{9,10},{10,1... | collective-permute-start | bytes 49160 | tf_op jit(solution)/shard_map/ppermute | solution.py:348
  157.7 18.6 %collective-permute-start.1 = (f32[4,8,128]{2,1,0:T(8,128)S(1)}, f32[4,8,128]{2,1,0:T(8,128)S(1)}, u32[]{:S(2)}, u32[]{:S(2)}) collective-permute-start(f32[4,8,128]{2,1,0:T(8,128)S(1)} %once_there.6), channel_id=1, source_target_pairs={{0,2},{1,3},{2,0},{3,1},{4,6},{5,7},{6,4},{7,5},{8,10},{9,11},{10,... | collective-permute-start | bytes 49160 | tf_op jit(solution)/shard_map/ppermute | solution.py:348
  160.1 16.1 %collective-permute-start.2 = (f32[4,8,128]{2,1,0:T(8,128)S(1)}, f32[4,8,128]{2,1,0:T(8,128)S(1)}, u32[]{:S(2)}, u32[]{:S(2)}) collective-permute-start(f32[4,8,128]{2,1,0:T(8,128)S(1)} %once_there.6), channel_id=1, source_target_pairs={{0,3},{1,0},{2,1},{3,2},{4,7},{5,4},{6,5},{7,6},{8,11},{9,8},{10,9... | collective-permute-start | bytes 49160 | tf_op jit(solution)/shard_map/ppermute | solution.py:348
  176.2 84.3 %collective-permute-start.3 = (bf16[2048,896]{1,0:T(8,128)(2,1)}, bf16[2048,896]{1,0:T(8,128)(2,1)}, u32[]{:S(2)}, u32[]{:S(2)}) collective-permute-start(bf16[2048,896]{1,0:T(8,128)(2,1)} %once_there.7), channel_id=1, source_target_pairs={{0,1},{1,2},{2,3},{3,0},{4,5},{5,6},{6,7},{7,4},{8,9},{9,10},{10,1... | collective-permute-start | bytes 11010056 | tf_op jit(solution)/shard_map/ppermute | solution.py:348
  181.1 181.9 %collective-permute-start.7 = (bf16[1024,896]{1,0:T(8,128)(2,1)}, bf16[1024,896]{1,0:T(8,128)(2,1)}, u32[]{:S(2)}, u32[]{:S(2)}) collective-permute-start(bf16[1024,896]{1,0:T(8,128)(2,1)} %once_there.11), channel_id=1, source_target_pairs={{0,3},{1,0},{2,1},{3,2},{4,7},{5,4},{6,5},{7,6},{8,11},{9,8},{10,9... | collective-permute-start | bytes 5505032 | tf_op jit(solution)/shard_map/ppermute | solution.py:348
  260.6 107.7 %collective-permute-start.6 = (bf16[768,896]{1,0:T(8,128)(2,1)S(1)}, bf16[768,896]{1,0:T(8,128)(2,1)}, u32[]{:S(2)}, u32[]{:S(2)}) collective-permute-start(bf16[768,896]{1,0:T(8,128)(2,1)S(1)} %once_there.10), channel_id=1, source_target_pairs={{0,3},{1,0},{2,1},{3,2},{4,7},{5,4},{6,5},{7,6},{8,11},{9,8},{10,9... | collective-permute-start | bytes 4128776 | tf_op jit(solution)/shard_map/ppermute | solution.py:348
  322.6 0.7 copy-start.4
  322.7 51.0 %collective-permute-start.4 = (bf16[256,896]{1,0:T(8,128)(2,1)}, bf16[256,896]{1,0:T(8,128)(2,1)}, u32[]{:S(2)}, u32[]{:S(2)}) collective-permute-start(bf16[256,896]{1,0:T(8,128)(2,1)} %once_there.8), channel_id=1, source_target_pairs={{0,3},{1,0},{2,1},{3,2},{4,7},{5,4},{6,5},{7,6},{8,11},{9,8},{10,9... | collective-permute-start | bytes 1376264 | tf_op jit(solution)/shard_map/ppermute | solution.py:348
  324.8 1.6 copy-start
Sparse Core Ops, SparseCore 0:
  29.6 55.8 all-reduce.4
  178.0 28.9 all-gather.2

commit v7 on v5

--- a/solution.py
+++ b/solution.py
@@ -371,16 +371,16 @@
     hessian = lax.psum(gram, "dp")
     table = error_table(hessian, grid_codes, residue, tile_spans, tile_scales, token_total)
     ready = [cast(*part, [table]) for part in second_parts]
-    crossing = once_there(table, ready[:1])
+    crossing = once_there(table, ready)
     tables = [table] + [shifted(crossing, shift) for shift in range(1, mp_count)]
     line = once_there(jnp.concatenate(tables), arrived)
     line_rows = line.shape[0]
     late = []
     for place, (part, sent) in enumerate(zip(second_parts, ready)):
         if place == 1:
-            sent = once_there(sent, arrived)
+            sent = once_there(sent, arrived + tables[1:])
         elif place > 1:
-            sent = once_there(sent, [late[0]])
+            sent = once_there(sent, late[:1])
         late.append(shifted(sent, part[0]))
 
     line = jnp.pad(line, ((0, max(0, 64 - line_rows)), (0, 0), (0, 0)))

time: 353 us -> 349 us (0.989)
    ppermute x8, waiting for transfers between devices: 99.5 us -> 89.5 us  [shifted(): lax.ppermute(value, 'mp', [(z, (z + shift) % mp_count) for z in range(mp_...]
    all_gather x1, waiting for transfers between devices: 15.1 us -> 23.2 us  [local(): gathered = lax.all_gather(line, 'dp')]
where the time goes in v7:
time: 349 us; the launch traced here: 348 us
  waiting for transfers between devices  169 us (48%)
  Pallas kernels  145 us (42%)
  between operations  14.8 us (4%)
  starting transfers between devices  14.2 us (4%)
  local copies, waits for them, and re-layouts  4.25 us (1%)
    ppermute x8, waiting for transfers between devices, shifted(): lax.ppermute(value, 'mp', [(z, (z + shift) % mp_count) for z in range(mp_...  89.5 us
    pallas_call x1, Pallas kernels, error_table(): pl.pallas_call(functools.partial(table_kernel, float(token_total), chunk,...  64.1 us
    psum x1, waiting for transfers between devices, local(): hessian = lax.psum(gram, 'dp')  55.9 us
    pallas_call x6, Pallas kernels, serve(): pl.pallas_call(functools.partial(serve_kernel, groups), out_shape=jax.Sha...  40.5 us
    all_gather x1, waiting for transfers between devices, local(): gathered = lax.all_gather(line, 'dp')  23.2 us
    pallas_call x5, Pallas kernels, codes_for(): pl.pallas_call(functools.partial(cast_kernel, reads), out_shape=jax.Shape...  18.8 us
    ppermute x8, starting transfers between devices, shifted(): lax.ppermute(value, 'mp', [(z, (z + shift) % mp_count) for z in range(mp_...  14.1 us
    pallas_call x1, Pallas kernels, gram_blocks(): pl.pallas_call(gram_kernel, out_shape=jax.ShapeDtypeStruct((group_count,...  12.7 us
  transfers between devices with their start and end apart: 10, of which 6 were waited for; matrix products, arithmetic and copies ran while one was open for 1% of the time, Pallas kernels for 39%

profile of v7, /device:TPU:0, one launch (start us, length us, event | category | flops | bytes accessed | tf_op | source)
XLA Modules:
  0.0 347.8 jit_solution(15199834034288074376)
XLA Ops:
  7.2 0.0 all-reduce.5.cloned.1.call-start
  7.2 5.4 %cast_codes.5.rest_0_ = bf16[2048,896]{1,0:T(8,128)(2,1)} custom-call(s32[1]{0:T(128)} %bitcast.2.where_ref, s32[2048,3584]{1,0:T(8,128)} %codes_ref.3, s32[2048,3584]{1,0:T(8,128)} %codes_ref.3, s32[2048,3584]{1,0:T(8,128)} %codes_ref.3, s32[2048,3584]{1,0:T(8,128)} %codes_ref.3), custom_call_target="tpu_custom_call" | custom-call | flops 1000 | bytes 1000 | tf_op jit(solution)/shard_map/cast_codes/pallas_call | solution.py:79
  12.7 0.0 copy-start.2
  12.7 0.0 copy-start.3
  12.7 4.1 %collective-permute-start.5 = (bf16[2048,896]{1,0:T(8,128)(2,1)}, bf16[2048,896]{1,0:T(8,128)(2,1)}, u32[]{:S(2)}, u32[]{:S(2)}) collective-permute-start(bf16[2048,896]{1,0:T(8,128)(2,1)} %cast_codes.5.rest_0_), channel_id=1, source_target_pairs={{0,2},{1,3},{2,0},{3,1},{4,6},{5,7},{6,4},{7,5},{8,10},{9,11},{10,... | collective-permute-start | bytes 11010056 | tf_op jit(solution)/shard_map/ppermute | solution.py:348
  16.8 12.7 %gram.1 = f32[16,128,128]{2,1,0:T(8,128)} custom-call(bf16[2048,2048]{1,0:T(8,128)(2,1)} %tokens_ref.1, bf16[2048,896]{1,0:T(8,128)(2,1)} %cast_codes.5.rest_0_), custom_call_target="tpu_custom_call" | custom-call | flops 1000 | bytes 1000 | tf_op jit(solution)/shard_map/gram/pallas_call | solution.py:103
  29.5 0.0 all-reduce.5.cloned.1.call-update
  29.5 0.0 all-gather.3.cloned.1.call-start
  29.6 0.0 copy-done.2
  29.6 0.0 copy-done.3
  29.7 55.9 %all-reduce.5.cloned.1.call-done.hessian_ref = f32[16,128,128]{2,1,0:T(8,128)} async-done(((f32[16,128,128]{2,1,0:T(8,128)}), f32[16,128,128]{2,1,0:T(8,128)}) %all-reduce.5.cloned.1.call-update) | async-done | bytes 1048592 | tf_op jit(solution)/shard_map/psum | solution.py:371
  85.6 0.0 copy-start.1
  85.6 1.2 copy-done.1
  86.8 64.1 %error_table.1.refs_4_ = f32[4,8,128]{2,1,0:T(8,128)S(1)} custom-call(s32[16,28]{1,0:T(8,128)S(1)} %copy-done.2, f32[16,128,128]{2,1,0:T(8,128)S(1)} %copy-done.1, s32[2048,3584]{1,0:T(8,128)} %codes_ref.3, bf16[2048,3584]{1,0:T(8,128)(2,1)} %residue_ref.1, f32[16,8,128]{2,1,0:T(8,128)S(1)} %pad.12.factor_ref, f32[16,8,128]{2,1,0:T(8,128)S(1)} %select_maximum_fusion.added_ref), custom_call_target="tpu_custom_call" | custom-call | flops 1000 | bytes 1000 | tf_op jit(solution)/shard_map/error_table/pallas_call | solution.py:184
  150.9 5.4 %cast_codes.7.refs_1_ = bf16[2048,896]{1,0:T(8,128)(2,1)} custom-call(s32[1]{0:T(128)} %bitcast.where_ref, s32[2048,3584]{1,0:T(8,128)} %codes_ref.3, s32[2048,3584]{1,0:T(8,128)} %codes_ref.3, s32[2048,3584]{1,0:T(8,128)} %codes_ref.3, s32[2048,3584]{1,0:T(8,128)} %codes_ref.3, f32[4,8,128]{2,1,0:T(8,128)S(1)} %error_table.1.refs_4_), custom_call_target="tpu_custom_call" | custom-call | flops 1000 | bytes 1000 | tf_op jit(solution)/shard_map/cast_codes/pallas_call | solution.py:79
  156.3 1.3 collective-permute-start
  157.7 2.1 cast_codes.6.refs_0_.refs_4_
  159.8 2.7 cast_codes.9.refs_3_.refs_0_
  162.5 3.1 cast_codes.8.refs_2_.refs_0_
  165.6 2.5 collective-permute-start.4
  168.2 0.4 collective-permute-start.3
  168.6 1.5 collective-permute-start.2
  170.1 69.2 %collective-permute-done.4.refs_4_ = f32[4,8,128]{2,1,0:T(8,128)S(1)} collective-permute-done((f32[4,8,128]{2,1,0:T(8,128)S(1)}, f32[4,8,128]{2,1,0:T(8,128)S(1)}, u32[]{:S(2)}, u32[]{:S(2)}) %collective-permute-start.4) | collective-permute-done | bytes 16416 | tf_op jit(solution)/shard_map/ppermute | solution.py:348
  239.3 15.8 %collective-permute-done.3.refs_3_ = f32[4,8,128]{2,1,0:T(8,128)S(1)} collective-permute-done((f32[4,8,128]{2,1,0:T(8,128)S(1)}, f32[4,8,128]{2,1,0:T(8,128)S(1)}, u32[]{:S(2)}, u32[]{:S(2)}) %collective-permute-start.3) | collective-permute-done | bytes 16416 | tf_op jit(solution)/shard_map/ppermute | solution.py:348
  255.1 0.0 collective-permute-done.2.refs_2_
  255.1 0.0 collective-permute-done.5.refs_1_.codes_ref
  255.1 0.7 pad.14
  255.8 0.0 all-gather.3.cloned.1.call-update
  255.8 3.3 collective-permute-start.7
  259.2 0.0 collective-permute-done.refs_1_.codes_ref
  259.2 0.0 copy-start.4
  259.2 0.8 collective-permute-start.6
  260.0 0.1 collective-permute-start.1
  260.1 0.0 copy-done.4
  260.1 0.7 reduce_sum.9
  261.4 0.1 pad_add_fusion.4.where_ref
  261.5 0.1 pad_add_fusion.3.me_ref
  261.6 0.1 pad_add_fusion.where_ref
  261.6 23.2 %all-gather.3.cloned.1.call-done = f32[512,8,128]{2,1,0:T(8,128)} async-done(((f32[64,8,128]{2,1,0:T(8,128)}), f32[512,8,128]{2,1,0:T(8,128)}) %all-gather.3.cloned.1.call-update) | async-done | bytes 2097168 | tf_op jit(solution)/shard_map/all_gather | solution.py:387
  284.8 0.0 copy-start
  284.8 1.6 copy-done
  286.4 8.8 %find_slope.1 = (f32[16,4,8,896]{3,2,1,0:T(8,128)S(1)}, f32[16,128]{1,0:T(8,128)S(1)}) custom-call(f32[1]{0:T(128)} %bitcast.5.goal_ref, s32[2]{0:T(128)S(1)} %pad_add_fusion.3.me_ref, f32[8,64,8,128]{3,2,1,0:T(8,128)S(1)} %bitcast.17), custom_call_target="tpu_custom_call" | custom-call | flops 1000 | bytes 1000 | tf_op jit(solution)/shard_map/find_slope/pallas_call | solution.py:270
  295.2 9.9 %serve.6.rest_0_ = bf16[8192,896]{1,0:T(8,128)(2,1)} custom-call(s32[2]{0:T(128)S(1)} %pad_add_fusion.4.where_ref, s32[2048,3584]{1,0:T(8,128)} %codes_ref.3, f32[64,8,896]{2,1,0:T(8,128)S(1)} %bitcast.11), custom_call_target="tpu_custom_call" | custom-call | flops 1000 | bytes 1000 | tf_op jit(solution)/shard_map/serve/pallas_call | solution.py:318
  305.0 0.1 pad_add_fusion.1
  305.1 8.9 %serve.7.rest_0_ = bf16[8192,896]{1,0:T(8,128)(2,1)} custom-call(s32[2]{0:T(128)S(1)} %pad_add_fusion.where_ref, bf16[2048,896]{1,0:T(8,128)(2,1)} %collective-permute-done.5.refs_1_.codes_ref, f32[64,8,896]{2,1,0:T(8,128)S(1)} %bitcast.12, bf16[8192,896]{1,0:T(8,128)(2,1)} %serve.6.rest_0_), custom_call_target="tpu_custom_call", output_to_operand_aliasing={{}: (3, {})} | custom-call | flops 1000 | bytes 1000 | tf_op jit(solution)/shard_map/serve/pallas_call | solution.py:318
  314.0 8.9 %serve.8.rest_0_ = bf16[8192,896]{1,0:T(8,128)(2,1)} custom-call(s32[2]{0:T(128)S(1)} %get-tuple-element.6.where_ref, bf16[2048,896]{1,0:T(8,128)(2,1)} %collective-permute-done.refs_1_.codes_ref, f32[64,8,896]{2,1,0:T(8,128)S(1)} %bitcast.13, bf16[8192,896]{1,0:T(8,128)(2,1)} %serve.7.rest_0_), custom_call_target="tpu_custom_call", output_to_operand_aliasing={{}: (3, {})} | custom-call | flops 1000 | bytes 1000 | tf_op jit(solution)/shard_map/serve/pallas_call | solution.py:318
  323.0 0.0 collective-permute-done.7.codes_ref
  323.0 5.3 %serve.9.rest_0_ = bf16[8192,896]{1,0:T(8,128)(2,1)} custom-call(s32[2]{0:T(128)S(1)} %get-tuple-element.7.where_ref, bf16[1024,896]{1,0:T(8,128)(2,1)} %collective-permute-done.7.codes_ref, f32[64,8,896]{2,1,0:T(8,128)S(1)} %bitcast.14, bf16[8192,896]{1,0:T(8,128)(2,1)} %serve.8.rest_0_), custom_call_target="tpu_custom_call", output_to_operand_aliasing={{}: (3, {})} | custom-call | flops 1000 | bytes 1000 | tf_op jit(solution)/shard_map/serve/pallas_call | solution.py:318
  328.3 1.0 collective-permute-done.6.codes_ref
  329.3 4.7 %serve.10.rest_0_ = bf16[8192,896]{1,0:T(8,128)(2,1)} custom-call(s32[2]{0:T(128)S(1)} %get-tuple-element.7.where_ref, bf16[768,896]{1,0:T(8,128)(2,1)} %collective-permute-done.6.codes_ref, f32[64,8,896]{2,1,0:T(8,128)S(1)} %bitcast.15, bf16[8192,896]{1,0:T(8,128)(2,1)} %serve.9.rest_0_), custom_call_target="tpu_custom_call", output_to_operand_aliasing={{}: (3, {})} | custom-call | flops 1000 | bytes 1000 | tf_op jit(solution)/shard_map/serve/pallas_call | solution.py:318
  334.0 0.7 reshape.27
  334.7 3.5 %collective-permute-done.1.codes_ref = bf16[256,896]{1,0:T(8,128)(2,1)} collective-permute-done((bf16[256,896]{1,0:T(8,128)(2,1)}, bf16[256,896]{1,0:T(8,128)(2,1)}, u32[]{:S(2)}, u32[]{:S(2)}) %collective-permute-start.1) | collective-permute-done | bytes 458784 | tf_op jit(solution)/shard_map/ppermute | solution.py:348
  338.2 2.8 serve.11
  (13 shorter events, 0.1 us)
Async XLA Ops:
  7.2 78.4 %all-reduce.5.cloned.1.call-start = ((), (), s32[]{:S(2)}) async-start(), calls=%async_computation | async-start | bytes 2097152 | tf_op jit(solution)/shard_map/psum | solution.py:371
  12.7 16.9 %copy-start.2 = (s32[16,28]{1,0:T(8,128)S(1)}, s32[16,28]{1,0:T(8,128)}, u32[]{:S(2)}) copy-start(s32[16,28]{1,0:T(8,128)} %spans_ref.1) | copy-start | bytes 5380
  12.7 16.9 %copy-start.3 = (f32[16,28]{1,0:T(8,128)S(1)}, f32[16,28]{1,0:T(8,128)}, u32[]{:S(2)}) copy-start(f32[16,28]{1,0:T(8,128)} %param.10) | copy-start | bytes 5380
  12.7 242.4 %collective-permute-start.5 = (bf16[2048,896]{1,0:T(8,128)(2,1)}, bf16[2048,896]{1,0:T(8,128)(2,1)}, u32[]{:S(2)}, u32[]{:S(2)}) collective-permute-start(bf16[2048,896]{1,0:T(8,128)(2,1)} %cast_codes.5.rest_0_), channel_id=1, source_target_pairs={{0,2},{1,3},{2,0},{3,1},{4,6},{5,7},{6,4},{7,5},{8,10},{9,11},{10,... | collective-permute-start | bytes 11010056 | tf_op jit(solution)/shard_map/ppermute | solution.py:348
  29.5 255.3 %all-gather.3.cloned.1.call-start = ((), (), s32[]{:S(2)}) async-start(), calls=%async_computation.1 | async-start | bytes 2359296 | tf_op jit(solution)/shard_map/all_gather | solution.py:387
  85.6 1.2 copy-start.1
  156.3 102.8 %collective-permute-start = (bf16[2048,896]{1,0:T(8,128)(2,1)}, bf16[2048,896]{1,0:T(8,128)(2,1)}, u32[]{:S(2)}, u32[]{:S(2)}) collective-permute-start(bf16[2048,896]{1,0:T(8,128)(2,1)} %cast_codes.7.refs_1_), channel_id=1, source_target_pairs={{0,1},{1,2},{2,3},{3,0},{4,5},{5,6},{6,7},{7,4},{8,9},{9,10},{10,1... | collective-permute-start | bytes 11010056 | tf_op jit(solution)/shard_map/ppermute | solution.py:348
  165.6 73.7 %collective-permute-start.4 = (f32[4,8,128]{2,1,0:T(8,128)S(1)}, f32[4,8,128]{2,1,0:T(8,128)S(1)}, u32[]{:S(2)}, u32[]{:S(2)}) collective-permute-start(f32[4,8,128]{2,1,0:T(8,128)S(1)} %once_there.6), channel_id=1, source_target_pairs={{0,3},{1,0},{2,1},{3,2},{4,7},{5,4},{6,5},{7,6},{8,11},{9,8},{10,9... | collective-permute-start | bytes 49160 | tf_op jit(solution)/shard_map/ppermute | solution.py:348
  168.2 86.9 %collective-permute-start.3 = (f32[4,8,128]{2,1,0:T(8,128)S(1)}, f32[4,8,128]{2,1,0:T(8,128)S(1)}, u32[]{:S(2)}, u32[]{:S(2)}) collective-permute-start(f32[4,8,128]{2,1,0:T(8,128)S(1)} %once_there.6), channel_id=1, source_target_pairs={{0,2},{1,3},{2,0},{3,1},{4,6},{5,7},{6,4},{7,5},{8,10},{9,11},{10,... | collective-permute-start | bytes 49160 | tf_op jit(solution)/shard_map/ppermute | solution.py:348
  168.6 86.5 %collective-permute-start.2 = (f32[4,8,128]{2,1,0:T(8,128)S(1)}, f32[4,8,128]{2,1,0:T(8,128)S(1)}, u32[]{:S(2)}, u32[]{:S(2)}) collective-permute-start(f32[4,8,128]{2,1,0:T(8,128)S(1)} %once_there.6), channel_id=1, source_target_pairs={{0,1},{1,2},{2,3},{3,0},{4,5},{5,6},{6,7},{7,4},{8,9},{9,10},{10,1... | collective-permute-start | bytes 49160 | tf_op jit(solution)/shard_map/ppermute | solution.py:348
  255.8 67.1 %collective-permute-start.7 = (bf16[1024,896]{1,0:T(8,128)(2,1)}, bf16[1024,896]{1,0:T(8,128)(2,1)}, u32[]{:S(2)}, u32[]{:S(2)}) collective-permute-start(bf16[1024,896]{1,0:T(8,128)(2,1)} %once_there.9), channel_id=1, source_target_pairs={{0,3},{1,0},{2,1},{3,2},{4,7},{5,4},{6,5},{7,6},{8,11},{9,8},{10,9... | collective-permute-start | bytes 5505032 | tf_op jit(solution)/shard_map/ppermute | solution.py:348
  259.2 0.9 copy-start.4
  259.2 70.1 %collective-permute-start.6 = (bf16[768,896]{1,0:T(8,128)(2,1)S(1)}, bf16[768,896]{1,0:T(8,128)(2,1)}, u32[]{:S(2)}, u32[]{:S(2)}) collective-permute-start(bf16[768,896]{1,0:T(8,128)(2,1)S(1)} %once_there.8), channel_id=1, source_target_pairs={{0,3},{1,0},{2,1},{3,2},{4,7},{5,4},{6,5},{7,6},{8,11},{9,8},{10,9... | collective-permute-start | bytes 4128776 | tf_op jit(solution)/shard_map/ppermute | solution.py:348
  260.0 78.2 %collective-permute-start.1 = (bf16[256,896]{1,0:T(8,128)(2,1)}, bf16[256,896]{1,0:T(8,128)(2,1)}, u32[]{:S(2)}, u32[]{:S(2)}) collective-permute-start(bf16[256,896]{1,0:T(8,128)(2,1)} %once_there.5), channel_id=1, source_target_pairs={{0,3},{1,0},{2,1},{3,2},{4,7},{5,4},{6,5},{7,6},{8,11},{9,8},{10,9... | collective-permute-start | bytes 1376264 | tf_op jit(solution)/shard_map/ppermute | solution.py:348
  284.8 1.6 copy-start
Sparse Core Ops, SparseCore 0:
  29.6 55.8 all-reduce.4
  256.0 28.8 all-gather.2

commit v8 on v7

--- a/solution.py
+++ b/solution.py
@@ -70,7 +70,7 @@
         part = lax.dynamic_slice(grid_codes, (jnp.int32(first_row), dest * width), (row_count, width))
         return (part.astype(jnp.float32) - MIDDLE).astype(jnp.bfloat16)
     reads = 4
-    block = largest_divisor(math.gcd(row_count // reads, first_row), GROUP, GROUP // reads)
+    block = largest_divisor(math.gcd(row_count // reads, first_row), GROUP // 2, GROUP // reads)
     first_block = first_row // block
 
     def read(place):

time: 349 us -> 351 us (level)
  Pallas kernels: 145 us -> 150 us
    pallas_call x5, Pallas kernels: 18.8 us -> 23.7 us  [codes_for(): pl.pallas_call(functools.partial(cast_kernel, reads), out_shape=jax.Shape...]
  transfers between devices with their start and end apart: 10 -> 10, of which waited for: 6 -> 6; matrix products, arithmetic and copies ran while one was open for 1% -> 1% of each run, Pallas kernels for 39% -> 40%
where the time goes in v8:
time: 351 us; the launch traced here: 350 us
  waiting for transfers between devices  166 us (47%)
  Pallas kernels  150 us (43%)
  between operations  14.8 us (4%)
  starting transfers between devices  14.2 us (4%)
  local copies, waits for them, and re-layouts  4.25 us (1%)
    ppermute x8, waiting for transfers between devices, shifted(): lax.ppermute(value, 'mp', [(z, (z + shift) % mp_count) for z in range(mp_...  86.5 us
    pallas_call x1, Pallas kernels, error_table(): pl.pallas_call(functools.partial(table_kernel, float(token_total), chunk,...  64.1 us
    psum x1, waiting for transfers between devices, local(): hessian = lax.psum(gram, 'dp')  55.9 us
    pallas_call x6, Pallas kernels, serve(): pl.pallas_call(functools.partial(serve_kernel, groups), out_shape=jax.Sha...  40.5 us
    pallas_call x5, Pallas kernels, codes_for(): pl.pallas_call(functools.partial(cast_kernel, reads), out_shape=jax.Shape...  23.7 us
    all_gather x1, waiting for transfers between devices, local(): gathered = lax.all_gather(line, 'dp')  23.2 us
    ppermute x8, starting transfers between devices, shifted(): lax.ppermute(value, 'mp', [(z, (z + shift) % mp_count) for z in range(mp_...  14.1 us
    pallas_call x1, Pallas kernels, gram_blocks(): pl.pallas_call(gram_kernel, out_shape=jax.ShapeDtypeStruct((group_count,...  12.7 us
  transfers between devices with their start and end apart: 10, of which 6 were waited for; matrix products, arithmetic and copies ran while one was open for 1% of the time, Pallas kernels for 40%

profile of v8, /device:TPU:0, one launch (start us, length us, event | category | flops | bytes accessed | tf_op | source)
XLA Modules:
  0.0 349.7 jit_solution(4689170890156301866)
XLA Ops:
  7.2 0.0 all-reduce.5.cloned.1.call-start
  7.2 7.3 %cast_codes.5.rest_0_ = bf16[2048,896]{1,0:T(8,128)(2,1)} custom-call(s32[1]{0:T(128)} %bitcast.2.where_ref, s32[2048,3584]{1,0:T(8,128)} %codes_ref.3, s32[2048,3584]{1,0:T(8,128)} %codes_ref.3, s32[2048,3584]{1,0:T(8,128)} %codes_ref.3, s32[2048,3584]{1,0:T(8,128)} %codes_ref.3), custom_call_target="tpu_custom_call" | custom-call | flops 1000 | bytes 1000 | tf_op jit(solution)/shard_map/cast_codes/pallas_call | solution.py:79
  14.5 0.0 copy-start.2
  14.5 0.0 copy-start.3
  14.5 4.1 %collective-permute-start.5 = (bf16[2048,896]{1,0:T(8,128)(2,1)}, bf16[2048,896]{1,0:T(8,128)(2,1)}, u32[]{:S(2)}, u32[]{:S(2)}) collective-permute-start(bf16[2048,896]{1,0:T(8,128)(2,1)} %cast_codes.5.rest_0_), channel_id=1, source_target_pairs={{0,2},{1,3},{2,0},{3,1},{4,6},{5,7},{6,4},{7,5},{8,10},{9,11},{10,... | collective-permute-start | bytes 11010056 | tf_op jit(solution)/shard_map/ppermute | solution.py:348
  18.6 12.7 %gram.1 = f32[16,128,128]{2,1,0:T(8,128)} custom-call(bf16[2048,2048]{1,0:T(8,128)(2,1)} %tokens_ref.1, bf16[2048,896]{1,0:T(8,128)(2,1)} %cast_codes.5.rest_0_), custom_call_target="tpu_custom_call" | custom-call | flops 1000 | bytes 1000 | tf_op jit(solution)/shard_map/gram/pallas_call | solution.py:103
  31.4 0.0 all-reduce.5.cloned.1.call-update
  31.4 0.0 all-gather.3.cloned.1.call-start
  31.5 0.0 copy-done.2
  31.5 0.0 copy-done.3
  31.6 55.9 %all-reduce.5.cloned.1.call-done.hessian_ref = f32[16,128,128]{2,1,0:T(8,128)} async-done(((f32[16,128,128]{2,1,0:T(8,128)}), f32[16,128,128]{2,1,0:T(8,128)}) %all-reduce.5.cloned.1.call-update) | async-done | bytes 1048592 | tf_op jit(solution)/shard_map/psum | solution.py:371
  87.4 0.0 copy-start.1
  87.4 1.2 copy-done.1
  88.7 64.1 %error_table.1.refs_4_ = f32[4,8,128]{2,1,0:T(8,128)S(1)} custom-call(s32[16,28]{1,0:T(8,128)S(1)} %copy-done.2, f32[16,128,128]{2,1,0:T(8,128)S(1)} %copy-done.1, s32[2048,3584]{1,0:T(8,128)} %codes_ref.3, bf16[2048,3584]{1,0:T(8,128)(2,1)} %residue_ref.1, f32[16,8,128]{2,1,0:T(8,128)S(1)} %pad.12.factor_ref, f32[16,8,128]{2,1,0:T(8,128)S(1)} %select_maximum_fusion.added_ref), custom_call_target="tpu_custom_call" | custom-call | flops 1000 | bytes 1000 | tf_op jit(solution)/shard_map/error_table/pallas_call | solution.py:184
  152.8 7.3 %cast_codes.7.refs_1_ = bf16[2048,896]{1,0:T(8,128)(2,1)} custom-call(s32[1]{0:T(128)} %bitcast.where_ref, s32[2048,3584]{1,0:T(8,128)} %codes_ref.3, s32[2048,3584]{1,0:T(8,128)} %codes_ref.3, s32[2048,3584]{1,0:T(8,128)} %codes_ref.3, s32[2048,3584]{1,0:T(8,128)} %codes_ref.3, f32[4,8,128]{2,1,0:T(8,128)S(1)} %error_table.1.refs_4_), custom_call_target="tpu_custom_call" | custom-call | flops 1000 | bytes 1000 | tf_op jit(solution)/shard_map/cast_codes/pallas_call | solution.py:79
  160.1 1.3 collective-permute-start
  161.4 2.1 cast_codes.6.refs_0_.refs_4_
  163.6 2.7 cast_codes.9.refs_3_.refs_0_
  166.2 4.3 %cast_codes.8.refs_2_.refs_0_ = bf16[1024,896]{1,0:T(8,128)(2,1)} custom-call(s32[1]{0:T(128)} %bitcast.1.where_ref, s32[2048,3584]{1,0:T(8,128)} %codes_ref.3, s32[2048,3584]{1,0:T(8,128)} %codes_ref.3, s32[2048,3584]{1,0:T(8,128)} %codes_ref.3, s32[2048,3584]{1,0:T(8,128)} %codes_ref.3, f32[4,8,128]{2,1,0:T(8,128)S(1)} %error_table.1.refs_4_), custom_call_target="tpu_custom_call" | custom-call | flops 1000 | bytes 1000 | tf_op jit(solution)/shard_map/cast_codes/pallas_call | solution.py:79
  170.5 2.5 collective-permute-start.4
  173.0 0.4 collective-permute-start.3
  173.5 1.5 collective-permute-start.2
  175.0 68.1 %collective-permute-done.4.refs_4_ = f32[4,8,128]{2,1,0:T(8,128)S(1)} collective-permute-done((f32[4,8,128]{2,1,0:T(8,128)S(1)}, f32[4,8,128]{2,1,0:T(8,128)S(1)}, u32[]{:S(2)}, u32[]{:S(2)}) %collective-permute-start.4) | collective-permute-done | bytes 16416 | tf_op jit(solution)/shard_map/ppermute | solution.py:348
  243.1 13.9 %collective-permute-done.3.refs_3_ = f32[4,8,128]{2,1,0:T(8,128)S(1)} collective-permute-done((f32[4,8,128]{2,1,0:T(8,128)S(1)}, f32[4,8,128]{2,1,0:T(8,128)S(1)}, u32[]{:S(2)}, u32[]{:S(2)}) %collective-permute-start.3) | collective-permute-done | bytes 16416 | tf_op jit(solution)/shard_map/ppermute | solution.py:348
  256.9 0.0 collective-permute-done.2.refs_2_
  256.9 0.0 collective-permute-done.5.refs_1_.codes_ref
  257.0 0.7 pad.14
  257.7 0.0 all-gather.3.cloned.1.call-update
  257.7 3.3 collective-permute-start.7
  261.0 0.0 collective-permute-done.refs_1_.codes_ref
  261.1 0.0 copy-start.4
  261.1 0.8 collective-permute-start.6
  261.9 0.1 collective-permute-start.1
  262.0 0.0 copy-done.4
  262.0 0.7 reduce_sum.9
  263.3 0.1 pad_add_fusion.4.where_ref
  263.4 0.1 pad_add_fusion.3.me_ref
  263.4 0.1 pad_add_fusion.where_ref
  263.5 23.2 %all-gather.3.cloned.1.call-done = f32[512,8,128]{2,1,0:T(8,128)} async-done(((f32[64,8,128]{2,1,0:T(8,128)}), f32[512,8,128]{2,1,0:T(8,128)}) %all-gather.3.cloned.1.call-update) | async-done | bytes 2097168 | tf_op jit(solution)/shard_map/all_gather | solution.py:387
  286.7 0.0 copy-start
  286.7 1.6 copy-done
  288.3 8.8 %find_slope.1 = (f32[16,4,8,896]{3,2,1,0:T(8,128)S(1)}, f32[16,128]{1,0:T(8,128)S(1)}) custom-call(f32[1]{0:T(128)} %bitcast.5.goal_ref, s32[2]{0:T(128)S(1)} %pad_add_fusion.3.me_ref, f32[8,64,8,128]{3,2,1,0:T(8,128)S(1)} %bitcast.17), custom_call_target="tpu_custom_call" | custom-call | flops 1000 | bytes 1000 | tf_op jit(solution)/shard_map/find_slope/pallas_call | solution.py:270
  297.0 9.9 %serve.6.rest_0_ = bf16[8192,896]{1,0:T(8,128)(2,1)} custom-call(s32[2]{0:T(128)S(1)} %pad_add_fusion.4.where_ref, s32[2048,3584]{1,0:T(8,128)} %codes_ref.3, f32[64,8,896]{2,1,0:T(8,128)S(1)} %bitcast.11), custom_call_target="tpu_custom_call" | custom-call | flops 1000 | bytes 1000 | tf_op jit(solution)/shard_map/serve/pallas_call | solution.py:318
  306.9 0.1 pad_add_fusion.1
  307.0 8.9 %serve.7.rest_0_ = bf16[8192,896]{1,0:T(8,128)(2,1)} custom-call(s32[2]{0:T(128)S(1)} %pad_add_fusion.where_ref, bf16[2048,896]{1,0:T(8,128)(2,1)} %collective-permute-done.5.refs_1_.codes_ref, f32[64,8,896]{2,1,0:T(8,128)S(1)} %bitcast.12, bf16[8192,896]{1,0:T(8,128)(2,1)} %serve.6.rest_0_), custom_call_target="tpu_custom_call", output_to_operand_aliasing={{}: (3, {})} | custom-call | flops 1000 | bytes 1000 | tf_op jit(solution)/shard_map/serve/pallas_call | solution.py:318
  315.9 8.9 %serve.8.rest_0_ = bf16[8192,896]{1,0:T(8,128)(2,1)} custom-call(s32[2]{0:T(128)S(1)} %get-tuple-element.6.where_ref, bf16[2048,896]{1,0:T(8,128)(2,1)} %collective-permute-done.refs_1_.codes_ref, f32[64,8,896]{2,1,0:T(8,128)S(1)} %bitcast.13, bf16[8192,896]{1,0:T(8,128)(2,1)} %serve.7.rest_0_), custom_call_target="tpu_custom_call", output_to_operand_aliasing={{}: (3, {})} | custom-call | flops 1000 | bytes 1000 | tf_op jit(solution)/shard_map/serve/pallas_call | solution.py:318
  324.8 0.0 collective-permute-done.7.codes_ref
  324.9 5.3 %serve.9.rest_0_ = bf16[8192,896]{1,0:T(8,128)(2,1)} custom-call(s32[2]{0:T(128)S(1)} %get-tuple-element.7.where_ref, bf16[1024,896]{1,0:T(8,128)(2,1)} %collective-permute-done.7.codes_ref, f32[64,8,896]{2,1,0:T(8,128)S(1)} %bitcast.14, bf16[8192,896]{1,0:T(8,128)(2,1)} %serve.8.rest_0_), custom_call_target="tpu_custom_call", output_to_operand_aliasing={{}: (3, {})} | custom-call | flops 1000 | bytes 1000 | tf_op jit(solution)/shard_map/serve/pallas_call | solution.py:318
  330.2 1.0 collective-permute-done.6.codes_ref
  331.2 4.7 %serve.10.rest_0_ = bf16[8192,896]{1,0:T(8,128)(2,1)} custom-call(s32[2]{0:T(128)S(1)} %get-tuple-element.7.where_ref, bf16[768,896]{1,0:T(8,128)(2,1)} %collective-permute-done.6.codes_ref, f32[64,8,896]{2,1,0:T(8,128)S(1)} %bitcast.15, bf16[8192,896]{1,0:T(8,128)(2,1)} %serve.9.rest_0_), custom_call_target="tpu_custom_call", output_to_operand_aliasing={{}: (3, {})} | custom-call | flops 1000 | bytes 1000 | tf_op jit(solution)/shard_map/serve/pallas_call | solution.py:318
  335.9 0.7 reshape.27
  336.5 3.5 %collective-permute-done.1.codes_ref = bf16[256,896]{1,0:T(8,128)(2,1)} collective-permute-done((bf16[256,896]{1,0:T(8,128)(2,1)}, bf16[256,896]{1,0:T(8,128)(2,1)}, u32[]{:S(2)}, u32[]{:S(2)}) %collective-permute-start.1) | collective-permute-done | bytes 458784 | tf_op jit(solution)/shard_map/ppermute | solution.py:348
  340.0 2.8 serve.11
  (13 shorter events, 0.1 us)
Async XLA Ops:
  7.2 80.3 %all-reduce.5.cloned.1.call-start = ((), (), s32[]{:S(2)}) async-start(), calls=%async_computation | async-start | bytes 2097152 | tf_op jit(solution)/shard_map/psum | solution.py:371
  14.5 16.9 %copy-start.2 = (s32[16,28]{1,0:T(8,128)S(1)}, s32[16,28]{1,0:T(8,128)}, u32[]{:S(2)}) copy-start(s32[16,28]{1,0:T(8,128)} %spans_ref.1) | copy-start | bytes 5380
  14.5 16.9 %copy-start.3 = (f32[16,28]{1,0:T(8,128)S(1)}, f32[16,28]{1,0:T(8,128)}, u32[]{:S(2)}) copy-start(f32[16,28]{1,0:T(8,128)} %param.10) | copy-start | bytes 5380
  14.5 242.4 %collective-permute-start.5 = (bf16[2048,896]{1,0:T(8,128)(2,1)}, bf16[2048,896]{1,0:T(8,128)(2,1)}, u32[]{:S(2)}, u32[]{:S(2)}) collective-permute-start(bf16[2048,896]{1,0:T(8,128)(2,1)} %cast_codes.5.rest_0_), channel_id=1, source_target_pairs={{0,2},{1,3},{2,0},{3,1},{4,6},{5,7},{6,4},{7,5},{8,10},{9,11},{10,... | collective-permute-start | bytes 11010056 | tf_op jit(solution)/shard_map/ppermute | solution.py:348
  31.4 255.3 %all-gather.3.cloned.1.call-start = ((), (), s32[]{:S(2)}) async-start(), calls=%async_computation.1 | async-start | bytes 2359296 | tf_op jit(solution)/shard_map/all_gather | solution.py:387
  87.4 1.2 copy-start.1
  160.1 100.9 %collective-permute-start = (bf16[2048,896]{1,0:T(8,128)(2,1)}, bf16[2048,896]{1,0:T(8,128)(2,1)}, u32[]{:S(2)}, u32[]{:S(2)}) collective-permute-start(bf16[2048,896]{1,0:T(8,128)(2,1)} %cast_codes.7.refs_1_), channel_id=1, source_target_pairs={{0,1},{1,2},{2,3},{3,0},{4,5},{5,6},{6,7},{7,4},{8,9},{9,10},{10,1... | collective-permute-start | bytes 11010056 | tf_op jit(solution)/shard_map/ppermute | solution.py:348
  170.5 72.6 %collective-permute-start.4 = (f32[4,8,128]{2,1,0:T(8,128)S(1)}, f32[4,8,128]{2,1,0:T(8,128)S(1)}, u32[]{:S(2)}, u32[]{:S(2)}) collective-permute-start(f32[4,8,128]{2,1,0:T(8,128)S(1)} %once_there.6), channel_id=1, source_target_pairs={{0,3},{1,0},{2,1},{3,2},{4,7},{5,4},{6,5},{7,6},{8,11},{9,8},{10,9... | collective-permute-start | bytes 49160 | tf_op jit(solution)/shard_map/ppermute | solution.py:348
  173.0 83.9 %collective-permute-start.3 = (f32[4,8,128]{2,1,0:T(8,128)S(1)}, f32[4,8,128]{2,1,0:T(8,128)S(1)}, u32[]{:S(2)}, u32[]{:S(2)}) collective-permute-start(f32[4,8,128]{2,1,0:T(8,128)S(1)} %once_there.6), channel_id=1, source_target_pairs={{0,2},{1,3},{2,0},{3,1},{4,6},{5,7},{6,4},{7,5},{8,10},{9,11},{10,... | collective-permute-start | bytes 49160 | tf_op jit(solution)/shard_map/ppermute | solution.py:348
  173.5 83.5 %collective-permute-start.2 = (f32[4,8,128]{2,1,0:T(8,128)S(1)}, f32[4,8,128]{2,1,0:T(8,128)S(1)}, u32[]{:S(2)}, u32[]{:S(2)}) collective-permute-start(f32[4,8,128]{2,1,0:T(8,128)S(1)} %once_there.6), channel_id=1, source_target_pairs={{0,1},{1,2},{2,3},{3,0},{4,5},{5,6},{6,7},{7,4},{8,9},{9,10},{10,1... | collective-permute-start | bytes 49160 | tf_op jit(solution)/shard_map/ppermute | solution.py:348
  257.7 67.1 %collective-permute-start.7 = (bf16[1024,896]{1,0:T(8,128)(2,1)}, bf16[1024,896]{1,0:T(8,128)(2,1)}, u32[]{:S(2)}, u32[]{:S(2)}) collective-permute-start(bf16[1024,896]{1,0:T(8,128)(2,1)} %once_there.9), channel_id=1, source_target_pairs={{0,3},{1,0},{2,1},{3,2},{4,7},{5,4},{6,5},{7,6},{8,11},{9,8},{10,9... | collective-permute-start | bytes 5505032 | tf_op jit(solution)/shard_map/ppermute | solution.py:348
  261.1 0.9 copy-start.4
  261.1 70.1 %collective-permute-start.6 = (bf16[768,896]{1,0:T(8,128)(2,1)S(1)}, bf16[768,896]{1,0:T(8,128)(2,1)}, u32[]{:S(2)}, u32[]{:S(2)}) collective-permute-start(bf16[768,896]{1,0:T(8,128)(2,1)S(1)} %once_there.8), channel_id=1, source_target_pairs={{0,3},{1,0},{2,1},{3,2},{4,7},{5,4},{6,5},{7,6},{8,11},{9,8},{10,9... | collective-permute-start | bytes 4128776 | tf_op jit(solution)/shard_map/ppermute | solution.py:348
  261.9 78.2 %collective-permute-start.1 = (bf16[256,896]{1,0:T(8,128)(2,1)}, bf16[256,896]{1,0:T(8,128)(2,1)}, u32[]{:S(2)}, u32[]{:S(2)}) collective-permute-start(bf16[256,896]{1,0:T(8,128)(2,1)} %once_there.5), channel_id=1, source_target_pairs={{0,3},{1,0},{2,1},{3,2},{4,7},{5,4},{6,5},{7,6},{8,11},{9,8},{10,9... | collective-permute-start | bytes 1376264 | tf_op jit(solution)/shard_map/ppermute | solution.py:348
  286.7 1.6 copy-start
Sparse Core Ops, SparseCore 0:
  31.5 55.8 all-reduce.4
  257.8 28.8 all-gather.2
